TPU v7x, 32 devices: a whole 2x2x4 slice. The times are simulated.
32 devices in a mesh: groups: 2 (over y), expert: 4 (over z), request: 4 (over x, core).
Axes of the slice: x: 2, y: 2, z: 4, core: 2. Of those that a mesh axis runs over, the one named last changes fastest.
Arguments:
- token_input: bfloat16 [2048, 4096], P(('groups', 'expert', 'request')), parts along dimension 0, may hold values from -6 to 6
- token_expert_index: int32 [2048, 8], P(('groups', 'expert', 'request')), parts along dimension 0, may hold values from 0 to 127, as said below
- token_request_index: int32 [2048], P(('groups', 'expert', 'request')), parts along dimension 0, may hold values from 0 to 15
- choice_weight: float32 [2048, 8], P(('groups', 'expert', 'request')), parts along dimension 0, may hold values from 0.05 to 1
- gate_weight: bfloat16 [4, 4096, 1024], P('expert', None, 'request'), may hold values from -0.09375 to 0.09375
- up_weight: bfloat16 [4, 4096, 1024], P('expert', None, 'request'), may hold values from -0.09375 to 0.09375
- down_weight: bfloat16 [4, 1024, 4096], P('expert', None, 'request'), may hold values from -0.1875 to 0.1875
- adapter_first_weight: bfloat16 [8, 16, 8, 1024], P(('groups', 'expert'), 'request'), parts along dimension 0, may hold values from -0.1875 to 0.1875
- adapter_second_weight: bfloat16 [8, 16, 8, 4096], P(('groups', 'expert'), 'request'), parts along dimension 0, may hold values from -2 to 2
Outputs:
- mixed: bfloat16 [2048, 4096], P(('groups', 'expert', 'request')), parts along dimension 0
There are 2 independent parts, one for each index of `groups`. A program takes and returns all parts, laid end to end along the dimension named above; an argument that names none is the same for every part. Nothing has to cross between parts.
Inputs may be any that keep to these rules, and one draw needn't show every extreme that they name: `token_expert_index`: each row names 8 different experts. Within the 64 rows of one device each expert is named by no row or by exactly 4 rows.
All inputs are finite; a program needn't handle non-finite values.
Results may differ from a plain program's by a relative error of at most 0.0062.
Values may be sent and summed in bfloat16 or wider, within the bound.
No kernel may reach another device: no remote copies, remote signals or barrier semaphores. Data moves between devices by JAX's collectives and lax.ppermute only.
A program may use at most 64 MiB of HBM per device.

v0:
```python
import jax
import jax.numpy as jnp
from jax import lax
from jax.sharding import PartitionSpec as P

CAP = 4


def slot_rank(expert_ids, experts_live):
    count = expert_ids.shape[-2]
    lanes = jnp.arange(experts_live, dtype=jnp.int32)
    one_hot = (expert_ids[..., None] == lanes).astype(jnp.float32)
    per_token = jnp.sum(one_hot, axis=-2)
    lower = (
        jnp.arange(count, dtype=jnp.int32)[None, :] < jnp.arange(count, dtype=jnp.int32)[:, None]
    ).astype(jnp.float32)
    prefix = jnp.einsum(
        "ts,...se->...te",
        lower,
        per_token,
        precision=lax.Precision.HIGHEST,
        preferred_element_type=jnp.float32,
    )
    ranks = jnp.sum(one_hot * prefix[..., None, :], axis=-1)
    return ranks.astype(jnp.int32)


def slot_table(token_expert_index, values, experts_live, capacity):
    choice_slot_index = slot_rank(token_expert_index, experts_live)
    slot_key = jnp.where(
        token_expert_index < experts_live, token_expert_index * capacity + choice_slot_index, -1
    )
    lanes = jnp.arange(experts_live * capacity, dtype=jnp.int32)
    match = slot_key[..., None, :, :] == lanes[:, None, None]
    return jnp.sum(jnp.where(match, values[..., None, :, :], 0.0), axis=-1)


def slot_owner(table, token_request_index):
    marked = jnp.where(table > 0, token_request_index[..., None, :] + 1, 0)
    return (jnp.sum(marked, axis=-1) - 1).astype(jnp.int32)


def body(
    token_input,
    token_expert_index,
    token_request_index,
    choice_weight,
    gate_weight,
    up_weight,
    down_weight,
    adapter_first_weight,
    adapter_second_weight,
):
    experts_live = gate_weight.shape[0] * lax.axis_size("expert")
    request_devs = lax.axis_size("request")
    feature_width = token_input.shape[1]
    tokens_dev = token_input.shape[0]
    capacity = CAP
    combine_table = slot_table(token_expert_index, choice_weight, experts_live, capacity)
    all_hidden, all_ids, all_requests = (
        lax.all_gather(token_input, "request", axis=0, tiled=True),
        lax.all_gather(token_expert_index, "request", axis=0, tiled=True),
        lax.all_gather(token_request_index, "request", axis=0, tiled=True),
    )
    ids_grid = all_ids.reshape(request_devs, tokens_dev, -1)
    tables = slot_table(ids_grid, jnp.ones(ids_grid.shape, jnp.float32), experts_live, capacity)
    hidden_grid = all_hidden.reshape(request_devs, tokens_dev, feature_width)
    packed = jnp.einsum(
        "rst,rtd->rsd", tables.astype(jnp.bfloat16), hidden_grid, preferred_element_type=jnp.float32
    ).astype(jnp.bfloat16)
    owners = slot_owner(tables, all_requests.reshape(request_devs, tokens_dev))
    packed, owners = (
        lax.all_to_all(packed, "expert", split_axis=1, concat_axis=1, tiled=True),
        lax.all_to_all(owners, "expert", split_axis=1, concat_axis=1, tiled=True),
    )
    slot_rows = packed.reshape(-1, feature_width)
    slot_requests = owners.reshape(-1)
    gate_act = jnp.dot(slot_rows, gate_weight[0], preferred_element_type=jnp.float32)
    up_act = jnp.dot(slot_rows, up_weight[0], preferred_element_type=jnp.float32)
    hidden_units = (jax.nn.silu(gate_act) * up_act).astype(jnp.bfloat16)
    leading_factor = lax.all_gather(adapter_first_weight, "request", axis=1, tiled=True)
    first_flat = leading_factor.reshape(-1, leading_factor.shape[3])
    down_local = down_weight[0]
    cols_dev = down_local.shape[1]
    portion = lax.all_gather(hidden_units, "request", axis=1, tiled=True)
    base_sum = jnp.dot(portion, down_local, preferred_element_type=jnp.float32)
    rank_sum = lax.dot_general(
        portion, first_flat, (((1,), (1,)), ((), ())), preferred_element_type=jnp.float32
    )
    base_sum, reduced_rank_output = (base_sum, rank_sum)
    column_holder = (
        jnp.arange(reduced_rank_output.shape[1], dtype=jnp.int32) // adapter_first_weight.shape[2]
    )
    selected = jnp.where(
        column_holder[None, :] == slot_requests[:, None], reduced_rank_output, 0.0
    ).astype(jnp.bfloat16)
    second_factor_full = lax.all_gather(
        adapter_second_weight, "request", axis=1, tiled=True
    ).reshape(-1, feature_width)
    second_flat = lax.dynamic_slice_in_dim(
        second_factor_full, lax.axis_index("request") * cols_dev, cols_dev, 1
    )
    expert_out = (
        base_sum + jnp.dot(selected, second_flat, preferred_element_type=jnp.float32)
    ).astype(jnp.bfloat16)
    expert_out = expert_out.reshape(request_devs, experts_live, capacity, cols_dev)
    returned = lax.all_to_all(
        lax.all_to_all(expert_out, "expert", split_axis=1, concat_axis=1, tiled=True),
        "request",
        split_axis=0,
        concat_axis=3,
        tiled=True,
    )
    returned = returned.reshape(experts_live * capacity, feature_width).astype(jnp.float32)
    mixed = lax.dot_general(
        combine_table,
        returned,
        (((0,), (0,)), ((), ())),
        precision=lax.Precision.HIGHEST,
        preferred_element_type=jnp.float32,
    )
    return mixed.astype(jnp.bfloat16)


def solution(mesh):
    in_specs = (
        P(("groups", "expert", "request"), None),
        P(("groups", "expert", "request"), None),
        P(("groups", "expert", "request")),
        P(("groups", "expert", "request"), None),
        P("expert", None, "request"),
        P("expert", None, "request"),
        P("expert", None, "request"),
        P(("groups", "expert"), "request", None, None),
        P(("groups", "expert"), "request", None, None),
    )
    out_specs = P(("groups", "expert", "request"), None)
    return jax.shard_map(body, mesh=mesh, in_specs=in_specs, out_specs=out_specs, check_vma=False)
```

profile of v0, /device:TPU:0, one launch (start us, length us, event | category | flops | bytes accessed | tf_op | source)
XLA Modules:
  0.0 94.9 jit_solution(10075805443654792432)
XLA Ops:
  6.5 0.7 all-gather.4.cloned.1.call-update
  7.3 1.2 %dynamic-slice = u32[1]{0:T(128)} dynamic-slice(u32[32]{0:T(128)} %constant.50, u32[]{:T(128)S(6)} %add.50), dynamic_slice_sizes={1} | dynamic-slice | bytes 12
  9.2 0.9 dynamic-update-slice
  10.0 6.3 %all-reduce = s32[256]{0:T(256)S(1)} all-reduce(s32[256]{0:T(256)S(1)} %dynamic-update-slice), channel_id=1, replica_groups=mesh['groups'=2,'expert'=4,'request'=4] {'request'}, use_global_device_ids=true, to_apply=%add | all-reduce | flops 256 | bytes 2048
  16.5 5.3 %all-gather = s32[4,64,8]{1,2,0:T(8,128)S(1)} all-gather(s32[1,64,8]{1,2,0:T(8,128)} %bitcast.56), channel_id=1, replica_groups=mesh['groups'=2,'expert'=4,'request'=4] {'request'}, dimensions={0}, use_global_device_ids=true | all-gather | bytes 10240 | tf_op jit(solution)/shard_map/all_gather | solution.py:62
  21.8 0.2 convolution_bitcast_fusion
  22.1 0.1 select_reduce_fusion.3
  22.3 0.6 copy.68
  23.0 4.9 %all-to-all-start.1 = ((s32[4,4,4]{2,0,1:T(4,128)}), s32[4,4,4]{2,0,1:T(4,128)S(1)}, u32[]{:S(2)}, u32[]{:S(2)}) async-start(s32[4,4,4]{2,0,1:T(4,128)} %copy.68), calls=%async_computation.1 | async-start | bytes 16384 | tf_op jit(solution)/shard_map/all_to_all | solution.py:74
  27.8 0.7 all-gather.6.cloned.1.call-update
  28.6 5.7 %all-gather.4.cloned.1.call-done = bf16[256,4096]{1,0:T(8,128)(2,1)} async-done(((bf16[64,4096]{1,0:T(8,128)(2,1)}), bf16[256,4096]{1,0:T(8,128)(2,1)}) %all-gather.4.cloned.1.call-update) | async-done | bytes 2097168 | tf_op jit(solution)/shard_map/all_gather | solution.py:61
  34.2 2.0 %convolution_convert_fusion.1 = bf16[4,16,4096]{2,1,0:T(8,128)(2,1)S(1)} fusion(bf16[4,64,4096]{2,1,0:T(8,128)(2,1)} %bitcast.50, f32[4,16,64]{2,1,0:T(8,128)S(1)} %select_reduce_fusion), kind=kOutput, calls=%fused_computation.1 | convolution fusion | flops 33820672 | bytes 2637824 | tf_op jit(solution)/shard_map/rst,rtd->rsd/dot_general | solution.py:68
  36.3 1.2 %copy.66 = bf16[4,16,4096]{2,0,1:T(4,128)(2,1)} copy(bf16[4,16,4096]{2,1,0:T(8,128)(2,1)S(1)} %convolution_convert_fusion.1) | data formatting | bytes 1048576 | tf_op jit(solution)/shard_map/convert_element_type | solution.py:70
  37.5 4.6 %all-to-all-start = ((bf16[4,16,4096]{2,0,1:T(4,128)(2,1)}), bf16[4,16,4096]{2,0,1:T(4,128)(2,1)S(1)}, u32[]{:S(2)}, u32[]{:S(2)}) async-start(bf16[4,16,4096]{2,0,1:T(4,128)(2,1)} %copy.66), calls=%async_computation | async-start | bytes 1048576 | tf_op jit(solution)/shard_map/all_to_all | solution.py:73
  42.1 7.0 %all_gather.22 = bf16[1,16,8,1024]{3,2,0,1:T(8,128)(2,1)S(1)} all-gather(bf16[1,4,8,1024]{3,2,0,1:T(8,128)(2,1)S(1)} %bitcast.55), channel_id=1, replica_groups=mesh['groups'=2,'expert'=4,'request'=4] {'request'}, dimensions={1}, use_global_device_ids=true | all-gather | bytes 327680 | tf_op jit(solution)/shard_map/all_gather | solution.py:81
  49.1 0.1 fusion.24
  49.3 0.1 eq.80
  49.4 7.6 %all-to-all-done = bf16[4,16,4096]{2,0,1:T(4,128)(2,1)S(1)} async-done(((bf16[4,16,4096]{2,0,1:T(4,128)(2,1)}), bf16[4,16,4096]{2,0,1:T(4,128)(2,1)S(1)}, u32[]{:S(2)}, u32[]{:S(2)}) %all-to-all-start) | async-done | bytes 524320 | tf_op jit(solution)/shard_map/all_to_all | solution.py:73
  57.0 0.3 copy.67
  57.3 2.2 %fusion.4 = f32[64,256]{1,0:T(8,128)S(1)} fusion(bf16[64,4096]{1,0:T(8,128)(2,1)S(1)} %bitcast.48, bf16[1,4096,256]{2,1,0:T(8,128)(2,1)} %param.13), kind=kOutput, calls=%fused_computation.6 | convolution fusion | flops 134217728 | bytes 2686976 | tf_op jit(solution)/shard_map/dot_general | solution.py:78
  59.5 0.5 fusion.15
  60.0 5.4 %all_gather.20 = bf16[64,1024]{1,0:T(8,128)(2,1)S(1)} all-gather(bf16[64,256]{1,0:T(8,128)(2,1)S(1)} %fusion.15), channel_id=1, replica_groups=mesh['groups'=2,'expert'=4,'request'=4] {'request'}, dimensions={1}, use_global_device_ids=true | all-gather | bytes 163840 | tf_op jit(solution)/shard_map/all_gather | solution.py:85
  65.4 1.4 %fusion.19 = f32[64,1024]{1,0:T(8,128)S(1)} fusion(bf16[64,1024]{1,0:T(8,128)(2,1)S(1)} %all_gather.20, bf16[1,16,8,1024]{3,2,0,1:T(8,128)(2,1)S(1)} %all_gather.22, bf16[128,4096]{1,0:T(8,128)(2,1)} %bitcast.57, s32[]{:T(128)S(6)} %select_n.47, s32[128]{0:T(128)S(1)} %and_select_fusion, s32[64]{0:T(128)S(1)} %eq.80), kind=kOutput, calls=%fused_computation.14 | convolution fusion | flops 33579008 | bytes 918276 | tf_op jit(solution)/shard_map/dot_general | solution.py:104
  66.8 0.5 fusion.9
  67.3 0.7 copy.72
  68.0 3.3 %all-to-all-start.2 = ((bf16[4,4,4,1024]{3,2,0,1:T(4,128)(2,1)}), bf16[4,4,4,1024]{3,2,0,1:T(4,128)(2,1)S(1)}, u32[]{:S(2)}, u32[]{:S(2)}) async-start(bf16[4,4,4,1024]{3,2,0,1:T(4,128)(2,1)} %copy.72), calls=%async_computation.2 | async-start | bytes 262144 | tf_op jit(solution)/shard_map/all_to_all | solution.py:108
  71.4 6.5 %all-to-all-done.2 = bf16[4,4,4,1024]{3,2,0,1:T(4,128)(2,1)S(1)} async-done(((bf16[4,4,4,1024]{3,2,0,1:T(4,128)(2,1)}), bf16[4,4,4,1024]{3,2,0,1:T(4,128)(2,1)S(1)}, u32[]{:S(2)}, u32[]{:S(2)}) %all-to-all-start.2) | async-done | bytes 131104 | tf_op jit(solution)/shard_map/all_to_all | solution.py:108
  77.8 0.7 copy.73
  78.5 3.3 %all-to-all-start.3 = ((bf16[4,4,4,1024]{3,2,1,0:T(4,128)(2,1)}), bf16[4,4,4,1024]{3,2,1,0:T(4,128)(2,1)S(1)}, u32[]{:S(2)}, u32[]{:S(2)}) async-start(bf16[4,4,4,1024]{3,2,1,0:T(4,128)(2,1)} %copy.73), calls=%async_computation.3 | async-start | bytes 262144 | tf_op jit(solution)/shard_map/all_to_all | solution.py:107
  81.9 4.6 %all-to-all-done.3 = bf16[4,4,4,1024]{3,2,1,0:T(4,128)(2,1)S(1)} async-done(((bf16[4,4,4,1024]{3,2,1,0:T(4,128)(2,1)}), bf16[4,4,4,1024]{3,2,1,0:T(4,128)(2,1)S(1)}, u32[]{:S(2)}, u32[]{:S(2)}) %all-to-all-start.3) | async-done | bytes 131104 | tf_op jit(solution)/shard_map/all_to_all | solution.py:107
  86.5 0.1 copy.74
  86.6 1.4 %convolution_convert_fusion = bf16[64,4096]{1,0:T(8,128)(2,1)} fusion(f32[16,64]{1,0:T(8,128)S(1)} %select_reduce_fusion.2, bf16[16,4096]{1,0:T(8,128)(2,1)S(1)} %bitcast.53), kind=kOutput, calls=%fused_computation | convolution fusion | flops 50593792 | bytes 659456 | tf_op jit(solution)/shard_map/dot_general | solution.py:115
  (31 shorter events, 0.6 us)
Async XLA Ops:
  6.5 60.2 %copy-start = (bf16[1,1024,1024]{2,1,0:T(8,128)(2,1)S(1)}, bf16[1,1024,1024]{2,1,0:T(8,128)(2,1)}, u32[]{:S(2)}) copy-start(bf16[1,1024,1024]{2,1,0:T(8,128)(2,1)} %param.15) | copy-start | bytes 6291460
  6.5 27.7 %all-gather.4.cloned.1.call-start = ((), (), s32[]{:S(2)}) async-start(), calls=%async_computation.4 | async-start | bytes 2621440 | tf_op jit(solution)/shard_map/all_gather | solution.py:61
  23.0 14.5 %all-to-all-start.1 = ((s32[4,4,4]{2,0,1:T(4,128)}), s32[4,4,4]{2,0,1:T(4,128)S(1)}, u32[]{:S(2)}, u32[]{:S(2)}) async-start(s32[4,4,4]{2,0,1:T(4,128)} %copy.68), calls=%async_computation.1 | async-start | bytes 16384 | tf_op jit(solution)/shard_map/all_to_all | solution.py:74
  27.8 37.6 %all-gather.6.cloned.1.call-start = ((), (), s32[]{:S(2)}) async-start(), calls=%async_computation.5 | async-start | bytes 1310720 | tf_op jit(solution)/shard_map/all_gather | solution.py:97
  34.2 7.8 %copy-start.2 = (bf16[1,4,8,1024]{3,2,1,0:T(8,128)(2,1)S(1)}, bf16[1,4,8,1024]{3,2,1,0:T(8,128)(2,1)}, u32[]{:S(2)}) copy-start(bf16[1,4,8,1024]{3,2,1,0:T(8,128)(2,1)} %param.16) | copy-start | bytes 196612
  34.2 14.9 %copy-start.3 = (s32[64,8]{0,1:T(8,128)S(1)}, s32[64,8]{0,1:T(8,128)}, u32[]{:S(2)}) copy-start(s32[64,8]{0,1:T(8,128)} %param.10) | copy-start | bytes 6148
  37.5 19.5 %all-to-all-start = ((bf16[4,16,4096]{2,0,1:T(4,128)(2,1)}), bf16[4,16,4096]{2,0,1:T(4,128)(2,1)S(1)}, u32[]{:S(2)}, u32[]{:S(2)}) async-start(bf16[4,16,4096]{2,0,1:T(4,128)(2,1)} %copy.66), calls=%async_computation | async-start | bytes 1048576 | tf_op jit(solution)/shard_map/all_to_all | solution.py:73
  57.0 2.5 %copy-start.1 = (bf16[1,4096,256]{2,1,0:T(8,128)(2,1)S(1)}, bf16[1,4096,256]{2,1,0:T(8,128)(2,1)}, u32[]{:S(2)}) copy-start(bf16[1,4096,256]{2,1,0:T(8,128)(2,1)} %param.14) | copy-start | bytes 6291460
  66.8 15.1 %copy-start.4 = (f32[64,8]{0,1:T(8,128)S(1)}, f32[64,8]{0,1:T(8,128)}, u32[]{:S(2)}) copy-start(f32[64,8]{0,1:T(8,128)} %param.12) | copy-start | bytes 6148
  68.0 9.8 %all-to-all-start.2 = ((bf16[4,4,4,1024]{3,2,0,1:T(4,128)(2,1)}), bf16[4,4,4,1024]{3,2,0,1:T(4,128)(2,1)S(1)}, u32[]{:S(2)}, u32[]{:S(2)}) async-start(bf16[4,4,4,1024]{3,2,0,1:T(4,128)(2,1)} %copy.72), calls=%async_computation.2 | async-start | bytes 262144 | tf_op jit(solution)/shard_map/all_to_all | solution.py:108
  78.5 7.9 %all-to-all-start.3 = ((bf16[4,4,4,1024]{3,2,1,0:T(4,128)(2,1)}), bf16[4,4,4,1024]{3,2,1,0:T(4,128)(2,1)S(1)}, u32[]{:S(2)}, u32[]{:S(2)}) async-start(bf16[4,4,4,1024]{3,2,1,0:T(4,128)(2,1)} %copy.73), calls=%async_computation.3 | async-start | bytes 262144 | tf_op jit(solution)/shard_map/all_to_all | solution.py:107
Sparse Core Ops, SparseCore 0:
  8.9 25.2 all-gather.3
  35.8 17.9 all-gather.5
where the time goes:
time: 95.4 us; the launch traced here: 94.9 us
  waiting for transfers between devices  25.7 us (27%)
  blocking collectives  24.1 us (25%)
  starting transfers between devices  16.1 us (17%)
  between operations  14.2 us (15%)
  matrix products  8.21 us (9%)
  local copies, waits for them, and re-layouts  6.12 us (6%)
    all_to_all x1, waiting for transfers between devices, body(): lax.all_to_all(packed, 'expert', split_axis=1, concat_axis=1, tiled=True)  7.55 us
    all_gather x1, blocking collectives, body(): lax.all_gather(adapter_first_weight, 'request', axis=1, tiled=True)  7.04 us
    all_to_all x1, waiting for transfers between devices, body(): lax.all_to_all(expert_out, 'expert', split_axis=1, concat_axis=1, tiled=T...  6.45 us
    unnamed x1, blocking collectives  6.35 us
    all_gather x1, waiting for transfers between devices, body(): lax.all_gather(token_input, 'request', axis=0, tiled=True)  5.68 us
    all_gather x1, blocking collectives, body(): portion = lax.all_gather(hidden_units, 'request', axis=1, tiled=True)  5.43 us
    all_gather x1, blocking collectives, body(): lax.all_gather(token_expert_index, 'request', axis=0, tiled=True)  5.3 us
    all_to_all x1, starting transfers between devices, body(): lax.all_to_all(owners, 'expert', split_axis=1, concat_axis=1, tiled=True)  4.87 us
  transfers between devices with their start and end apart: 6, of which 4 were waited for; matrix products, arithmetic and copies ran while one was open for 10% of the time, Pallas kernels for 0%

commit v1 on v0

v1 whole, which is shorter than its diff:
```python
import functools

import jax
import jax.numpy as jnp
from jax import lax
from jax.experimental import pallas as pl
from jax.experimental.pallas import tpu as pltpu
from jax.sharding import PartitionSpec as P

CAP = 4
LANES = 128
VMEM = pl.BlockSpec(memory_space=pltpu.VMEM)


def xor_permute(value, axis, offset):
    return lax.ppermute(value, axis, [(i, i ^ offset) for i in range(lax.axis_size(axis))])


def slot_values(ids, values, expert):
    tokens = ids.shape[1]
    match = ids == expert
    named = jnp.sum(match.astype(jnp.float32), axis=0, keepdims=True)
    row = lax.broadcasted_iota(jnp.int32, (tokens, tokens), 0)
    col = lax.broadcasted_iota(jnp.int32, (tokens, tokens), 1)
    earlier = (row < col).astype(jnp.bfloat16)
    rank = jnp.dot(named.astype(jnp.bfloat16), earlier, preferred_element_type=jnp.float32)
    slot = lax.broadcasted_iota(jnp.int32, (CAP, tokens), 0).astype(jnp.float32)
    held = jnp.logical_and(slot == rank, named > 0)
    value = jnp.sum(jnp.where(match, values, 0.0), axis=0, keepdims=True)
    return jnp.where(held, value, 0.0)


def pack_kernel(ids_ref, req_ref, x_ref, *refs):
    out_refs, scratch = refs[:-1], refs[-1]
    experts = len(out_refs)
    me = lax.axis_index("expert")
    width = x_ref.shape[1]
    ids = ids_ref[...]
    ones = jnp.ones(ids.shape, jnp.float32)
    table = jnp.concatenate([slot_values(ids, ones, me ^ s) for s in range(experts)], axis=0)
    owner = jnp.sum(table * (req_ref[...] + 1).astype(jnp.float32), axis=1, keepdims=True) - 1.0
    scratch[:, :width] = jnp.dot(
        table.astype(jnp.bfloat16), x_ref[...], preferred_element_type=jnp.float32
    )
    scratch[:, width:] = jnp.broadcast_to(owner, (owner.shape[0], LANES))
    for s, out_ref in enumerate(out_refs):
        out_ref[...] = scratch[pl.ds(s * CAP, CAP), :].astype(out_ref.dtype)


def hidden_kernel(near_ref, far_ref, gate_ref, up_ref, hidden_ref, owner_ref):
    width = gate_ref.shape[1]
    rows = jnp.concatenate([near_ref[:, :width], far_ref[:, :width]], axis=0)
    gate = jnp.dot(rows, gate_ref[0], preferred_element_type=jnp.float32)
    up = jnp.dot(rows, up_ref[0], preferred_element_type=jnp.float32)
    hidden_ref[...] = (gate / (1.0 + jnp.exp(-gate)) * up).astype(hidden_ref.dtype)
    owner_ref[...] = jnp.concatenate([near_ref[:, width:], far_ref[:, width:]], axis=0)


def down_kernel(order, n_req, *refs):
    size = len(order)
    hid_refs = refs[:size]
    owner_ref, down_ref, first_ref, second_ref, out_ref, scratch = refs[size:]
    me_e, me_r = lax.axis_index("expert"), lax.axis_index("request")
    total, cols = scratch.shape
    block = total // size
    part = hid_refs[0].shape[1]
    columns = first_ref.shape[0]
    base = jnp.zeros((total, cols), jnp.float32)
    low = jnp.zeros((total, columns), jnp.float32)
    for s, hid_ref in enumerate(hid_refs):
        picks = [order.index(o ^ s) for o in order]
        hid = jnp.concatenate([hid_ref[j * block : (j + 1) * block, :] for j in picks], axis=0)
        at = pl.ds(pl.multiple_of((me_r ^ s) * part, part), part)
        base += jnp.dot(hid, down_ref[0, at, :], preferred_element_type=jnp.float32)
        low += lax.dot_general(
            hid, first_ref[:, at], (((1,), (1,)), ((), ())), preferred_element_type=jnp.float32
        )
    lane = lax.broadcasted_iota(jnp.int32, (1, columns), 1)
    per_dev = columns // size
    rank = per_dev // n_req
    holder = jnp.zeros((1, columns), jnp.int32)
    for i, o in enumerate(order):
        mine = (me_r ^ o) * n_req + (lane - i * per_dev) // rank
        holder = jnp.where(lane // per_dev == i, mine, holder)
    owner = owner_ref[:, :1].astype(jnp.int32)
    selected = jnp.where(holder == owner, low, 0.0).astype(jnp.bfloat16)
    scratch[...] = base + jnp.dot(selected, second_ref[...], preferred_element_type=jnp.float32)
    experts = block // CAP
    for i, o in enumerate(order):
        for s in range(experts):
            target = (me_e ^ s) * size + (me_r ^ o)
            rows = scratch[pl.ds(i * block + s * CAP, CAP), :]
            out_ref[target] = rows.astype(out_ref.dtype)


def combine_kernel(ids_ref, weight_ref, back_ref, mixed_ref, scratch):
    experts = scratch.shape[0] // CAP
    size = back_ref.shape[0] // experts
    cols = back_ref.shape[2]
    ids, weights = ids_ref[...], weight_ref[...]
    table = jnp.concatenate([slot_values(ids, weights, e) for e in range(experts)], axis=0)
    high = table.astype(jnp.bfloat16)
    rest = table - high.astype(jnp.float32)
    middle = rest.astype(jnp.bfloat16)
    low = (rest - middle.astype(jnp.float32)).astype(jnp.bfloat16)
    for r in range(size):
        for e in range(experts):
            scratch[pl.ds(e * CAP, CAP), :] = back_ref[e * size + r].astype(jnp.float32)
        rows = scratch[...].astype(jnp.bfloat16)
        mixed = sum(
            lax.dot_general(
                piece, rows, (((0,), (0,)), ((), ())), preferred_element_type=jnp.float32
            )
            for piece in (low, middle, high)
        )
        mixed_ref[:, r * cols : (r + 1) * cols] = mixed.astype(mixed_ref.dtype)


def body(
    token_input,
    token_expert_index,
    token_request_index,
    choice_weight,
    gate_weight,
    up_weight,
    down_weight,
    adapter_first_weight,
    adapter_second_weight,
):
    experts = lax.axis_size("expert")
    size = lax.axis_size("request")
    me_r = lax.axis_index("request")
    tokens, width = token_input.shape
    part = gate_weight.shape[2]
    cols = down_weight.shape[2]
    n_req, rank = adapter_first_weight.shape[1:3]
    bf16, f32 = jnp.bfloat16, jnp.float32
    params = pltpu.CompilerParams(vmem_limit_bytes=32 * 2**20)

    ids = token_expert_index.T
    weights = choice_weight.T
    packed = pl.pallas_call(
        pack_kernel,
        out_shape=[jax.ShapeDtypeStruct((CAP, width + LANES), bf16)] * experts,
        in_specs=[VMEM] * 3,
        out_specs=[VMEM] * experts,
        scratch_shapes=[pltpu.VMEM((experts * CAP, width + LANES), f32)],
        compiler_params=params,
    )(ids, token_request_index[None], token_input)

    first = adapter_first_weight.reshape(n_req * rank, -1)
    second = adapter_second_weight.reshape(n_req * rank, -1)
    rows = jnp.concatenate(
        [packed[0]] + [xor_permute(packed[s], "expert", s) for s in range(1, experts)], axis=0
    )
    order = [0]
    bit = size // 2
    near = far = rows
    while bit:
        half = second.shape[1] // 2
        upper = (me_r // bit) % 2
        keep = lax.dynamic_slice_in_dim(second, upper * half, half, 1)
        give = lax.dynamic_slice_in_dim(second, (1 - upper) * half, half, 1)
        second = jnp.concatenate([keep, xor_permute(give, "request", bit)], axis=0)
        first = jnp.concatenate([first, xor_permute(first, "request", bit)], axis=0)
        near = rows
        far = xor_permute(rows, "request", bit)
        order = order + [o ^ bit for o in order]
        bit //= 2
        if bit:
            rows = jnp.concatenate([near, far], axis=0)

    total = experts * CAP * size
    hidden, owner = pl.pallas_call(
        hidden_kernel,
        out_shape=[
            jax.ShapeDtypeStruct((total, part), bf16),
            jax.ShapeDtypeStruct((total, LANES), bf16),
        ],
        in_specs=[VMEM] * 4,
        out_specs=[VMEM] * 2,
        compiler_params=params,
    )(near, far, gate_weight, up_weight)

    shared = [hidden] + [xor_permute(hidden, "request", s) for s in range(1, size)]
    out = pl.pallas_call(
        functools.partial(down_kernel, order, n_req),
        out_shape=jax.ShapeDtypeStruct((experts * size, CAP, cols), bf16),
        in_specs=[VMEM] * (size + 4),
        out_specs=VMEM,
        scratch_shapes=[pltpu.VMEM((total, cols), f32)],
        compiler_params=params,
    )(*shared, owner, down_weight, first, second)

    back = lax.all_to_all(out, ("expert", "request"), 0, 0, tiled=True)
    return pl.pallas_call(
        combine_kernel,
        out_shape=jax.ShapeDtypeStruct((tokens, width), bf16),
        in_specs=[VMEM] * 3,
        out_specs=VMEM,
        scratch_shapes=[pltpu.VMEM((experts * CAP, cols), f32)],
        compiler_params=params,
    )(ids, weights, back)


def solution(mesh):
    in_specs = (
        P(("groups", "expert", "request"), None),
        P(("groups", "expert", "request"), None),
        P(("groups", "expert", "request")),
        P(("groups", "expert", "request"), None),
        P("expert", None, "request"),
        P("expert", None, "request"),
        P("expert", None, "request"),
        P(("groups", "expert"), "request", None, None),
        P(("groups", "expert"), "request", None, None),
    )
    out_specs = P(("groups", "expert", "request"), None)
    return jax.shard_map(body, mesh=mesh, in_specs=in_specs, out_specs=out_specs, check_vma=False)
```

time: 95.4 us -> 43.5 us (0.46)
  waiting for transfers between devices: 25.7 us -> 10.6 us
  between operations: 14.2 us -> 0.13 us
  blocking collectives: 24.1 us -> 10.5 us
  matrix products: 8.21 us -> 0 us
  starting transfers between devices: 16.1 us -> 12.2 us
  Pallas kernels: 0 us -> 3.48 us
    all_to_all x4 -> x0, waiting for transfers between devices: 18.6 us -> none  [the longest x1 7.55 us: body(): lax.all_to_all(packed, 'expert', split_axis=1, concat_axis=1, tiled=True)]
    all_gather x3 -> x0, blocking collectives: 17.8 us -> none  [the longest x1 7.04 us: body(): lax.all_gather(adapter_first_weight, 'request', axis=1, tiled=True)]
    all_to_all x4 -> x0, starting transfers between devices: 16.1 us -> none  [the longest x1 4.87 us: body(): lax.all_to_all(owners, 'expert', split_axis=1, concat_axis=1, tiled=True)]
    ppermute x0 -> x12, starting transfers between devices: none -> 12.2 us  [xor_permute(): lax.ppermute(value, axis, [(i, i ^ offset) for i in range(lax.axis_size(a...]
    ppermute x0 -> x12, waiting for transfers between devices: none -> 10.6 us  [xor_permute(): lax.ppermute(value, axis, [(i, i ^ offset) for i in range(lax.axis_size(a...]
    all_to_all x0 -> x1, blocking collectives: none -> 10.5 us  [body(): back = lax.all_to_all(out, ('expert', 'request'), 0, 0, tiled=True)]
    dot_general x8 -> x0, matrix products: 8.21 us -> none  [the longest x1 2.21 us: body(): jnp.dot(slot_rows, gate_weight[0], preferred_element_type=jnp.float32)]
    unnamed x1 -> x0, blocking collectives: 6.35 us -> none
  transfers between devices with their start and end apart: 6 -> 12, of which waited for: 4 -> 6; matrix products, arithmetic and copies ran while one was open for 10% -> 5% of each run, Pallas kernels for 0% -> 2%
where the time goes in v1:
time: 43.5 us; the launch traced here: 43.2 us
  starting transfers between devices  12.2 us (28%)
  waiting for transfers between devices  10.6 us (24%)
  blocking collectives  10.5 us (24%)
  local copies, waits for them, and re-layouts  5.32 us (12%)
  Pallas kernels  3.48 us (8%)
  other arithmetic  0.99 us (2%)
    ppermute x12, starting transfers between devices, xor_permute(): lax.ppermute(value, axis, [(i, i ^ offset) for i in range(lax.axis_size(a...  12.2 us
    ppermute x12, waiting for transfers between devices, xor_permute(): lax.ppermute(value, axis, [(i, i ^ offset) for i in range(lax.axis_size(a...  10.6 us
    all_to_all x1, blocking collectives, body(): back = lax.all_to_all(out, ('expert', 'request'), 0, 0, tiled=True)  10.5 us
    unnamed x18, local copies, waits for them, and re-layouts  4.14 us
    pallas_call x1, Pallas kernels, body(): pl.pallas_call(combine_kernel, out_shape=jax.ShapeDtypeStruct((tokens, wi...  1.53 us
    dynamic_slice x1, local copies, waits for them, and re-layouts, body(): give = lax.dynamic_slice_in_dim(second, (1 - upper) * half, half, 1)  0.98 us
    concatenate x2, other arithmetic, body(): first = jnp.concatenate([first, xor_permute(first, 'request', bit)], axis=0)  0.87 us
  transfers between devices with their start and end apart: 12, of which 6 were waited for; matrix products, arithmetic and copies ran while one was open for 5% of the time, Pallas kernels for 2%

profile of v1, /device:TPU:0, one launch (start us, length us, event | category | flops | bytes accessed | tf_op | source)
XLA Modules:
  0.0 43.2 jit_solution(3894293743120439469)
XLA Ops:
  0.0 1.2 %copy-done.3 = bf16[64,4096]{1,0:T(8,128)(2,1)S(1)} copy-done((bf16[64,4096]{1,0:T(8,128)(2,1)S(1)}, bf16[64,4096]{1,0:T(8,128)(2,1)}, u32[]{:S(2)}) %copy-start.3) | copy-done | bytes 524312
  1.2 0.7 %copy-done.4 = s32[64,8]{0,1:T(8,128)S(1)} copy-done((s32[64,8]{0,1:T(8,128)S(1)}, s32[64,8]{0,1:T(8,128)}, u32[]{:S(2)}) %copy-start.4) | copy-done | bytes 2072
  1.9 0.7 %copy-done.7 = s32[64]{0:T(128)S(1)} copy-done((s32[64]{0:T(128)S(1)}, s32[64]{0:T(128)}, u32[]{:S(2)}) %copy-start.7) | copy-done | bytes 280
  2.5 0.3 shard_map.91
  2.9 3.1 %collective-permute-start = (bf16[4,4224]{1,0:T(4,128)(2,1)S(1)}, bf16[4,4224]{1,0:T(4,128)(2,1)S(1)}, u32[]{:S(2)}, u32[]{:S(2)}) collective-permute-start(bf16[4,4224]{1,0:T(4,128)(2,1)S(1)} %get-tuple-element.12), channel_id=1, source_target_pairs={{0,4},{4,0},{8,12},{12,8},{1,5},{5,1},{9,13},{13,9},{2,6},{6,2},{1... | collective-permute-start | bytes 101384 | tf_op jit(solution)/shard_map/ppermute | solution.py:16
  6.0 2.6 %collective-permute-start.1 = (bf16[4,4224]{1,0:T(4,128)(2,1)S(1)}, bf16[4,4224]{1,0:T(4,128)(2,1)S(1)}, u32[]{:S(2)}, u32[]{:S(2)}) collective-permute-start(bf16[4,4224]{1,0:T(4,128)(2,1)S(1)} %get-tuple-element.13), channel_id=1, source_target_pairs={{0,8},{4,12},{8,0},{12,4},{1,9},{5,13},{9,1},{13,5},{2,10},{6,14},... | collective-permute-start | bytes 101384 | tf_op jit(solution)/shard_map/ppermute | solution.py:16
  8.6 1.7 %collective-permute-start.8 = (bf16[32,1024]{1,0:T(8,128)(2,1)}, bf16[32,1024]{1,0:T(8,128)(2,1)S(1)}, u32[]{:S(2)}, u32[]{:S(2)}) collective-permute-start(bf16[32,1024]{1,0:T(8,128)(2,1)} %bitcast.10), channel_id=1, source_target_pairs={{0,2},{1,3},{2,0},{3,1},{4,6},{5,7},{6,4},{7,5},{8,10},{9,11},{10,... | collective-permute-start | bytes 196616 | tf_op jit(solution)/shard_map/ppermute | solution.py:16
  10.3 1.1 %collective-permute-done.1 = bf16[4,4224]{1,0:T(4,128)(2,1)S(1)} collective-permute-done((bf16[4,4224]{1,0:T(4,128)(2,1)S(1)}, bf16[4,4224]{1,0:T(4,128)(2,1)S(1)}, u32[]{:S(2)}, u32[]{:S(2)}) %collective-permute-start.1) | collective-permute-done | bytes 33824 | tf_op jit(solution)/shard_map/ppermute | solution.py:16
  11.4 2.9 %collective-permute-done.2 = bf16[4,4224]{1,0:T(4,128)(2,1)S(1)} collective-permute-done((bf16[4,4224]{1,0:T(4,128)(2,1)S(1)}, bf16[4,4224]{1,0:T(4,128)(2,1)S(1)}, u32[]{:S(2)}, u32[]{:S(2)}) %collective-permute-start.2) | collective-permute-done | bytes 33824 | tf_op jit(solution)/shard_map/ppermute | solution.py:16
  14.3 0.1 pad_maximum_fusion.2
  14.4 1.6 %collective-permute-start.3 = (bf16[16,4224]{1,0:T(8,128)(2,1)S(1)}, bf16[16,4224]{1,0:T(8,128)(2,1)S(1)}, u32[]{:S(2)}, u32[]{:S(2)}) collective-permute-start(bf16[16,4224]{1,0:T(8,128)(2,1)S(1)} %pad_maximum_fusion.2), channel_id=1, source_target_pairs={{0,2},{1,3},{2,0},{3,1},{4,6},{5,7},{6,4},{7,5},{8,10},{9,11},{10,... | collective-permute-start | bytes 405512 | tf_op jit(solution)/shard_map/ppermute | solution.py:16
  15.9 1.0 %constant_dynamic-slice_fusion = (bf16[32,2048]{1,0:T(8,128)(2,1)S(1)}, bf16[32,2048]{1,0:T(8,128)(2,1)S(1)}) fusion(bf16[32,4096]{1,0:T(8,128)(2,1)} %bitcast.9, s32[]{:T(128)S(6)} %select_n.31, s32[]{:T(128)S(6)} %select_n.30), kind=kLoop, calls=%fused_computation.10 | loop fusion | bytes 524296 | tf_op jit(solution)/shard_map/dynamic_slice | solution.py:163
  16.9 0.6 %collective-permute-start.10 = (bf16[32,2048]{1,0:T(8,128)(2,1)S(1)}, bf16[32,2048]{1,0:T(8,128)(2,1)S(1)}, u32[]{:S(2)}, u32[]{:S(2)}) collective-permute-start(bf16[32,2048]{1,0:T(8,128)(2,1)S(1)} %get-tuple-element.19), channel_id=1, source_target_pairs={{0,2},{1,3},{2,0},{3,1},{4,6},{5,7},{6,4},{7,5},{8,10},{9,11},{10,... | collective-permute-start | bytes 393224 | tf_op jit(solution)/shard_map/ppermute | solution.py:16
  17.5 2.9 %collective-permute-done.3 = bf16[16,4224]{1,0:T(8,128)(2,1)S(1)} collective-permute-done((bf16[16,4224]{1,0:T(8,128)(2,1)S(1)}, bf16[16,4224]{1,0:T(8,128)(2,1)S(1)}, u32[]{:S(2)}, u32[]{:S(2)}) %collective-permute-start.3) | collective-permute-done | bytes 135200 | tf_op jit(solution)/shard_map/ppermute | solution.py:16
  20.4 0.2 concatenate.21.near_ref
  20.6 0.1 collective-permute-start.4
  20.7 0.9 %pad_maximum_fusion.3 = bf16[64,1024]{1,0:T(8,128)(2,1)S(1)} fusion(bf16[32,1024]{1,0:T(8,128)(2,1)S(1)} %collective-permute-done.8, bf16[32,1024]{1,0:T(8,128)(2,1)} %bitcast.11), kind=kLoop, calls=%fused_computation.9 | loop fusion | flops 262144 | bytes 262144 | tf_op jit(solution)/shard_map/concatenate | solution.py:165
  21.5 0.6 %collective-permute-start.9 = (bf16[64,1024]{1,0:T(8,128)(2,1)S(1)}, bf16[64,1024]{1,0:T(8,128)(2,1)S(1)}, u32[]{:S(2)}, u32[]{:S(2)}) collective-permute-start(bf16[64,1024]{1,0:T(8,128)(2,1)S(1)} %pad_maximum_fusion.3), channel_id=1, source_target_pairs={{0,1},{1,0},{2,3},{3,2},{4,5},{5,4},{6,7},{7,6},{8,9},{9,8},{10,11... | collective-permute-start | bytes 393224 | tf_op jit(solution)/shard_map/ppermute | solution.py:16
  22.1 0.1 collective-permute-start.11
  22.2 0.9 %collective-permute-done.9 = bf16[64,1024]{1,0:T(8,128)(2,1)S(1)} collective-permute-done((bf16[64,1024]{1,0:T(8,128)(2,1)S(1)}, bf16[64,1024]{1,0:T(8,128)(2,1)S(1)}, u32[]{:S(2)}, u32[]{:S(2)}) %collective-permute-start.9) | collective-permute-done | bytes 131104 | tf_op jit(solution)/shard_map/ppermute | solution.py:16
  23.1 0.0 copy-start.1
  23.1 1.6 %copy-done.1 = bf16[1,4096,256]{2,1,0:T(8,128)(2,1)S(1)} copy-done((bf16[1,4096,256]{2,1,0:T(8,128)(2,1)S(1)}, bf16[1,4096,256]{2,1,0:T(8,128)(2,1)}, u32[]{:S(2)}) %copy-start.1) | copy-done | bytes 2097176
  24.7 0.9 %shard_map.92 = (bf16[64,256]{1,0:T(8,128)(2,1)S(1)}, bf16[64,128]{1,0:T(8,128)(2,1)S(1)}) custom-call(bf16[32,4224]{1,0:T(8,128)(2,1)S(1)} %concatenate.21.near_ref, bf16[32,4224]{1,0:T(8,128)(2,1)S(1)} %collective-permute-done.4.far_ref, bf16[1,4096,256]{2,1,0:T(8,128)(2,1)S(1)} %copy-done, bf16[1,4096,256]{2,1,0:T(8,128)(2,1)S(1)} %copy-done.1), custom_call_target="tpu_custom_call" | custom-call | tf_op jit(solution)/shard_map/pallas_call | solution.py:174
  25.6 0.0 copy-start.6
  25.6 0.4 collective-permute-start.5
  26.0 0.7 %collective-permute-start.6 = (bf16[64,256]{1,0:T(8,128)(2,1)S(1)}, bf16[64,256]{1,0:T(8,128)(2,1)S(1)}, u32[]{:S(2)}, u32[]{:S(2)}) collective-permute-start(bf16[64,256]{1,0:T(8,128)(2,1)S(1)} %get-tuple-element.15.refs_0_), channel_id=1, source_target_pairs={{0,2},{1,3},{2,0},{3,1},{4,6},{5,7},{6,4},{7,5},{8,10},{9,11},{10,... | collective-permute-start | bytes 98312 | tf_op jit(solution)/shard_map/ppermute | solution.py:16
  26.7 0.8 %collective-permute-start.7 = (bf16[64,256]{1,0:T(8,128)(2,1)S(1)}, bf16[64,256]{1,0:T(8,128)(2,1)S(1)}, u32[]{:S(2)}, u32[]{:S(2)}) collective-permute-start(bf16[64,256]{1,0:T(8,128)(2,1)S(1)} %get-tuple-element.15.refs_0_), channel_id=1, source_target_pairs={{0,3},{1,2},{2,1},{3,0},{4,7},{5,6},{6,5},{7,4},{8,11},{9,10},{10,... | collective-permute-start | bytes 98312 | tf_op jit(solution)/shard_map/ppermute | solution.py:16
  27.6 2.6 %collective-permute-done.6.refs_2_ = bf16[64,256]{1,0:T(8,128)(2,1)S(1)} collective-permute-done((bf16[64,256]{1,0:T(8,128)(2,1)S(1)}, bf16[64,256]{1,0:T(8,128)(2,1)S(1)}, u32[]{:S(2)}, u32[]{:S(2)}) %collective-permute-start.6) | collective-permute-done | bytes 32800 | tf_op jit(solution)/shard_map/ppermute | solution.py:16
  30.2 0.2 collective-permute-done.7.refs_3_
  30.4 0.7 %shard_map.93 = bf16[16,4,1024]{2,1,0:T(4,128)(2,1)S(1)} custom-call(bf16[64,256]{1,0:T(8,128)(2,1)S(1)} %get-tuple-element.15.refs_0_, bf16[64,256]{1,0:T(8,128)(2,1)S(1)} %collective-permute-done.5.refs_1_, bf16[64,256]{1,0:T(8,128)(2,1)S(1)} %collective-permute-done.6.refs_2_, bf16[64,256]{1,0:T(8,128)(2,1)S(1)} %collective-permute-done.7.refs_3_, ...), custom_call_target="tpu_custom_call" | custom-call | tf_op jit(solution)/shard_map/pallas_call | solution.py:186
  31.1 10.5 %all_to_all.5.back_ref = bf16[16,4,1024]{2,1,0:T(4,128)(2,1)S(1)} all-to-all(bf16[16,4,1024]{2,1,0:T(4,128)(2,1)S(1)} %shard_map.93), channel_id=1, replica_groups=mesh['groups'=2,'expert'=4,'request'=4] {'expert','request'}, dimensions={0} | all-to-all | bytes 262144 | tf_op jit(solution)/shard_map/all_to_all | solution.py:195
  41.7 1.5 %shard_map.94 = bf16[64,4096]{1,0:T(8,128)(2,1)} custom-call(s32[8,64]{1,0:T(8,128)S(1)} %bitcast.6, f32[8,64]{1,0:T(8,128)S(1)} %bitcast.7, bf16[16,4,1024]{2,1,0:T(4,128)(2,1)S(1)} %all_to_all.5.back_ref), custom_call_target="tpu_custom_call" | custom-call | tf_op jit(solution)/shard_map/pallas_call | solution.py:196
  (22 shorter events, 0.1 us)
Async XLA Ops:
  0.0 23.1 %copy-start = (bf16[1,4096,256]{2,1,0:T(8,128)(2,1)S(1)}, bf16[1,4096,256]{2,1,0:T(8,128)(2,1)}, u32[]{:S(2)}) copy-start(bf16[1,4096,256]{2,1,0:T(8,128)(2,1)} %gate_ref.1) | copy-start | bytes 6291460
  0.0 1.2 %copy-start.3 = (bf16[64,4096]{1,0:T(8,128)(2,1)S(1)}, bf16[64,4096]{1,0:T(8,128)(2,1)}, u32[]{:S(2)}) copy-start(bf16[64,4096]{1,0:T(8,128)(2,1)} %x_ref.1) | copy-start | bytes 1572868
  1.2 0.7 %copy-start.4 = (s32[64,8]{0,1:T(8,128)S(1)}, s32[64,8]{0,1:T(8,128)}, u32[]{:S(2)}) copy-start(s32[64,8]{0,1:T(8,128)} %param.10) | copy-start | bytes 6148
  1.9 0.7 %copy-start.7 = (s32[64]{0:T(128)S(1)}, s32[64]{0:T(128)}, u32[]{:S(2)}) copy-start(s32[64]{0:T(128)} %param.11) | copy-start | bytes 772
  2.5 20.5 %copy-start.8 = (bf16[1,4,8,1024]{3,2,1,0:T(8,128)(2,1)S(1)}, bf16[1,4,8,1024]{3,2,1,0:T(8,128)(2,1)}, u32[]{:S(2)}) copy-start(bf16[1,4,8,1024]{3,2,1,0:T(8,128)(2,1)} %param.16) | copy-start | bytes 196612
  2.9 7.4 %collective-permute-start = (bf16[4,4224]{1,0:T(4,128)(2,1)S(1)}, bf16[4,4224]{1,0:T(4,128)(2,1)S(1)}, u32[]{:S(2)}, u32[]{:S(2)}) collective-permute-start(bf16[4,4224]{1,0:T(4,128)(2,1)S(1)} %get-tuple-element.12), channel_id=1, source_target_pairs={{0,4},{4,0},{8,12},{12,8},{1,5},{5,1},{9,13},{13,9},{2,6},{6,2},{1... | collective-permute-start | bytes 101384 | tf_op jit(solution)/shard_map/ppermute | solution.py:16
  6.0 5.4 %collective-permute-start.1 = (bf16[4,4224]{1,0:T(4,128)(2,1)S(1)}, bf16[4,4224]{1,0:T(4,128)(2,1)S(1)}, u32[]{:S(2)}, u32[]{:S(2)}) collective-permute-start(bf16[4,4224]{1,0:T(4,128)(2,1)S(1)} %get-tuple-element.13), channel_id=1, source_target_pairs={{0,8},{4,12},{8,0},{12,4},{1,9},{5,13},{9,1},{13,5},{2,10},{6,14},... | collective-permute-start | bytes 101384 | tf_op jit(solution)/shard_map/ppermute | solution.py:16
  8.6 5.7 %collective-permute-start.2 = (bf16[4,4224]{1,0:T(4,128)(2,1)S(1)}, bf16[4,4224]{1,0:T(4,128)(2,1)S(1)}, u32[]{:S(2)}, u32[]{:S(2)}) collective-permute-start(bf16[4,4224]{1,0:T(4,128)(2,1)S(1)} %get-tuple-element.14), channel_id=1, source_target_pairs={{0,12},{4,8},{8,4},{12,0},{1,13},{5,9},{9,5},{13,1},{2,14},{6,10},... | collective-permute-start | bytes 101384 | tf_op jit(solution)/shard_map/ppermute | solution.py:16
  8.6 12.1 %collective-permute-start.8 = (bf16[32,1024]{1,0:T(8,128)(2,1)}, bf16[32,1024]{1,0:T(8,128)(2,1)S(1)}, u32[]{:S(2)}, u32[]{:S(2)}) collective-permute-start(bf16[32,1024]{1,0:T(8,128)(2,1)} %bitcast.10), channel_id=1, source_target_pairs={{0,2},{1,3},{2,0},{3,1},{4,6},{5,7},{6,4},{7,5},{8,10},{9,11},{10,... | collective-permute-start | bytes 196616 | tf_op jit(solution)/shard_map/ppermute | solution.py:16
  14.4 6.0 %collective-permute-start.3 = (bf16[16,4224]{1,0:T(8,128)(2,1)S(1)}, bf16[16,4224]{1,0:T(8,128)(2,1)S(1)}, u32[]{:S(2)}, u32[]{:S(2)}) collective-permute-start(bf16[16,4224]{1,0:T(8,128)(2,1)S(1)} %pad_maximum_fusion.2), channel_id=1, source_target_pairs={{0,2},{1,3},{2,0},{3,1},{4,6},{5,7},{6,4},{7,5},{8,10},{9,11},{10,... | collective-permute-start | bytes 405512 | tf_op jit(solution)/shard_map/ppermute | solution.py:16
  16.9 5.2 %collective-permute-start.10 = (bf16[32,2048]{1,0:T(8,128)(2,1)S(1)}, bf16[32,2048]{1,0:T(8,128)(2,1)S(1)}, u32[]{:S(2)}, u32[]{:S(2)}) collective-permute-start(bf16[32,2048]{1,0:T(8,128)(2,1)S(1)} %get-tuple-element.19), channel_id=1, source_target_pairs={{0,2},{1,3},{2,0},{3,1},{4,6},{5,7},{6,4},{7,5},{8,10},{9,11},{10,... | collective-permute-start | bytes 393224 | tf_op jit(solution)/shard_map/ppermute | solution.py:16
  20.6 2.5 %collective-permute-start.4 = (bf16[32,4224]{1,0:T(8,128)(2,1)S(1)}, bf16[32,4224]{1,0:T(8,128)(2,1)S(1)}, u32[]{:S(2)}, u32[]{:S(2)}) collective-permute-start(bf16[32,4224]{1,0:T(8,128)(2,1)S(1)} %concatenate.21.near_ref), channel_id=1, source_target_pairs={{0,1},{1,0},{2,3},{3,2},{4,5},{5,4},{6,7},{7,6},{8,9},{9,8},{10,11... | collective-permute-start | bytes 811016 | tf_op jit(solution)/shard_map/ppermute | solution.py:16
  21.5 1.5 %collective-permute-start.9 = (bf16[64,1024]{1,0:T(8,128)(2,1)S(1)}, bf16[64,1024]{1,0:T(8,128)(2,1)S(1)}, u32[]{:S(2)}, u32[]{:S(2)}) collective-permute-start(bf16[64,1024]{1,0:T(8,128)(2,1)S(1)} %pad_maximum_fusion.3), channel_id=1, source_target_pairs={{0,1},{1,0},{2,3},{3,2},{4,5},{5,4},{6,7},{7,6},{8,9},{9,8},{10,11... | collective-permute-start | bytes 393224 | tf_op jit(solution)/shard_map/ppermute | solution.py:16
  22.1 5.4 %collective-permute-start.11 = (bf16[64,1024]{1,0:T(8,128)(2,1)S(1)}, bf16[64,1024]{1,0:T(8,128)(2,1)S(1)}, u32[]{:S(2)}, u32[]{:S(2)}) collective-permute-start(bf16[64,1024]{1,0:T(8,128)(2,1)S(1)} %get-tuple-element.18), channel_id=1, source_target_pairs={{0,1},{1,0},{2,3},{3,2},{4,5},{5,4},{6,7},{7,6},{8,9},{9,8},{10,11... | collective-permute-start | bytes 393224 | tf_op jit(solution)/shard_map/ppermute | solution.py:16
  23.1 1.6 %copy-start.1 = (bf16[1,4096,256]{2,1,0:T(8,128)(2,1)S(1)}, bf16[1,4096,256]{2,1,0:T(8,128)(2,1)}, u32[]{:S(2)}) copy-start(bf16[1,4096,256]{2,1,0:T(8,128)(2,1)} %up_ref.1) | copy-start | bytes 6291460
  24.7 5.7 %copy-start.2 = (bf16[1,1024,1024]{2,1,0:T(8,128)(2,1)S(1)}, bf16[1,1024,1024]{2,1,0:T(8,128)(2,1)}, u32[]{:S(2)}) copy-start(bf16[1,1024,1024]{2,1,0:T(8,128)(2,1)} %refs_5_.1) | copy-start | bytes 6291460
  25.6 16.1 %copy-start.5 = (s32[64,8]{0,1:T(8,128)S(1)}, s32[64,8]{0,1:T(8,128)}, u32[]{:S(2)}) copy-start(s32[64,8]{0,1:T(8,128)} %param.10) | copy-start | bytes 6148
  25.6 16.1 %copy-start.6 = (f32[64,8]{0,1:T(8,128)S(1)}, f32[64,8]{0,1:T(8,128)}, u32[]{:S(2)}) copy-start(f32[64,8]{0,1:T(8,128)} %param.12) | copy-start | bytes 6148
  25.6 2.0 %collective-permute-start.5 = (bf16[64,256]{1,0:T(8,128)(2,1)S(1)}, bf16[64,256]{1,0:T(8,128)(2,1)S(1)}, u32[]{:S(2)}, u32[]{:S(2)}) collective-permute-start(bf16[64,256]{1,0:T(8,128)(2,1)S(1)} %get-tuple-element.15.refs_0_), channel_id=1, source_target_pairs={{0,1},{1,0},{2,3},{3,2},{4,5},{5,4},{6,7},{7,6},{8,9},{9,8},{10,11... | collective-permute-start | bytes 98312 | tf_op jit(solution)/shard_map/ppermute | solution.py:16
  26.0 4.2 %collective-permute-start.6 = (bf16[64,256]{1,0:T(8,128)(2,1)S(1)}, bf16[64,256]{1,0:T(8,128)(2,1)S(1)}, u32[]{:S(2)}, u32[]{:S(2)}) collective-permute-start(bf16[64,256]{1,0:T(8,128)(2,1)S(1)} %get-tuple-element.15.refs_0_), channel_id=1, source_target_pairs={{0,2},{1,3},{2,0},{3,1},{4,6},{5,7},{6,4},{7,5},{8,10},{9,11},{10,... | collective-permute-start | bytes 98312 | tf_op jit(solution)/shard_map/ppermute | solution.py:16
  26.7 3.7 %collective-permute-start.7 = (bf16[64,256]{1,0:T(8,128)(2,1)S(1)}, bf16[64,256]{1,0:T(8,128)(2,1)S(1)}, u32[]{:S(2)}, u32[]{:S(2)}) collective-permute-start(bf16[64,256]{1,0:T(8,128)(2,1)S(1)} %get-tuple-element.15.refs_0_), channel_id=1, source_target_pairs={{0,3},{1,2},{2,1},{3,0},{4,7},{5,6},{6,5},{7,4},{8,11},{9,10},{10,... | collective-permute-start | bytes 98312 | tf_op jit(solution)/shard_map/ppermute | solution.py:16

commit v2 on v1

v2 whole, which is shorter than its diff:
```python
import functools

import jax
import jax.numpy as jnp
from jax import lax
from jax.experimental import pallas as pl
from jax.experimental.pallas import tpu as pltpu
from jax.sharding import Mesh, PartitionSpec as P

CAP = 4
LANES = 128
PAIR = 2
REQUEST = ("quad", "pair")
VMEM = pl.BlockSpec(memory_space=pltpu.VMEM)
HBM = pl.BlockSpec(memory_space=pltpu.HBM)
PARAMS = pltpu.CompilerParams(vmem_limit_bytes=16 * 2**20)


def xor_permute(value, axis, offset):
    return lax.ppermute(value, axis, [(i, i ^ offset) for i in range(lax.axis_size(axis))])


def slot_values(ids, values, expert):
    tokens = ids.shape[1]
    match = ids == expert
    named = jnp.sum(match.astype(jnp.float32), axis=0, keepdims=True)
    row = lax.broadcasted_iota(jnp.int32, (tokens, tokens), 0)
    col = lax.broadcasted_iota(jnp.int32, (tokens, tokens), 1)
    earlier = (row < col).astype(jnp.bfloat16)
    rank = jnp.dot(named.astype(jnp.bfloat16), earlier, preferred_element_type=jnp.float32)
    slot = lax.broadcasted_iota(jnp.int32, (CAP, tokens), 0).astype(jnp.float32)
    held = jnp.logical_and(slot == rank, named > 0)
    value = jnp.sum(jnp.where(match, values, 0.0), axis=0, keepdims=True)
    return jnp.where(held, value, 0.0)


def in_hbm(*values):
    return [pltpu.with_memory_space_constraint(v, pltpu.HBM) for v in values]


def copy_all(pairs, sems):
    copies = [pltpu.make_async_copy(a, b, sems.at[i]) for i, (a, b) in enumerate(pairs)]
    for copy in copies:
        copy.start()
    return copies


def pack_kernel(quads, ids_hbm, req_hbm, x_hbm, first_hbm, second_hbm, *refs):
    factor_refs, out_refs, scratches = refs[:quads], refs[quads:-5], refs[-5:]
    ids_ref, req_ref, x_ref, scratch, sems = scratches
    half = second_hbm.shape[1] // quads
    pairs = [(ids_hbm, ids_ref), (req_hbm, req_ref), (x_hbm, x_ref)]
    for q, factor_ref in enumerate(factor_refs):
        at = pl.multiple_of((lax.axis_index("quad") ^ q) * half, half)
        pairs.append((second_hbm.at[:, pl.ds(at, half)], factor_ref.at[:, pl.ds(0, half)]))
        pairs.append((first_hbm, factor_ref.at[:, pl.ds(half, first_hbm.shape[1])]))
    copies = copy_all(pairs, sems)
    experts = len(out_refs)
    me = lax.axis_index("expert")
    width = x_ref.shape[1]
    copies[0].wait()
    copies[1].wait()
    ids = ids_ref[...]
    ones = jnp.ones(ids.shape, jnp.float32)
    table = jnp.concatenate([slot_values(ids, ones, me ^ s) for s in range(experts)], axis=0)
    owner = jnp.sum(table * (req_ref[...] + 1).astype(jnp.float32), axis=1, keepdims=True) - 1.0
    scratch[:, width:] = jnp.broadcast_to(owner, (owner.shape[0], LANES))
    copies[2].wait()
    scratch[:, :width] = jnp.dot(
        table.astype(jnp.bfloat16), x_ref[...], preferred_element_type=jnp.float32
    )
    for s, out_ref in enumerate(out_refs):
        out_ref[...] = scratch[pl.ds(s * CAP, CAP), :].astype(out_ref.dtype)
    for copy in copies[3:]:
        copy.wait()


def stage_kernel(
    ids_hbm, weight_hbm, gate_hbm, up_hbm, down_hbm, after_ref,
    table_ref, own_ref, down_ref, ids_ref, weight_ref, sems,
):
    part = gate_hbm.shape[2]
    pairs = [
        (ids_hbm, ids_ref),
        (weight_hbm, weight_ref),
        (gate_hbm.at[0], own_ref.at[:, pl.ds(0, part)]),
        (up_hbm.at[0], own_ref.at[:, pl.ds(part, part)]),
        (down_hbm.at[0], down_ref),
    ]
    copies = copy_all(pairs, sems)
    copies[0].wait()
    copies[1].wait()
    ids, weights = ids_ref[...], weight_ref[...]
    experts = table_ref.shape[0] // (3 * CAP)
    table = jnp.concatenate([slot_values(ids, weights, e) for e in range(experts)], axis=0)
    high = table.astype(jnp.bfloat16)
    rest = table - high.astype(jnp.float32)
    middle = rest.astype(jnp.bfloat16)
    low = (rest - middle.astype(jnp.float32)).astype(jnp.bfloat16)
    table_ref[...] = jnp.concatenate([low, middle, high], axis=0)
    for copy in copies[2:]:
        copy.wait()


def hidden_kernel(near_ref, far_ref, own_ref, peer_ref, hidden_ref, owner_ref):
    width = near_ref.shape[1] - LANES
    part = own_ref.shape[1] // PAIR
    rows = jnp.concatenate([near_ref[:, :width], far_ref[:, :width]], axis=0)
    owner_ref[...] = jnp.concatenate([near_ref[:, width:], far_ref[:, width:]], axis=0)
    for b, ref in enumerate((own_ref, peer_ref)):
        both = jnp.dot(rows, ref[...], preferred_element_type=jnp.float32)
        gate, up = both[:, :part], both[:, part:]
        hidden = gate / (1.0 + jnp.exp(-gate)) * up
        hidden_ref[:, b * part : (b + 1) * part] = hidden.astype(hidden_ref.dtype)


def down_kernel(order, n_req, cols, *refs):
    quads = len(order)
    hid_refs, factor_refs = refs[:quads], refs[quads : 3 * quads]
    owner_ref, own_ref, peer_ref, out_ref, whole, scratch = refs[3 * quads :]
    me_e, me_q, me_p = (lax.axis_index(a) for a in ("expert", "quad", "pair"))
    me_r = me_q * PAIR + me_p
    total, depth = whole.shape
    block = total // quads
    part = hid_refs[0].shape[1] // PAIR
    for q, hid_ref in enumerate(hid_refs):
        picks = [order.index(o ^ q) for o in order]
        hid = jnp.concatenate([hid_ref[j * block : (j + 1) * block, :] for j in picks], axis=0)
        for b in range(PAIR):
            at = pl.multiple_of((me_r ^ (q * PAIR + b)) * part, part)
            whole[:, pl.ds(at, part)] = hid[:, b * part : (b + 1) * part]
    hidden = whole[...]
    owner = owner_ref[:, :1].astype(jnp.int32)
    per_dev = factor_refs[0].shape[0]
    rank = per_dev // n_req
    lane = lax.broadcasted_iota(jnp.int32, (1, per_dev * len(factor_refs)), 1)
    first = jnp.concatenate([ref[:, PAIR * cols :] for ref in factor_refs], axis=0)
    low = lax.dot_general(
        hidden, first, (((1,), (1,)), ((), ())), preferred_element_type=jnp.float32
    )
    holder = jnp.zeros_like(lane)
    for i in range(len(factor_refs)):
        mine = (me_r ^ i) * n_req + (lane - i * per_dev) // rank
        holder = jnp.where(lane // per_dev == i, mine, holder)
    chosen = jnp.where(holder == owner, low, 0.0).astype(jnp.bfloat16)
    for b, ref in enumerate((own_ref, peer_ref)):
        at = pl.ds(pl.multiple_of((me_p ^ b) * cols, cols), cols)
        second = jnp.concatenate([f[:, at] for f in factor_refs], axis=0)
        scratch[:, at] = jnp.dot(
            hidden, ref[...], preferred_element_type=jnp.float32
        ) + jnp.dot(chosen, second, preferred_element_type=jnp.float32)
    experts = block // CAP
    for i, o in enumerate(order):
        for s in range(experts):
            target = (me_e ^ s) * quads + (me_q ^ o)
            rows = scratch[pl.ds(i * block + s * CAP, CAP), :]
            out_ref[target] = rows.astype(out_ref.dtype)


def combine_kernel(table_ref, back_ref, mixed_hbm, scratch, done, sems):
    experts = scratch.shape[0] // CAP
    quads = done.shape[0]
    cols = done.shape[2]
    copies = []
    for q in range(quads):
        for e in range(experts):
            scratch[pl.ds(e * CAP, CAP), :] = back_ref[e * quads + q].astype(jnp.float32)
        rows = scratch[...].astype(jnp.bfloat16)
        mixed = lax.dot_general(
            table_ref[...], jnp.concatenate([rows] * 3, axis=0), (((0,), (0,)), ((), ())),
            preferred_element_type=jnp.float32,
        )
        done[q] = mixed.astype(done.dtype)
        at = pl.ds(q * cols, cols)
        copies.append(pltpu.make_async_copy(done.at[q], mixed_hbm.at[:, at], sems.at[q]))
        copies[-1].start()
    for copy in copies:
        copy.wait()


def body(
    token_input,
    token_expert_index,
    token_request_index,
    choice_weight,
    gate_weight,
    up_weight,
    down_weight,
    adapter_first_weight,
    adapter_second_weight,
):
    experts, quads = lax.axis_size("expert"), lax.axis_size("quad")
    tokens, width = token_input.shape
    part = gate_weight.shape[2]
    cols = down_weight.shape[2]
    n_req, rank, depth = adapter_first_weight.shape[1:]
    bf16, f32 = jnp.bfloat16, jnp.float32
    dma = pltpu.SemaphoreType.DMA
    own = n_req * rank

    ids = token_expert_index.T
    weights = choice_weight.T
    outs = pl.pallas_call(
        functools.partial(pack_kernel, quads),
        out_shape=[jax.ShapeDtypeStruct((own, width // quads + depth), bf16)] * quads
        + [jax.ShapeDtypeStruct((CAP, width + LANES), bf16)] * experts,
        in_specs=[HBM] * 5,
        out_specs=[VMEM] * (quads + experts),
        scratch_shapes=[
            pltpu.VMEM(ids.shape, jnp.int32),
            pltpu.VMEM((1, tokens), jnp.int32),
            pltpu.VMEM(token_input.shape, bf16),
            pltpu.VMEM((experts * CAP, width + LANES), f32),
            dma((3 + 2 * quads,)),
        ],
        compiler_params=PARAMS,
    )(
        *in_hbm(
            ids,
            token_request_index[None],
            token_input,
            adapter_first_weight.reshape(own, depth),
            adapter_second_weight.reshape(own, width),
        )
    )
    factors, packed = outs[:quads], outs[quads:]

    table, mine, down = pl.pallas_call(
        stage_kernel,
        out_shape=[
            jax.ShapeDtypeStruct((3 * experts * CAP, tokens), bf16),
            jax.ShapeDtypeStruct((width, PAIR * part), bf16),
            jax.ShapeDtypeStruct((depth, cols), bf16),
        ],
        in_specs=[HBM] * 5 + [VMEM],
        out_specs=[VMEM] * 3,
        scratch_shapes=[
            pltpu.VMEM(ids.shape, jnp.int32),
            pltpu.VMEM(weights.shape, f32),
            dma((5,)),
        ],
        compiler_params=PARAMS,
    )(*in_hbm(ids, weights, gate_weight, up_weight, down_weight), packed[0])

    blocks = [packed[0]] + [xor_permute(packed[s], "expert", s) for s in range(1, experts)]
    factors = [factors[0]] + [xor_permute(factors[q], REQUEST, q * PAIR) for q in range(1, quads)]
    mine, home = lax.optimization_barrier((mine, factors[0]))
    factors[0], peers = home, [xor_permute(home, REQUEST, 1)]
    blocks, mine, factors[1:] = lax.optimization_barrier((blocks, mine, factors[1:]))
    theirs = xor_permute(mine, REQUEST, 1)
    rows = jnp.concatenate(blocks, axis=0)
    rows, down, factors[1:] = lax.optimization_barrier((rows, down, factors[1:]))
    down2 = xor_permute(down, REQUEST, 1)
    peers += [xor_permute(f, REQUEST, 1) for f in factors[1:]]
    factors = [v for both in zip(factors, peers) for v in both]
    order = [0]
    bit = quads // 2
    while True:
        near = rows
        far = xor_permute(rows, REQUEST, bit * PAIR)
        order = order + [o ^ bit for o in order]
        bit //= 2
        if not bit:
            break
        rows = jnp.concatenate([near, far], axis=0)

    total = experts * CAP * quads
    hidden, owner = pl.pallas_call(
        hidden_kernel,
        out_shape=[
            jax.ShapeDtypeStruct((total, PAIR * part), bf16),
            jax.ShapeDtypeStruct((total, LANES), bf16),
        ],
        in_specs=[VMEM] * 4,
        out_specs=[VMEM] * 2,
        compiler_params=PARAMS,
    )(near, far, mine, theirs)

    shared = [hidden] + [xor_permute(hidden, REQUEST, q * PAIR) for q in range(1, quads)]
    out = pl.pallas_call(
        functools.partial(down_kernel, order, n_req, cols),
        out_shape=jax.ShapeDtypeStruct((experts * quads, CAP, PAIR * cols), bf16),
        in_specs=[VMEM] * (3 * quads + 3),
        out_specs=VMEM,
        scratch_shapes=[
            pltpu.VMEM((total, depth), bf16),
            pltpu.VMEM((total, PAIR * cols), f32),
        ],
        compiler_params=PARAMS,
    )(*shared, *factors, owner, down, down2)

    back = lax.all_to_all(out, ("expert", "quad"), 0, 0, tiled=True)
    return pl.pallas_call(
        combine_kernel,
        out_shape=jax.ShapeDtypeStruct((tokens, width), bf16),
        in_specs=[VMEM] * 2,
        out_specs=HBM,
        scratch_shapes=[
            pltpu.VMEM((experts * CAP, PAIR * cols), f32),
            pltpu.VMEM((quads, tokens, PAIR * cols), bf16),
            dma((quads,)),
        ],
        compiler_params=PARAMS,
    )(table, back)


def solution(mesh):
    groups, experts, requests = mesh.devices.shape
    fine = Mesh(
        mesh.devices.reshape(groups, experts, requests // PAIR, PAIR), ("groups", "expert", *REQUEST)
    )
    everyone = P(("groups", "expert", *REQUEST), None)
    weight = P("expert", None, REQUEST)
    adapter = P(("groups", "expert"), REQUEST, None, None)
    in_specs = (everyone, everyone, P(everyone[0]), everyone) + (weight,) * 3 + (adapter,) * 2
    return jax.shard_map(body, mesh=fine, in_specs=in_specs, out_specs=everyone, check_vma=False)
```

time: 43.5 us -> 39.1 us (0.90)
  local copies, waits for them, and re-layouts: 5.32 us -> 0 us
  Pallas kernels: 3.48 us -> 8.02 us
  starting transfers between devices: 12.2 us -> 9.61 us
  other arithmetic: 0.99 us -> 0.08 us
  waiting for transfers between devices: 10.6 us -> 11.4 us
  blocking collectives: 10.5 us -> 9.74 us
    pallas_call x3 -> x4, Pallas kernels: 1.95 us -> 6.97 us  [the longest x1 2.93 us: body(): pl.pallas_call(stage_kernel, out_shape=[jax.ShapeDtypeStruct((3 * experts...]
    unnamed x18 -> x0, local copies, waits for them, and re-layouts: 4.14 us -> none
    ppermute x12 -> x10, starting transfers between devices: 12.2 us -> 9.61 us  [xor_permute(): lax.ppermute(value, axis, [(i, i ^ offset) for i in range(lax.axis_size(a...]
    dynamic_slice x1 -> x0, local copies, waits for them, and re-layouts: 0.98 us -> none  [body(): give = lax.dynamic_slice_in_dim(second, (1 - upper) * half, half, 1)]
    concatenate x5 -> x1, other arithmetic: 0.99 us -> 0.08 us  [body(): rows = jnp.concatenate(blocks, axis=0)]
    ppermute x12 -> x10, waiting for transfers between devices: 10.6 us -> 11.4 us  [xor_permute(): lax.ppermute(value, axis, [(i, i ^ offset) for i in range(lax.axis_size(a...]
    all_to_all x1, blocking collectives: 10.5 us -> 9.74 us  [body(): back = lax.all_to_all(out, ('expert', 'quad'), 0, 0, tiled=True)]
    pallas_call x1, Pallas kernels: 1.53 us -> 1.05 us  [body(): pl.pallas_call(combine_kernel, out_shape=jax.ShapeDtypeStruct((tokens, wi...]
  transfers between devices with their start and end apart: 12 -> 10, of which waited for: 6 -> 6; matrix products, arithmetic and copies ran while one was open for 5% -> 0% of each run, Pallas kernels for 2% -> 12%
where the time goes in v2:
time: 39.1 us; the launch traced here: 38.9 us
  waiting for transfers between devices  11.4 us (29%)
  blocking collectives  9.74 us (25%)
  starting transfers between devices  9.61 us (25%)
  Pallas kernels  8.02 us (21%)
    ppermute x10, waiting for transfers between devices, xor_permute(): lax.ppermute(value, axis, [(i, i ^ offset) for i in range(lax.axis_size(a...  11.4 us
    all_to_all x1, blocking collectives, body(): back = lax.all_to_all(out, ('expert', 'quad'), 0, 0, tiled=True)  9.74 us
    ppermute x10, starting transfers between devices, xor_permute(): lax.ppermute(value, axis, [(i, i ^ offset) for i in range(lax.axis_size(a...  9.61 us
    pallas_call x1, Pallas kernels, body(): pl.pallas_call(stage_kernel, out_shape=[jax.ShapeDtypeStruct((3 * experts...  2.93 us
    pallas_call x1, Pallas kernels, body(): pl.pallas_call(hidden_kernel, out_shape=[jax.ShapeDtypeStruct((total, PAI...  1.55 us
    pallas_call x1, Pallas kernels, body(): pl.pallas_call(functools.partial(pack_kernel, quads), out_shape=[jax.Shap...  1.35 us
    pallas_call x1, Pallas kernels, body(): pl.pallas_call(functools.partial(down_kernel, order, n_req, cols), out_sh...  1.14 us
    pallas_call x1, Pallas kernels, body(): pl.pallas_call(combine_kernel, out_shape=jax.ShapeDtypeStruct((tokens, wi...  1.05 us
  transfers between devices with their start and end apart: 10, of which 6 were waited for; matrix products, arithmetic and copies ran while one was open for 0% of the time, Pallas kernels for 12%

profile of v2, /device:TPU:0, one launch (start us, length us, event | category | flops | bytes accessed | tf_op | source)
XLA Modules:
  0.0 38.9 jit_solution(14671758390123286376)
XLA Ops:
  0.0 1.4 %shard_map.91 = (bf16[32,3072]{1,0:T(8,128)(2,1)S(1)}, bf16[32,3072]{1,0:T(8,128)(2,1)S(1)}, bf16[4,4224]{1,0:T(4,128)(2,1)S(1)}, bf16[4,4224]{1,0:T(4,128)(2,1)...) custom-call(s32[8,64]{1,0:T(8,128)} %bitcast.7, s32[1,64]{1,0:T(1,128)} %bitcast.10, ...), custom_call_target="tpu_custom_call" | custom-call | tf_op jit(solution)/shard_map/pallas_call | solution.py:203
  1.4 3.0 %collective-permute-start.3 = (bf16[32,3072]{1,0:T(8,128)(2,1)S(1)}, bf16[32,3072]{1,0:T(8,128)(2,1)S(1)}, u32[]{:S(2)}, u32[]{:S(2)}) collective-permute-start(bf16[32,3072]{1,0:T(8,128)(2,1)S(1)} %get-tuple-element.35), channel_id=1, source_target_pairs={{0,2},{1,3},{2,0},{3,1},{4,6},{5,7},{6,4},{7,5},{8,10},{9,11},{10,... | collective-permute-start | bytes 589832 | tf_op jit(solution)/shard_map/ppermute | solution.py:20
  4.4 1.6 %collective-permute-start = (bf16[4,4224]{1,0:T(4,128)(2,1)S(1)}, bf16[4,4224]{1,0:T(4,128)(2,1)S(1)}, u32[]{:S(2)}, u32[]{:S(2)}) collective-permute-start(bf16[4,4224]{1,0:T(4,128)(2,1)S(1)} %get-tuple-element.29), channel_id=1, source_target_pairs={{0,4},{4,0},{8,12},{12,8},{1,5},{5,1},{9,13},{13,9},{2,6},{6,2},{1... | collective-permute-start | bytes 101384 | tf_op jit(solution)/shard_map/ppermute | solution.py:20
  5.9 2.6 %collective-permute-start.1 = (bf16[4,4224]{1,0:T(4,128)(2,1)S(1)}, bf16[4,4224]{1,0:T(4,128)(2,1)S(1)}, u32[]{:S(2)}, u32[]{:S(2)}) collective-permute-start(bf16[4,4224]{1,0:T(4,128)(2,1)S(1)} %get-tuple-element.30), channel_id=1, source_target_pairs={{0,8},{4,12},{8,0},{12,4},{1,9},{5,13},{9,1},{13,5},{2,10},{6,14},... | collective-permute-start | bytes 101384 | tf_op jit(solution)/shard_map/ppermute | solution.py:20
  8.5 0.2 collective-permute-start.2
  8.8 2.9 %shard_map.92 = (bf16[48,64]{1,0:T(8,128)(2,1)S(1)}, bf16[4096,512]{1,0:T(8,128)(2,1)S(1)}, bf16[1024,1024]{1,0:T(8,128)(2,1)S(1)}) custom-call(s32[8,64]{1,0:T(8,128)} %bitcast.8, f32[8,64]{1,0:T(8,128)} %bitcast.9, bf16[1,4096,256]{2,1,0:T(8,128)(2,1)} %gate_hbm.1, bf16[1,4096,256]{2,1,0:T(8,128)(2,1)} %up_hbm.1, bf16[1,1024,1024]{2,1,0:T(8,128)(2,1)} %down_hbm.1, ...), custom_call_target="tpu_custom_call" | custom-call | tf_op jit(solution)/shard_map/pallas_call | solution.py:228
  11.7 0.0 collective-permute-done
  11.7 0.0 collective-permute-done.1
  11.7 2.5 %collective-permute-done.2 = bf16[4,4224]{1,0:T(4,128)(2,1)S(1)} collective-permute-done((bf16[4,4224]{1,0:T(4,128)(2,1)S(1)}, bf16[4,4224]{1,0:T(4,128)(2,1)S(1)}, u32[]{:S(2)}, u32[]{:S(2)}) %collective-permute-start.2) | collective-permute-done | bytes 33824 | tf_op jit(solution)/shard_map/ppermute | solution.py:20
  14.3 0.0 collective-permute-done.3.refs_4_
  14.3 0.0 collective-permute-start.5
  14.3 0.1 pad_maximum_fusion.near_ref
  14.4 0.6 %collective-permute-start.9 = (bf16[1024,1024]{1,0:T(8,128)(2,1)S(1)}, bf16[1024,1024]{1,0:T(8,128)(2,1)S(1)}, u32[]{:S(2)}, u32[]{:S(2)}) collective-permute-start(bf16[1024,1024]{1,0:T(8,128)(2,1)S(1)} %get-tuple-element.48.refs_7_), channel_id=1, source_target_pairs={{0,1},{1,0},{2,3},{3,2},{4,5},{5,4},{6,7},{7,6},{8,9},{9,8},{10,11... | collective-permute-start | bytes 6291464 | tf_op jit(solution)/shard_map/ppermute | solution.py:20
  14.9 0.1 collective-permute-start.7
  15.0 0.4 %collective-permute-start.8 = (bf16[32,3072]{1,0:T(8,128)(2,1)S(1)}, bf16[32,3072]{1,0:T(8,128)(2,1)S(1)}, u32[]{:S(2)}, u32[]{:S(2)}) collective-permute-start(bf16[32,3072]{1,0:T(8,128)(2,1)S(1)} %collective-permute-done.3.refs_4_), channel_id=1, source_target_pairs={{0,1},{1,0},{2,3},{3,2},{4,5},{5,4},{6,7},{7,6},{8,9},{9,8},{10,11... | collective-permute-start | bytes 589832 | tf_op jit(solution)/shard_map/ppermute | solution.py:20
  15.4 0.5 %collective-permute-start.4 = (bf16[16,4224]{1,0:T(8,128)(2,1)S(1)}, bf16[16,4224]{1,0:T(8,128)(2,1)S(1)}, u32[]{:S(2)}, u32[]{:S(2)}) collective-permute-start(bf16[16,4224]{1,0:T(8,128)(2,1)S(1)} %pad_maximum_fusion.near_ref), channel_id=1, source_target_pairs={{0,2},{1,3},{2,0},{3,1},{4,6},{5,7},{6,4},{7,5},{8,10},{9,11},{10,... | collective-permute-start | bytes 405512 | tf_op jit(solution)/shard_map/ppermute | solution.py:20
  16.0 5.0 %collective-permute-done.4.far_ref = bf16[16,4224]{1,0:T(8,128)(2,1)S(1)} collective-permute-done((bf16[16,4224]{1,0:T(8,128)(2,1)S(1)}, bf16[16,4224]{1,0:T(8,128)(2,1)S(1)}, u32[]{:S(2)}, u32[]{:S(2)}) %collective-permute-start.4) | collective-permute-done | bytes 135200 | tf_op jit(solution)/shard_map/ppermute | solution.py:20
  21.0 0.4 %collective-permute-done.5.peer_ref = bf16[4096,512]{1,0:T(8,128)(2,1)S(1)} collective-permute-done((bf16[4096,512]{1,0:T(8,128)(2,1)S(1)}, bf16[4096,512]{1,0:T(8,128)(2,1)S(1)}, u32[]{:S(2)}, u32[]{:S(2)}) %collective-permute-start.5) | collective-permute-done | bytes 4194336 | tf_op jit(solution)/shard_map/ppermute | solution.py:20
  21.4 1.5 %shard_map.93 = (bf16[32,512]{1,0:T(8,128)(2,1)S(1)}, bf16[32,128]{1,0:T(8,128)(2,1)S(1)}) custom-call(bf16[16,4224]{1,0:T(8,128)(2,1)S(1)} %pad_maximum_fusion.near_ref, bf16[16,4224]{1,0:T(8,128)(2,1)S(1)} %collective-permute-done.4.far_ref, bf16[4096,512]{1,0:T(8,128)(2,1)S(1)} %get-tuple-element.43.own_ref, ...), custom_call_target="tpu_custom_call" | custom-call | tf_op jit(solution)/shard_map/pallas_call | solution.py:268
  23.0 0.6 %collective-permute-start.6 = (bf16[32,512]{1,0:T(8,128)(2,1)S(1)}, bf16[32,512]{1,0:T(8,128)(2,1)S(1)}, u32[]{:S(2)}, u32[]{:S(2)}) collective-permute-start(bf16[32,512]{1,0:T(8,128)(2,1)S(1)} %get-tuple-element.44.refs_0_), channel_id=1, source_target_pairs={{0,2},{1,3},{2,0},{3,1},{4,6},{5,7},{6,4},{7,5},{8,10},{9,11},{10,... | collective-permute-start | bytes 98312 | tf_op jit(solution)/shard_map/ppermute | solution.py:20
  23.6 1.1 %collective-permute-done.7.refs_3_ = bf16[32,3072]{1,0:T(8,128)(2,1)S(1)} collective-permute-done((bf16[32,3072]{1,0:T(8,128)(2,1)S(1)}, bf16[32,3072]{1,0:T(8,128)(2,1)S(1)}, u32[]{:S(2)}, u32[]{:S(2)}) %collective-permute-start.7) | collective-permute-done | bytes 196640 | tf_op jit(solution)/shard_map/ppermute | solution.py:20
  24.7 0.3 collective-permute-done.8.refs_5_
  25.0 0.0 collective-permute-done.9.refs_8_
  25.0 2.0 %collective-permute-done.6.refs_1_ = bf16[32,512]{1,0:T(8,128)(2,1)S(1)} collective-permute-done((bf16[32,512]{1,0:T(8,128)(2,1)S(1)}, bf16[32,512]{1,0:T(8,128)(2,1)S(1)}, u32[]{:S(2)}, u32[]{:S(2)}) %collective-permute-start.6) | collective-permute-done | bytes 32800 | tf_op jit(solution)/shard_map/ppermute | solution.py:20
  27.0 1.1 %shard_map.94 = bf16[8,4,2048]{2,1,0:T(4,128)(2,1)S(1)} custom-call(bf16[32,512]{1,0:T(8,128)(2,1)S(1)} %get-tuple-element.44.refs_0_, bf16[32,512]{1,0:T(8,128)(2,1)S(1)} %collective-permute-done.6.refs_1_, bf16[32,3072]{1,0:T(8,128)(2,1)S(1)} %get-tuple-element.45.refs_2_, bf16[32,3072]{1,0:T(8,128)(2,1)S(1)} %collective-permute-done.7.refs_3_, ...), custom_call_target="tpu_custom_call" | custom-call | tf_op jit(solution)/shard_map/pallas_call | solution.py:280
  28.1 9.7 %all_to_all.5.back_ref = bf16[8,4,2048]{2,1,0:T(4,128)(2,1)S(1)} all-to-all(bf16[8,4,2048]{2,1,0:T(4,128)(2,1)S(1)} %shard_map.94), channel_id=1, replica_groups=mesh['groups'=2,'expert'=4,'quad'=2,'pair'=2] {'expert','quad'}, dimensions={0} | all-to-all | bytes 262144 | tf_op jit(solution)/shard_map/all_to_all | solution.py:292
  37.8 1.1 %shard_map.95 = bf16[64,4096]{1,0:T(8,128)(2,1)} custom-call(bf16[48,64]{1,0:T(8,128)(2,1)S(1)} %get-tuple-element.28.table_ref, bf16[8,4,2048]{2,1,0:T(4,128)(2,1)S(1)} %all_to_all.5.back_ref), custom_call_target="tpu_custom_call" | custom-call | tf_op jit(solution)/shard_map/pallas_call | solution.py:293
Async XLA Ops:
  1.4 12.9 %collective-permute-start.3 = (bf16[32,3072]{1,0:T(8,128)(2,1)S(1)}, bf16[32,3072]{1,0:T(8,128)(2,1)S(1)}, u32[]{:S(2)}, u32[]{:S(2)}) collective-permute-start(bf16[32,3072]{1,0:T(8,128)(2,1)S(1)} %get-tuple-element.35), channel_id=1, source_target_pairs={{0,2},{1,3},{2,0},{3,1},{4,6},{5,7},{6,4},{7,5},{8,10},{9,11},{10,... | collective-permute-start | bytes 589832 | tf_op jit(solution)/shard_map/ppermute | solution.py:20
  4.4 7.3 %collective-permute-start = (bf16[4,4224]{1,0:T(4,128)(2,1)S(1)}, bf16[4,4224]{1,0:T(4,128)(2,1)S(1)}, u32[]{:S(2)}, u32[]{:S(2)}) collective-permute-start(bf16[4,4224]{1,0:T(4,128)(2,1)S(1)} %get-tuple-element.29), channel_id=1, source_target_pairs={{0,4},{4,0},{8,12},{12,8},{1,5},{5,1},{9,13},{13,9},{2,6},{6,2},{1... | collective-permute-start | bytes 101384 | tf_op jit(solution)/shard_map/ppermute | solution.py:20
  5.9 5.8 %collective-permute-start.1 = (bf16[4,4224]{1,0:T(4,128)(2,1)S(1)}, bf16[4,4224]{1,0:T(4,128)(2,1)S(1)}, u32[]{:S(2)}, u32[]{:S(2)}) collective-permute-start(bf16[4,4224]{1,0:T(4,128)(2,1)S(1)} %get-tuple-element.30), channel_id=1, source_target_pairs={{0,8},{4,12},{8,0},{12,4},{1,9},{5,13},{9,1},{13,5},{2,10},{6,14},... | collective-permute-start | bytes 101384 | tf_op jit(solution)/shard_map/ppermute | solution.py:20
  8.5 5.7 %collective-permute-start.2 = (bf16[4,4224]{1,0:T(4,128)(2,1)S(1)}, bf16[4,4224]{1,0:T(4,128)(2,1)S(1)}, u32[]{:S(2)}, u32[]{:S(2)}) collective-permute-start(bf16[4,4224]{1,0:T(4,128)(2,1)S(1)} %get-tuple-element.31), channel_id=1, source_target_pairs={{0,12},{4,8},{8,4},{12,0},{1,13},{5,9},{9,5},{13,1},{2,14},{6,10},... | collective-permute-start | bytes 101384 | tf_op jit(solution)/shard_map/ppermute | solution.py:20
  14.3 7.2 %collective-permute-start.5 = (bf16[4096,512]{1,0:T(8,128)(2,1)S(1)}, bf16[4096,512]{1,0:T(8,128)(2,1)S(1)}, u32[]{:S(2)}, u32[]{:S(2)}) collective-permute-start(bf16[4096,512]{1,0:T(8,128)(2,1)S(1)} %get-tuple-element.43.own_ref), channel_id=1, source_target_pairs={{0,1},{1,0},{2,3},{3,2},{4,5},{5,4},{6,7},{7,6},{8,9},{9,8},{10,11... | collective-permute-start | bytes 12582920 | tf_op jit(solution)/shard_map/ppermute | solution.py:20
  14.4 10.6 %collective-permute-start.9 = (bf16[1024,1024]{1,0:T(8,128)(2,1)S(1)}, bf16[1024,1024]{1,0:T(8,128)(2,1)S(1)}, u32[]{:S(2)}, u32[]{:S(2)}) collective-permute-start(bf16[1024,1024]{1,0:T(8,128)(2,1)S(1)} %get-tuple-element.48.refs_7_), channel_id=1, source_target_pairs={{0,1},{1,0},{2,3},{3,2},{4,5},{5,4},{6,7},{7,6},{8,9},{9,8},{10,11... | collective-permute-start | bytes 6291464 | tf_op jit(solution)/shard_map/ppermute | solution.py:20
  14.9 9.8 %collective-permute-start.7 = (bf16[32,3072]{1,0:T(8,128)(2,1)S(1)}, bf16[32,3072]{1,0:T(8,128)(2,1)S(1)}, u32[]{:S(2)}, u32[]{:S(2)}) collective-permute-start(bf16[32,3072]{1,0:T(8,128)(2,1)S(1)} %get-tuple-element.45.refs_2_), channel_id=1, source_target_pairs={{0,1},{1,0},{2,3},{3,2},{4,5},{5,4},{6,7},{7,6},{8,9},{9,8},{10,11... | collective-permute-start | bytes 589832 | tf_op jit(solution)/shard_map/ppermute | solution.py:20
  15.0 10.0 %collective-permute-start.8 = (bf16[32,3072]{1,0:T(8,128)(2,1)S(1)}, bf16[32,3072]{1,0:T(8,128)(2,1)S(1)}, u32[]{:S(2)}, u32[]{:S(2)}) collective-permute-start(bf16[32,3072]{1,0:T(8,128)(2,1)S(1)} %collective-permute-done.3.refs_4_), channel_id=1, source_target_pairs={{0,1},{1,0},{2,3},{3,2},{4,5},{5,4},{6,7},{7,6},{8,9},{9,8},{10,11... | collective-permute-start | bytes 589832 | tf_op jit(solution)/shard_map/ppermute | solution.py:20
  15.4 5.6 %collective-permute-start.4 = (bf16[16,4224]{1,0:T(8,128)(2,1)S(1)}, bf16[16,4224]{1,0:T(8,128)(2,1)S(1)}, u32[]{:S(2)}, u32[]{:S(2)}) collective-permute-start(bf16[16,4224]{1,0:T(8,128)(2,1)S(1)} %pad_maximum_fusion.near_ref), channel_id=1, source_target_pairs={{0,2},{1,3},{2,0},{3,1},{4,6},{5,7},{6,4},{7,5},{8,10},{9,11},{10,... | collective-permute-start | bytes 405512 | tf_op jit(solution)/shard_map/ppermute | solution.py:20
  23.0 4.0 %collective-permute-start.6 = (bf16[32,512]{1,0:T(8,128)(2,1)S(1)}, bf16[32,512]{1,0:T(8,128)(2,1)S(1)}, u32[]{:S(2)}, u32[]{:S(2)}) collective-permute-start(bf16[32,512]{1,0:T(8,128)(2,1)S(1)} %get-tuple-element.44.refs_0_), channel_id=1, source_target_pairs={{0,2},{1,3},{2,0},{3,1},{4,6},{5,7},{6,4},{7,5},{8,10},{9,11},{10,... | collective-permute-start | bytes 98312 | tf_op jit(solution)/shard_map/ppermute | solution.py:20

commit v3 on v2

--- a/solution.py
+++ b/solution.py
@@ -45,8 +45,11 @@
     return copies
 
 
-def pack_kernel(quads, ids_hbm, req_hbm, x_hbm, first_hbm, second_hbm, *refs):
+def pack_kernel(
+    quads, ids_hbm, req_hbm, x_hbm, first_hbm, second_hbm, gate_hbm, up_hbm, own_ref, *refs
+):
     factor_refs, out_refs, scratches = refs[:quads], refs[quads:-5], refs[-5:]
+    part = gate_hbm.shape[2]
     ids_ref, req_ref, x_ref, scratch, sems = scratches
     half = second_hbm.shape[1] // quads
     pairs = [(ids_hbm, ids_ref), (req_hbm, req_ref), (x_hbm, x_ref)]
@@ -54,6 +57,8 @@
         at = pl.multiple_of((lax.axis_index("quad") ^ q) * half, half)
         pairs.append((second_hbm.at[:, pl.ds(at, half)], factor_ref.at[:, pl.ds(0, half)]))
         pairs.append((first_hbm, factor_ref.at[:, pl.ds(half, first_hbm.shape[1])]))
+    pairs.append((gate_hbm.at[0], own_ref.at[:, pl.ds(0, part)]))
+    pairs.append((up_hbm.at[0], own_ref.at[:, pl.ds(part, part)]))
     copies = copy_all(pairs, sems)
     experts = len(out_refs)
     me = lax.axis_index("expert")
@@ -69,24 +74,16 @@
     scratch[:, :width] = jnp.dot(
         table.astype(jnp.bfloat16), x_ref[...], preferred_element_type=jnp.float32
     )
-    for s, out_ref in enumerate(out_refs):
+    for s, out_ref in enumerate(out_refs[::-1]):
         out_ref[...] = scratch[pl.ds(s * CAP, CAP), :].astype(out_ref.dtype)
     for copy in copies[3:]:
         copy.wait()
 
 
 def stage_kernel(
-    ids_hbm, weight_hbm, gate_hbm, up_hbm, down_hbm, after_ref,
-    table_ref, own_ref, down_ref, ids_ref, weight_ref, sems,
+    ids_hbm, weight_hbm, down_hbm, after_ref, table_ref, down_ref, ids_ref, weight_ref, sems
 ):
-    part = gate_hbm.shape[2]
-    pairs = [
-        (ids_hbm, ids_ref),
-        (weight_hbm, weight_ref),
-        (gate_hbm.at[0], own_ref.at[:, pl.ds(0, part)]),
-        (up_hbm.at[0], own_ref.at[:, pl.ds(part, part)]),
-        (down_hbm.at[0], down_ref),
-    ]
+    pairs = [(ids_hbm, ids_ref), (weight_hbm, weight_ref), (down_hbm.at[0], down_ref)]
     copies = copy_all(pairs, sems)
     copies[0].wait()
     copies[1].wait()
@@ -102,11 +99,13 @@
         copy.wait()
 
 
-def hidden_kernel(near_ref, far_ref, own_ref, peer_ref, hidden_ref, owner_ref):
-    width = near_ref.shape[1] - LANES
+def hidden_kernel(pieces, *refs):
+    slot_refs, (own_ref, peer_ref, hidden_ref, owner_ref) = refs[:pieces], refs[pieces:]
+    width = slot_refs[0].shape[1] - LANES
     part = own_ref.shape[1] // PAIR
-    rows = jnp.concatenate([near_ref[:, :width], far_ref[:, :width]], axis=0)
-    owner_ref[...] = jnp.concatenate([near_ref[:, width:], far_ref[:, width:]], axis=0)
+    slots = jnp.concatenate([ref[...].astype(jnp.float32) for ref in slot_refs], axis=0)
+    rows = slots[:, :width].astype(jnp.bfloat16)
+    owner_ref[...] = slots[:, width:].astype(owner_ref.dtype)
     for b, ref in enumerate((own_ref, peer_ref)):
         both = jnp.dot(rows, ref[...], preferred_element_type=jnp.float32)
         gate, up = both[:, :part], both[:, part:]
@@ -116,8 +115,8 @@
 
 def down_kernel(order, n_req, cols, *refs):
     quads = len(order)
-    hid_refs, factor_refs = refs[:quads], refs[quads : 3 * quads]
-    owner_ref, own_ref, peer_ref, out_ref, whole, scratch = refs[3 * quads :]
+    hid_refs, factor_refs = refs[:quads], refs[quads : quads + PAIR]
+    owner_ref, own_ref, peer_ref, out_ref, whole, scratch = refs[quads + PAIR :]
     me_e, me_q, me_p = (lax.axis_index(a) for a in ("expert", "quad", "pair"))
     me_r = me_q * PAIR + me_p
     total, depth = whole.shape
@@ -131,16 +130,17 @@
             whole[:, pl.ds(at, part)] = hid[:, b * part : (b + 1) * part]
     hidden = whole[...]
     owner = owner_ref[:, :1].astype(jnp.int32)
-    per_dev = factor_refs[0].shape[0]
+    per_dev = factor_refs[0].shape[0] // quads
     rank = per_dev // n_req
-    lane = lax.broadcasted_iota(jnp.int32, (1, per_dev * len(factor_refs)), 1)
+    lane = lax.broadcasted_iota(jnp.int32, (1, per_dev * quads * PAIR), 1)
     first = jnp.concatenate([ref[:, PAIR * cols :] for ref in factor_refs], axis=0)
     low = lax.dot_general(
         hidden, first, (((1,), (1,)), ((), ())), preferred_element_type=jnp.float32
     )
     holder = jnp.zeros_like(lane)
-    for i in range(len(factor_refs)):
-        mine = (me_r ^ i) * n_req + (lane - i * per_dev) // rank
+    for i in range(quads * PAIR):
+        holder_r = me_r ^ (i % quads * PAIR + i // quads)
+        mine = holder_r * n_req + (lane - i * per_dev) // rank
         holder = jnp.where(lane // per_dev == i, mine, holder)
     chosen = jnp.where(holder == owner, low, 0.0).astype(jnp.bfloat16)
     for b, ref in enumerate((own_ref, peer_ref)):
@@ -200,18 +200,19 @@
 
     ids = token_expert_index.T
     weights = choice_weight.T
-    outs = pl.pallas_call(
+    mine, *outs = pl.pallas_call(
         functools.partial(pack_kernel, quads),
-        out_shape=[jax.ShapeDtypeStruct((own, width // quads + depth), bf16)] * quads
+        out_shape=[jax.ShapeDtypeStruct((width, PAIR * part), bf16)]
+        + [jax.ShapeDtypeStruct((own, width // quads + depth), bf16)] * quads
         + [jax.ShapeDtypeStruct((CAP, width + LANES), bf16)] * experts,
-        in_specs=[HBM] * 5,
-        out_specs=[VMEM] * (quads + experts),
+        in_specs=[HBM] * 7,
+        out_specs=[VMEM] * (1 + quads + experts),
         scratch_shapes=[
             pltpu.VMEM(ids.shape, jnp.int32),
             pltpu.VMEM((1, tokens), jnp.int32),
             pltpu.VMEM(token_input.shape, bf16),
             pltpu.VMEM((experts * CAP, width + LANES), f32),
-            dma((3 + 2 * quads,)),
+            dma((5 + 2 * quads,)),
         ],
         compiler_params=PARAMS,
     )(
@@ -221,66 +222,65 @@
             token_input,
             adapter_first_weight.reshape(own, depth),
             adapter_second_weight.reshape(own, width),
+            gate_weight,
+            up_weight,
         )
     )
-    factors, packed = outs[:quads], outs[quads:]
-
-    table, mine, down = pl.pallas_call(
+    theirs = xor_permute(mine, REQUEST, 1)
+    factors, packed = outs[:quads], outs[quads:][::-1]
+
+    blocks = [xor_permute(packed[s], "expert", s) for s in reversed(range(1, experts))]
+    blocks = [packed[0]] + blocks[::-1]
+    table, down = pl.pallas_call(
         stage_kernel,
         out_shape=[
             jax.ShapeDtypeStruct((3 * experts * CAP, tokens), bf16),
-            jax.ShapeDtypeStruct((width, PAIR * part), bf16),
             jax.ShapeDtypeStruct((depth, cols), bf16),
         ],
-        in_specs=[HBM] * 5 + [VMEM],
-        out_specs=[VMEM] * 3,
+        in_specs=[HBM] * 3 + [VMEM],
+        out_specs=[VMEM] * 2,
         scratch_shapes=[
             pltpu.VMEM(ids.shape, jnp.int32),
             pltpu.VMEM(weights.shape, f32),
-            dma((5,)),
-        ],
-        compiler_params=PARAMS,
-    )(*in_hbm(ids, weights, gate_weight, up_weight, down_weight), packed[0])
-
-    blocks = [packed[0]] + [xor_permute(packed[s], "expert", s) for s in range(1, experts)]
+            dma((3,)),
+        ],
+        compiler_params=PARAMS,
+    )(*in_hbm(ids, weights, down_weight), packed[0])
+
     factors = [factors[0]] + [xor_permute(factors[q], REQUEST, q * PAIR) for q in range(1, quads)]
-    mine, home = lax.optimization_barrier((mine, factors[0]))
-    factors[0], peers = home, [xor_permute(home, REQUEST, 1)]
-    blocks, mine, factors[1:] = lax.optimization_barrier((blocks, mine, factors[1:]))
-    theirs = xor_permute(mine, REQUEST, 1)
+    blocks, down, factors[1:] = lax.optimization_barrier((blocks[::-1], down, factors[1:]))
+    blocks = blocks[::-1]
     rows = jnp.concatenate(blocks, axis=0)
-    rows, down, factors[1:] = lax.optimization_barrier((rows, down, factors[1:]))
-    down2 = xor_permute(down, REQUEST, 1)
-    peers += [xor_permute(f, REQUEST, 1) for f in factors[1:]]
-    factors = [v for both in zip(factors, peers) for v in both]
-    order = [0]
-    bit = quads // 2
-    while True:
-        near = rows
+    order, bit, slots = [0], quads // 2, []
+    while bit:
         far = xor_permute(rows, REQUEST, bit * PAIR)
         order = order + [o ^ bit for o in order]
         bit //= 2
-        if not bit:
-            break
-        rows = jnp.concatenate([near, far], axis=0)
+        slots = [rows, far]
+        rows = jnp.concatenate(slots, axis=0) if bit else rows
+
+    factors = jnp.concatenate(factors, axis=0)
+    slots, down, factors = lax.optimization_barrier((slots, down, factors))
+    down2 = xor_permute(down, REQUEST, 1)
+    factors = (factors, xor_permute(factors, REQUEST, 1))
 
     total = experts * CAP * quads
     hidden, owner = pl.pallas_call(
-        hidden_kernel,
+        functools.partial(hidden_kernel, len(slots)),
         out_shape=[
             jax.ShapeDtypeStruct((total, PAIR * part), bf16),
             jax.ShapeDtypeStruct((total, LANES), bf16),
         ],
-        in_specs=[VMEM] * 4,
+        in_specs=[VMEM] * (len(slots) + 2),
         out_specs=[VMEM] * 2,
         compiler_params=PARAMS,
-    )(near, far, mine, theirs)
+    )(*slots, mine, theirs)
 
     shared = [hidden] + [xor_permute(hidden, REQUEST, q * PAIR) for q in range(1, quads)]
     out = pl.pallas_call(
         functools.partial(down_kernel, order, n_req, cols),
         out_shape=jax.ShapeDtypeStruct((experts * quads, CAP, PAIR * cols), bf16),
-        in_specs=[VMEM] * (3 * quads + 3),
+        in_specs=[VMEM] * (quads + PAIR + 3),
         out_specs=VMEM,
         scratch_shapes=[
             pltpu.VMEM((total, depth), bf16),

time: 39.1 us -> 38.3 us (0.980)
  waiting for transfers between devices: 11.4 us -> 10.2 us
  blocking collectives: 9.74 us -> 10.4 us
  starting transfers between devices: 9.61 us -> 9.18 us
    pallas_call x1, Pallas kernels: 2.93 us -> 1.65 us  [body(): pl.pallas_call(stage_kernel, out_shape=[jax.ShapeDtypeStruct((3 * experts...]
    pallas_call x1, Pallas kernels: 1.35 us -> 2.62 us  [body(): pl.pallas_call(functools.partial(pack_kernel, quads), out_shape=[jax.Shap...]
    ppermute x10 -> x9, waiting for transfers between devices: 11.4 us -> 10.2 us  [xor_permute(): lax.ppermute(value, axis, [(i, i ^ offset) for i in range(lax.axis_size(a...]
    all_to_all x1, blocking collectives: 9.74 us -> 10.4 us  [body(): back = lax.all_to_all(out, ('expert', 'quad'), 0, 0, tiled=True)]
    ppermute x10 -> x9, starting transfers between devices: 9.61 us -> 9.18 us  [xor_permute(): lax.ppermute(value, axis, [(i, i ^ offset) for i in range(lax.axis_size(a...]
  transfers between devices with their start and end apart: 10 -> 9, of which waited for: 6 -> 4; matrix products, arithmetic and copies ran while one was open for 0% -> 0% of each run, Pallas kernels for 12% -> 8%
where the time goes in v3:
time: 38.3 us; the launch traced here: 38 us
  blocking collectives  10.4 us (27%)
  waiting for transfers between devices  10.2 us (27%)
  starting transfers between devices  9.18 us (24%)
  Pallas kernels  8.01 us (21%)
    all_to_all x1, blocking collectives, body(): back = lax.all_to_all(out, ('expert', 'quad'), 0, 0, tiled=True)  10.4 us
    ppermute x9, waiting for transfers between devices, xor_permute(): lax.ppermute(value, axis, [(i, i ^ offset) for i in range(lax.axis_size(a...  10.2 us
    ppermute x9, starting transfers between devices, xor_permute(): lax.ppermute(value, axis, [(i, i ^ offset) for i in range(lax.axis_size(a...  9.18 us
    pallas_call x1, Pallas kernels, body(): pl.pallas_call(functools.partial(pack_kernel, quads), out_shape=[jax.Shap...  2.62 us
    pallas_call x1, Pallas kernels, body(): pl.pallas_call(stage_kernel, out_shape=[jax.ShapeDtypeStruct((3 * experts...  1.65 us
    pallas_call x1, Pallas kernels, body(): pl.pallas_call(functools.partial(hidden_kernel, len(slots)), out_shape=[j...  1.55 us
    pallas_call x1, Pallas kernels, body(): pl.pallas_call(functools.partial(down_kernel, order, n_req, cols), out_sh...  1.14 us
    pallas_call x1, Pallas kernels, body(): pl.pallas_call(combine_kernel, out_shape=jax.ShapeDtypeStruct((tokens, wi...  1.05 us
  transfers between devices with their start and end apart: 9, of which 4 were waited for; matrix products, arithmetic and copies ran while one was open for 0% of the time, Pallas kernels for 8%

profile of v3, /device:TPU:0, one launch (start us, length us, event | category | flops | bytes accessed | tf_op | source)
XLA Modules:
  0.0 38.0 jit_solution(6725711596094007943)
XLA Ops:
  0.0 2.6 %shard_map.91 = (bf16[4096,512]{1,0:T(8,128)(2,1)S(1)}, bf16[32,3072]{1,0:T(8,128)(2,1)S(1)}, bf16[32,3072]{1,0:T(8,128)(2,1)S(1)}, bf16[4,4224]{1,0:T(4,128)(2,...) custom-call(s32[8,64]{1,0:T(8,128)} %bitcast.7, s32[1,64]{1,0:T(1,128)} %bitcast.10, ...), custom_call_target="tpu_custom_call" | custom-call | tf_op jit(solution)/shard_map/pallas_call | solution.py:203
  2.6 0.5 %collective-permute-start.5 = (bf16[4096,512]{1,0:T(8,128)(2,1)S(1)}, bf16[4096,512]{1,0:T(8,128)(2,1)S(1)}, u32[]{:S(2)}, u32[]{:S(2)}) collective-permute-start(bf16[4096,512]{1,0:T(8,128)(2,1)S(1)} %get-tuple-element.42.refs_2_), channel_id=1, source_target_pairs={{0,1},{1,0},{2,3},{3,2},{4,5},{5,4},{6,7},{7,6},{8,9},{9,8},{10,11... | collective-permute-start | bytes 12582920 | tf_op jit(solution)/shard_map/ppermute | solution.py:20
  3.1 2.6 %collective-permute-start.3 = (bf16[32,3072]{1,0:T(8,128)(2,1)S(1)}, bf16[32,3072]{1,0:T(8,128)(2,1)S(1)}, u32[]{:S(2)}, u32[]{:S(2)}) collective-permute-start(bf16[32,3072]{1,0:T(8,128)(2,1)S(1)} %get-tuple-element.32), channel_id=1, source_target_pairs={{0,2},{1,3},{2,0},{3,1},{4,6},{5,7},{6,4},{7,5},{8,10},{9,11},{10,... | collective-permute-start | bytes 589832 | tf_op jit(solution)/shard_map/ppermute | solution.py:20
  5.7 3.6 %collective-permute-start = (bf16[4,4224]{1,0:T(4,128)(2,1)S(1)}, bf16[4,4224]{1,0:T(4,128)(2,1)S(1)}, u32[]{:S(2)}, u32[]{:S(2)}) collective-permute-start(bf16[4,4224]{1,0:T(4,128)(2,1)S(1)} %get-tuple-element.28), channel_id=1, source_target_pairs={{0,12},{4,8},{8,4},{12,0},{1,13},{5,9},{9,5},{13,1},{2,14},{6,10},... | collective-permute-start | bytes 101384 | tf_op jit(solution)/shard_map/ppermute | solution.py:20
  9.3 0.0 collective-permute-start.1
  9.3 0.8 %collective-permute-start.2 = (bf16[4,4224]{1,0:T(4,128)(2,1)S(1)}, bf16[4,4224]{1,0:T(4,128)(2,1)S(1)}, u32[]{:S(2)}, u32[]{:S(2)}) collective-permute-start(bf16[4,4224]{1,0:T(4,128)(2,1)S(1)} %get-tuple-element.30), channel_id=1, source_target_pairs={{0,4},{4,0},{8,12},{12,8},{1,5},{5,1},{9,13},{13,9},{2,6},{6,2},{1... | collective-permute-start | bytes 101384 | tf_op jit(solution)/shard_map/ppermute | solution.py:20
  10.1 1.6 %shard_map.92 = (bf16[48,64]{1,0:T(8,128)(2,1)S(1)}, bf16[1024,1024]{1,0:T(8,128)(2,1)S(1)}) custom-call(s32[8,64]{1,0:T(8,128)} %bitcast.8, f32[8,64]{1,0:T(8,128)} %bitcast.9, bf16[1,1024,1024]{2,1,0:T(8,128)(2,1)} %down_hbm.1, bf16[4,4224]{1,0:T(4,128)(2,1)S(1)} %get-tuple-element.33.after_ref), custom_call_target="tpu_custom_call" | custom-call | tf_op jit(solution)/shard_map/pallas_call | solution.py:234
  11.8 0.0 collective-permute-done
  11.8 2.4 %collective-permute-done.1 = bf16[4,4224]{1,0:T(4,128)(2,1)S(1)} collective-permute-done((bf16[4,4224]{1,0:T(4,128)(2,1)S(1)}, bf16[4,4224]{1,0:T(4,128)(2,1)S(1)}, u32[]{:S(2)}, u32[]{:S(2)}) %collective-permute-start.1) | collective-permute-done | bytes 33824 | tf_op jit(solution)/shard_map/ppermute | solution.py:20
  14.1 0.0 collective-permute-done.2
  14.1 0.0 collective-permute-done.3
  14.1 0.1 pad_maximum_fusion.1.refs_0_
  14.2 0.6 %collective-permute-start.4 = (bf16[16,4224]{1,0:T(8,128)(2,1)S(1)}, bf16[16,4224]{1,0:T(8,128)(2,1)S(1)}, u32[]{:S(2)}, u32[]{:S(2)}) collective-permute-start(bf16[16,4224]{1,0:T(8,128)(2,1)S(1)} %pad_maximum_fusion.1.refs_0_), channel_id=1, source_target_pairs={{0,2},{1,3},{2,0},{3,1},{4,6},{5,7},{6,4},{7,5},{8,10},{9,11},{10,... | collective-permute-start | bytes 405512 | tf_op jit(solution)/shard_map/ppermute | solution.py:20
  14.9 4.4 %collective-permute-done.4.refs_1_ = bf16[16,4224]{1,0:T(8,128)(2,1)S(1)} collective-permute-done((bf16[16,4224]{1,0:T(8,128)(2,1)S(1)}, bf16[16,4224]{1,0:T(8,128)(2,1)S(1)}, u32[]{:S(2)}, u32[]{:S(2)}) %collective-permute-start.4) | collective-permute-done | bytes 135200 | tf_op jit(solution)/shard_map/ppermute | solution.py:20
  19.3 0.0 collective-permute-start.8
  19.3 0.5 %collective-permute-start.7 = (bf16[64,3072]{1,0:T(8,128)(2,1)S(1)}, bf16[64,3072]{1,0:T(8,128)(2,1)S(1)}, u32[]{:S(2)}, u32[]{:S(2)}) collective-permute-start(bf16[64,3072]{1,0:T(8,128)(2,1)S(1)} %pad_maximum_fusion.refs_2_), channel_id=1, source_target_pairs={{0,1},{1,0},{2,3},{3,2},{4,5},{5,4},{6,7},{7,6},{8,9},{9,8},{10,11... | collective-permute-start | bytes 1179656 | tf_op jit(solution)/shard_map/ppermute | solution.py:20
  19.8 0.0 collective-permute-done.5.refs_3_
  19.8 1.6 %shard_map.93 = (bf16[32,512]{1,0:T(8,128)(2,1)S(1)}, bf16[32,128]{1,0:T(8,128)(2,1)S(1)}) custom-call(bf16[16,4224]{1,0:T(8,128)(2,1)S(1)} %pad_maximum_fusion.1.refs_0_, bf16[16,4224]{1,0:T(8,128)(2,1)S(1)} %collective-permute-done.4.refs_1_, bf16[4096,512]{1,0:T(8,128)(2,1)S(1)} %get-tuple-element.42.refs_2_, ...), custom_call_target="tpu_custom_call" | custom-call | tf_op jit(solution)/shard_map/pallas_call | solution.py:268
  21.4 0.6 %collective-permute-start.6 = (bf16[32,512]{1,0:T(8,128)(2,1)S(1)}, bf16[32,512]{1,0:T(8,128)(2,1)S(1)}, u32[]{:S(2)}, u32[]{:S(2)}) collective-permute-start(bf16[32,512]{1,0:T(8,128)(2,1)S(1)} %get-tuple-element.43.refs_0_), channel_id=1, source_target_pairs={{0,2},{1,3},{2,0},{3,1},{4,6},{5,7},{6,4},{7,5},{8,10},{9,11},{10,... | collective-permute-start | bytes 98312 | tf_op jit(solution)/shard_map/ppermute | solution.py:20
  22.0 2.0 %collective-permute-done.7.refs_3_ = bf16[64,3072]{1,0:T(8,128)(2,1)S(1)} collective-permute-done((bf16[64,3072]{1,0:T(8,128)(2,1)S(1)}, bf16[64,3072]{1,0:T(8,128)(2,1)S(1)}, u32[]{:S(2)}, u32[]{:S(2)}) %collective-permute-start.7) | collective-permute-done | bytes 393248 | tf_op jit(solution)/shard_map/ppermute | solution.py:20
  24.0 0.0 collective-permute-done.8.refs_6_
  24.0 1.3 %collective-permute-done.6.refs_1_ = bf16[32,512]{1,0:T(8,128)(2,1)S(1)} collective-permute-done((bf16[32,512]{1,0:T(8,128)(2,1)S(1)}, bf16[32,512]{1,0:T(8,128)(2,1)S(1)}, u32[]{:S(2)}, u32[]{:S(2)}) %collective-permute-start.6) | collective-permute-done | bytes 32800 | tf_op jit(solution)/shard_map/ppermute | solution.py:20
  25.4 1.1 %shard_map.94 = bf16[8,4,2048]{2,1,0:T(4,128)(2,1)S(1)} custom-call(bf16[32,512]{1,0:T(8,128)(2,1)S(1)} %get-tuple-element.43.refs_0_, bf16[32,512]{1,0:T(8,128)(2,1)S(1)} %collective-permute-done.6.refs_1_, bf16[64,3072]{1,0:T(8,128)(2,1)S(1)} %pad_maximum_fusion.refs_2_, bf16[64,3072]{1,0:T(8,128)(2,1)S(1)} %collective-permute-done.7.refs_3_, ...), custom_call_target="tpu_custom_call" | custom-call | tf_op jit(solution)/shard_map/pallas_call | solution.py:280
  26.5 10.4 %all_to_all.5.back_ref = bf16[8,4,2048]{2,1,0:T(4,128)(2,1)S(1)} all-to-all(bf16[8,4,2048]{2,1,0:T(4,128)(2,1)S(1)} %shard_map.94), channel_id=1, replica_groups=mesh['groups'=2,'expert'=4,'quad'=2,'pair'=2] {'expert','quad'}, dimensions={0} | all-to-all | bytes 262144 | tf_op jit(solution)/shard_map/all_to_all | solution.py:292
  37.0 1.1 %shard_map.95 = bf16[64,4096]{1,0:T(8,128)(2,1)} custom-call(bf16[48,64]{1,0:T(8,128)(2,1)S(1)} %get-tuple-element.27.table_ref, bf16[8,4,2048]{2,1,0:T(4,128)(2,1)S(1)} %all_to_all.5.back_ref), custom_call_target="tpu_custom_call" | custom-call | tf_op jit(solution)/shard_map/pallas_call | solution.py:293
  (1 shorter events, 0.0 us)
Async XLA Ops:
  2.6 17.2 %collective-permute-start.5 = (bf16[4096,512]{1,0:T(8,128)(2,1)S(1)}, bf16[4096,512]{1,0:T(8,128)(2,1)S(1)}, u32[]{:S(2)}, u32[]{:S(2)}) collective-permute-start(bf16[4096,512]{1,0:T(8,128)(2,1)S(1)} %get-tuple-element.42.refs_2_), channel_id=1, source_target_pairs={{0,1},{1,0},{2,3},{3,2},{4,5},{5,4},{6,7},{7,6},{8,9},{9,8},{10,11... | collective-permute-start | bytes 12582920 | tf_op jit(solution)/shard_map/ppermute | solution.py:20
  3.1 11.0 %collective-permute-start.3 = (bf16[32,3072]{1,0:T(8,128)(2,1)S(1)}, bf16[32,3072]{1,0:T(8,128)(2,1)S(1)}, u32[]{:S(2)}, u32[]{:S(2)}) collective-permute-start(bf16[32,3072]{1,0:T(8,128)(2,1)S(1)} %get-tuple-element.32), channel_id=1, source_target_pairs={{0,2},{1,3},{2,0},{3,1},{4,6},{5,7},{6,4},{7,5},{8,10},{9,11},{10,... | collective-permute-start | bytes 589832 | tf_op jit(solution)/shard_map/ppermute | solution.py:20
  5.7 6.0 %collective-permute-start = (bf16[4,4224]{1,0:T(4,128)(2,1)S(1)}, bf16[4,4224]{1,0:T(4,128)(2,1)S(1)}, u32[]{:S(2)}, u32[]{:S(2)}) collective-permute-start(bf16[4,4224]{1,0:T(4,128)(2,1)S(1)} %get-tuple-element.28), channel_id=1, source_target_pairs={{0,12},{4,8},{8,4},{12,0},{1,13},{5,9},{9,5},{13,1},{2,14},{6,10},... | collective-permute-start | bytes 101384 | tf_op jit(solution)/shard_map/ppermute | solution.py:20
  9.3 4.8 %collective-permute-start.1 = (bf16[4,4224]{1,0:T(4,128)(2,1)S(1)}, bf16[4,4224]{1,0:T(4,128)(2,1)S(1)}, u32[]{:S(2)}, u32[]{:S(2)}) collective-permute-start(bf16[4,4224]{1,0:T(4,128)(2,1)S(1)} %get-tuple-element.29), channel_id=1, source_target_pairs={{0,8},{4,12},{8,0},{12,4},{1,9},{5,13},{9,1},{13,5},{2,10},{6,14},... | collective-permute-start | bytes 101384 | tf_op jit(solution)/shard_map/ppermute | solution.py:20
  9.3 4.8 %collective-permute-start.2 = (bf16[4,4224]{1,0:T(4,128)(2,1)S(1)}, bf16[4,4224]{1,0:T(4,128)(2,1)S(1)}, u32[]{:S(2)}, u32[]{:S(2)}) collective-permute-start(bf16[4,4224]{1,0:T(4,128)(2,1)S(1)} %get-tuple-element.30), channel_id=1, source_target_pairs={{0,4},{4,0},{8,12},{12,8},{1,5},{5,1},{9,13},{13,9},{2,6},{6,2},{1... | collective-permute-start | bytes 101384 | tf_op jit(solution)/shard_map/ppermute | solution.py:20
  14.2 5.1 %collective-permute-start.4 = (bf16[16,4224]{1,0:T(8,128)(2,1)S(1)}, bf16[16,4224]{1,0:T(8,128)(2,1)S(1)}, u32[]{:S(2)}, u32[]{:S(2)}) collective-permute-start(bf16[16,4224]{1,0:T(8,128)(2,1)S(1)} %pad_maximum_fusion.1.refs_0_), channel_id=1, source_target_pairs={{0,2},{1,3},{2,0},{3,1},{4,6},{5,7},{6,4},{7,5},{8,10},{9,11},{10,... | collective-permute-start | bytes 405512 | tf_op jit(solution)/shard_map/ppermute | solution.py:20
  19.3 4.7 %collective-permute-start.8 = (bf16[1024,1024]{1,0:T(8,128)(2,1)S(1)}, bf16[1024,1024]{1,0:T(8,128)(2,1)S(1)}, u32[]{:S(2)}, u32[]{:S(2)}) collective-permute-start(bf16[1024,1024]{1,0:T(8,128)(2,1)S(1)} %get-tuple-element.46.refs_5_), channel_id=1, source_target_pairs={{0,1},{1,0},{2,3},{3,2},{4,5},{5,4},{6,7},{7,6},{8,9},{9,8},{10,11... | collective-permute-start | bytes 6291464 | tf_op jit(solution)/shard_map/ppermute | solution.py:20
  19.3 4.7 %collective-permute-start.7 = (bf16[64,3072]{1,0:T(8,128)(2,1)S(1)}, bf16[64,3072]{1,0:T(8,128)(2,1)S(1)}, u32[]{:S(2)}, u32[]{:S(2)}) collective-permute-start(bf16[64,3072]{1,0:T(8,128)(2,1)S(1)} %pad_maximum_fusion.refs_2_), channel_id=1, source_target_pairs={{0,1},{1,0},{2,3},{3,2},{4,5},{5,4},{6,7},{7,6},{8,9},{9,8},{10,11... | collective-permute-start | bytes 1179656 | tf_op jit(solution)/shard_map/ppermute | solution.py:20
  21.4 4.0 %collective-permute-start.6 = (bf16[32,512]{1,0:T(8,128)(2,1)S(1)}, bf16[32,512]{1,0:T(8,128)(2,1)S(1)}, u32[]{:S(2)}, u32[]{:S(2)}) collective-permute-start(bf16[32,512]{1,0:T(8,128)(2,1)S(1)} %get-tuple-element.43.refs_0_), channel_id=1, source_target_pairs={{0,2},{1,3},{2,0},{3,1},{4,6},{5,7},{6,4},{7,5},{8,10},{9,11},{10,... | collective-permute-start | bytes 98312 | tf_op jit(solution)/shard_map/ppermute | solution.py:20

commit v4 on v3

--- a/solution.py
+++ b/solution.py
@@ -46,10 +46,9 @@
 
 
 def pack_kernel(
-    quads, ids_hbm, req_hbm, x_hbm, first_hbm, second_hbm, gate_hbm, up_hbm, own_ref, *refs
+    quads, ids_hbm, req_hbm, x_hbm, first_hbm, second_hbm, *refs
 ):
     factor_refs, out_refs, scratches = refs[:quads], refs[quads:-5], refs[-5:]
-    part = gate_hbm.shape[2]
     ids_ref, req_ref, x_ref, scratch, sems = scratches
     half = second_hbm.shape[1] // quads
     pairs = [(ids_hbm, ids_ref), (req_hbm, req_ref), (x_hbm, x_ref)]
@@ -57,8 +56,6 @@
         at = pl.multiple_of((lax.axis_index("quad") ^ q) * half, half)
         pairs.append((second_hbm.at[:, pl.ds(at, half)], factor_ref.at[:, pl.ds(0, half)]))
         pairs.append((first_hbm, factor_ref.at[:, pl.ds(half, first_hbm.shape[1])]))
-    pairs.append((gate_hbm.at[0], own_ref.at[:, pl.ds(0, part)]))
-    pairs.append((up_hbm.at[0], own_ref.at[:, pl.ds(part, part)]))
     copies = copy_all(pairs, sems)
     experts = len(out_refs)
     me = lax.axis_index("expert")
@@ -81,9 +78,9 @@
 
 
 def stage_kernel(
-    ids_hbm, weight_hbm, down_hbm, after_ref, table_ref, down_ref, ids_ref, weight_ref, sems
+    ids_hbm, weight_hbm, up_hbm, after_ref, table_ref, up_ref, ids_ref, weight_ref, sems
 ):
-    pairs = [(ids_hbm, ids_ref), (weight_hbm, weight_ref), (down_hbm.at[0], down_ref)]
+    pairs = [(ids_hbm, ids_ref), (weight_hbm, weight_ref), (up_hbm, up_ref)]
     copies = copy_all(pairs, sems)
     copies[0].wait()
     copies[1].wait()
@@ -100,15 +97,15 @@
 
 
 def hidden_kernel(pieces, *refs):
-    slot_refs, (own_ref, peer_ref, hidden_ref, owner_ref) = refs[:pieces], refs[pieces:]
-    width = slot_refs[0].shape[1] - LANES
-    part = own_ref.shape[1] // PAIR
+    slot_refs, refs = refs[:pieces], refs[pieces:]
+    gate_ref, up_ref, gate2_ref, up2_ref, hidden_ref, owner_ref = refs
+    width, part = gate_ref.shape[1:]
     slots = jnp.concatenate([ref[...].astype(jnp.float32) for ref in slot_refs], axis=0)
     rows = slots[:, :width].astype(jnp.bfloat16)
     owner_ref[...] = slots[:, width:].astype(owner_ref.dtype)
-    for b, ref in enumerate((own_ref, peer_ref)):
-        both = jnp.dot(rows, ref[...], preferred_element_type=jnp.float32)
-        gate, up = both[:, :part], both[:, part:]
+    for b, (g_ref, u_ref) in enumerate(((gate_ref, up_ref), (gate2_ref, up2_ref))):
+        gate = jnp.dot(rows, g_ref[0], preferred_element_type=jnp.float32)
+        up = jnp.dot(rows, u_ref[0], preferred_element_type=jnp.float32)
         hidden = gate / (1.0 + jnp.exp(-gate)) * up
         hidden_ref[:, b * part : (b + 1) * part] = hidden.astype(hidden_ref.dtype)
 
@@ -200,19 +197,18 @@
 
     ids = token_expert_index.T
     weights = choice_weight.T
-    mine, *outs = pl.pallas_call(
+    outs = pl.pallas_call(
         functools.partial(pack_kernel, quads),
-        out_shape=[jax.ShapeDtypeStruct((width, PAIR * part), bf16)]
-        + [jax.ShapeDtypeStruct((own, width // quads + depth), bf16)] * quads
+        out_shape=[jax.ShapeDtypeStruct((own, width // quads + depth), bf16)] * quads
         + [jax.ShapeDtypeStruct((CAP, width + LANES), bf16)] * experts,
-        in_specs=[HBM] * 7,
-        out_specs=[VMEM] * (1 + quads + experts),
+        in_specs=[HBM] * 5,
+        out_specs=[VMEM] * (quads + experts),
         scratch_shapes=[
             pltpu.VMEM(ids.shape, jnp.int32),
             pltpu.VMEM((1, tokens), jnp.int32),
             pltpu.VMEM(token_input.shape, bf16),
             pltpu.VMEM((experts * CAP, width + LANES), f32),
-            dma((5 + 2 * quads,)),
+            dma((3 + 2 * quads,)),
         ],
         compiler_params=PARAMS,
     )(
@@ -222,20 +218,18 @@
             token_input,
             adapter_first_weight.reshape(own, depth),
             adapter_second_weight.reshape(own, width),
-            gate_weight,
-            up_weight,
         )
     )
-    theirs = xor_permute(mine, REQUEST, 1)
+    gate2 = xor_permute(gate_weight, REQUEST, 1)
     factors, packed = outs[:quads], outs[quads:][::-1]
 
     blocks = [xor_permute(packed[s], "expert", s) for s in reversed(range(1, experts))]
     blocks = [packed[0]] + blocks[::-1]
-    table, down = pl.pallas_call(
+    table, up = pl.pallas_call(
         stage_kernel,
         out_shape=[
             jax.ShapeDtypeStruct((3 * experts * CAP, tokens), bf16),
-            jax.ShapeDtypeStruct((depth, cols), bf16),
+            jax.ShapeDtypeStruct(up_weight.shape, bf16),
         ],
         in_specs=[HBM] * 3 + [VMEM],
         out_specs=[VMEM] * 2,
@@ -245,12 +239,14 @@
             dma((3,)),
         ],
         compiler_params=PARAMS,
-    )(*in_hbm(ids, weights, down_weight), packed[0])
+    )(*in_hbm(ids, weights, up_weight), packed[0])
 
     factors = [factors[0]] + [xor_permute(factors[q], REQUEST, q * PAIR) for q in range(1, quads)]
-    blocks, down, factors[1:] = lax.optimization_barrier((blocks[::-1], down, factors[1:]))
+    blocks, up, factors[1:] = lax.optimization_barrier((blocks[::-1], up, factors[1:]))
     blocks = blocks[::-1]
     rows = jnp.concatenate(blocks, axis=0)
+    rows, up_source = lax.optimization_barrier((rows, up))
+    up2 = xor_permute(up_source, REQUEST, 1)
     order, bit, slots = [0], quads // 2, []
     while bit:
         far = xor_permute(rows, REQUEST, bit * PAIR)
@@ -260,6 +256,7 @@
         rows = jnp.concatenate(slots, axis=0) if bit else rows
 
     factors = jnp.concatenate(factors, axis=0)
+    down = down_weight[0]
     slots, down, factors = lax.optimization_barrier((slots, down, factors))
     down2 = xor_permute(down, REQUEST, 1)
     factors = (factors, xor_permute(factors, REQUEST, 1))
@@ -271,10 +268,10 @@
             jax.ShapeDtypeStruct((total, PAIR * part), bf16),
             jax.ShapeDtypeStruct((total, LANES), bf16),
         ],
-        in_specs=[VMEM] * (len(slots) + 2),
+        in_specs=[VMEM] * (len(slots) + 4),
         out_specs=[VMEM] * 2,
         compiler_params=PARAMS,
-    )(*slots, mine, theirs)
+    )(*slots, gate_weight, up, gate2, up2)
 
     shared = [hidden] + [xor_permute(hidden, REQUEST, q * PAIR) for q in range(1, quads)]
     out = pl.pallas_call(

time: 38.3 us -> 37.3 us (0.974)
  Pallas kernels: 8.01 us -> 6.92 us
    pallas_call x1, Pallas kernels: 2.62 us -> 1.5 us  [body(): pl.pallas_call(functools.partial(pack_kernel, quads), out_shape=[jax.Shap...]
    ppermute x9 -> x10, waiting for transfers between devices: 10.2 us -> 10.1 us  [xor_permute(): lax.ppermute(value, axis, [(i, i ^ offset) for i in range(lax.axis_size(a...]
    ppermute x9 -> x10, starting transfers between devices: 9.18 us -> 9.22 us  [xor_permute(): lax.ppermute(value, axis, [(i, i ^ offset) for i in range(lax.axis_size(a...]
  transfers between devices with their start and end apart: 9 -> 10, of which waited for: 4 -> 4; matrix products, arithmetic and copies ran while one was open for 0% -> 0% of each run, Pallas kernels for 8% -> 9%
where the time goes in v4:
time: 37.3 us; the launch traced here: 37.1 us
  blocking collectives  10.7 us (29%)
  waiting for transfers between devices  10.1 us (27%)
  starting transfers between devices  9.22 us (25%)
  Pallas kernels  6.92 us (19%)
    all_to_all x1, blocking collectives, body(): back = lax.all_to_all(out, ('expert', 'quad'), 0, 0, tiled=True)  10.7 us
    ppermute x10, waiting for transfers between devices, xor_permute(): lax.ppermute(value, axis, [(i, i ^ offset) for i in range(lax.axis_size(a...  10.1 us
    ppermute x10, starting transfers between devices, xor_permute(): lax.ppermute(value, axis, [(i, i ^ offset) for i in range(lax.axis_size(a...  9.22 us
    pallas_call x1, Pallas kernels, body(): pl.pallas_call(stage_kernel, out_shape=[jax.ShapeDtypeStruct((3 * experts...  1.65 us
    pallas_call x1, Pallas kernels, body(): pl.pallas_call(functools.partial(hidden_kernel, len(slots)), out_shape=[j...  1.56 us
    pallas_call x1, Pallas kernels, body(): pl.pallas_call(functools.partial(pack_kernel, quads), out_shape=[jax.Shap...  1.5 us
    pallas_call x1, Pallas kernels, body(): pl.pallas_call(functools.partial(down_kernel, order, n_req, cols), out_sh...  1.14 us
    pallas_call x1, Pallas kernels, body(): pl.pallas_call(combine_kernel, out_shape=jax.ShapeDtypeStruct((tokens, wi...  1.06 us
  transfers between devices with their start and end apart: 10, of which 4 were waited for; matrix products, arithmetic and copies ran while one was open for 0% of the time, Pallas kernels for 9%

profile of v4, /device:TPU:0, one launch (start us, length us, event | category | flops | bytes accessed | tf_op | source)
XLA Modules:
  0.0 37.1 jit_solution(11603846015964123882)
XLA Ops:
  0.0 0.0 copy-start
  0.0 1.5 %shard_map.91 = (bf16[32,3072]{1,0:T(8,128)(2,1)S(1)}, bf16[32,3072]{1,0:T(8,128)(2,1)S(1)}, bf16[4,4224]{1,0:T(4,128)(2,1)S(1)}, bf16[4,4224]{1,0:T(4,128)(2,1)...) custom-call(s32[8,64]{1,0:T(8,128)} %bitcast.10, s32[1,64]{1,0:T(1,128)} %bitcast.13, ...), custom_call_target="tpu_custom_call" | custom-call | tf_op jit(solution)/shard_map/pallas_call | solution.py:200
  1.5 3.0 %collective-permute-start.3 = (bf16[32,3072]{1,0:T(8,128)(2,1)S(1)}, bf16[32,3072]{1,0:T(8,128)(2,1)S(1)}, u32[]{:S(2)}, u32[]{:S(2)}) collective-permute-start(bf16[32,3072]{1,0:T(8,128)(2,1)S(1)} %get-tuple-element.33), channel_id=1, source_target_pairs={{0,2},{1,3},{2,0},{3,1},{4,6},{5,7},{6,4},{7,5},{8,10},{9,11},{10,... | collective-permute-start | bytes 589832 | tf_op jit(solution)/shard_map/ppermute | solution.py:20
  4.5 3.6 %collective-permute-start = (bf16[4,4224]{1,0:T(4,128)(2,1)S(1)}, bf16[4,4224]{1,0:T(4,128)(2,1)S(1)}, u32[]{:S(2)}, u32[]{:S(2)}) collective-permute-start(bf16[4,4224]{1,0:T(4,128)(2,1)S(1)} %get-tuple-element.29), channel_id=1, source_target_pairs={{0,12},{4,8},{8,4},{12,0},{1,13},{5,9},{9,5},{13,1},{2,14},{6,10},... | collective-permute-start | bytes 101384 | tf_op jit(solution)/shard_map/ppermute | solution.py:20
  8.1 0.0 collective-permute-start.1
  8.1 0.8 %collective-permute-start.2 = (bf16[4,4224]{1,0:T(4,128)(2,1)S(1)}, bf16[4,4224]{1,0:T(4,128)(2,1)S(1)}, u32[]{:S(2)}, u32[]{:S(2)}) collective-permute-start(bf16[4,4224]{1,0:T(4,128)(2,1)S(1)} %get-tuple-element.31), channel_id=1, source_target_pairs={{0,4},{4,0},{8,12},{12,8},{1,5},{5,1},{9,13},{13,9},{2,6},{6,2},{1... | collective-permute-start | bytes 101384 | tf_op jit(solution)/shard_map/ppermute | solution.py:20
  8.9 0.0 collective-permute-start.5
  8.9 1.6 %shard_map.92 = (bf16[48,64]{1,0:T(8,128)(2,1)S(1)}, bf16[1,4096,256]{2,1,0:T(8,128)(2,1)S(1)}) custom-call(s32[8,64]{1,0:T(8,128)} %bitcast.11, f32[8,64]{1,0:T(8,128)} %bitcast.12, bf16[1,4096,256]{2,1,0:T(8,128)(2,1)} %up_hbm.1, bf16[4,4224]{1,0:T(4,128)(2,1)S(1)} %get-tuple-element.34.after_ref), custom_call_target="tpu_custom_call" | custom-call | tf_op jit(solution)/shard_map/pallas_call | solution.py:228
  10.6 0.0 collective-permute-done
  10.6 2.3 %collective-permute-done.1 = bf16[4,4224]{1,0:T(4,128)(2,1)S(1)} collective-permute-done((bf16[4,4224]{1,0:T(4,128)(2,1)S(1)}, bf16[4,4224]{1,0:T(4,128)(2,1)S(1)}, u32[]{:S(2)}, u32[]{:S(2)}) %collective-permute-start.1) | collective-permute-done | bytes 33824 | tf_op jit(solution)/shard_map/ppermute | solution.py:20
  12.9 0.0 collective-permute-done.2
  12.9 0.0 collective-permute-done.3
  13.0 0.1 pad_maximum_fusion.1.refs_0_
  13.0 0.6 %collective-permute-start.4 = (bf16[16,4224]{1,0:T(8,128)(2,1)S(1)}, bf16[16,4224]{1,0:T(8,128)(2,1)S(1)}, u32[]{:S(2)}, u32[]{:S(2)}) collective-permute-start(bf16[16,4224]{1,0:T(8,128)(2,1)S(1)} %pad_maximum_fusion.1.refs_0_), channel_id=1, source_target_pairs={{0,2},{1,3},{2,0},{3,1},{4,6},{5,7},{6,4},{7,5},{8,10},{9,11},{10,... | collective-permute-start | bytes 405512 | tf_op jit(solution)/shard_map/ppermute | solution.py:20
  13.6 0.0 collective-permute-start.6
  13.7 4.4 %collective-permute-done.4.refs_1_ = bf16[16,4224]{1,0:T(8,128)(2,1)S(1)} collective-permute-done((bf16[16,4224]{1,0:T(8,128)(2,1)S(1)}, bf16[16,4224]{1,0:T(8,128)(2,1)S(1)}, u32[]{:S(2)}, u32[]{:S(2)}) %collective-permute-start.4) | collective-permute-done | bytes 135200 | tf_op jit(solution)/shard_map/ppermute | solution.py:20
  18.1 0.0 copy-start.1
  18.1 0.0 collective-permute-start.9
  18.1 0.5 %collective-permute-start.8 = (bf16[64,3072]{1,0:T(8,128)(2,1)S(1)}, bf16[64,3072]{1,0:T(8,128)(2,1)S(1)}, u32[]{:S(2)}, u32[]{:S(2)}) collective-permute-start(bf16[64,3072]{1,0:T(8,128)(2,1)S(1)} %pad_maximum_fusion.refs_2_), channel_id=1, source_target_pairs={{0,1},{1,0},{2,3},{3,2},{4,5},{5,4},{6,7},{7,6},{8,9},{9,8},{10,11... | collective-permute-start | bytes 1179656 | tf_op jit(solution)/shard_map/ppermute | solution.py:20
  18.6 0.0 collective-permute-done.5.refs_4_
  18.6 0.0 collective-permute-done.6.refs_5_
  18.6 0.0 copy-done
  18.6 1.6 %shard_map.93 = (bf16[32,512]{1,0:T(8,128)(2,1)S(1)}, bf16[32,128]{1,0:T(8,128)(2,1)S(1)}) custom-call(bf16[16,4224]{1,0:T(8,128)(2,1)S(1)} %pad_maximum_fusion.1.refs_0_, bf16[16,4224]{1,0:T(8,128)(2,1)S(1)} %collective-permute-done.4.refs_1_, bf16[1,4096,256]{2,1,0:T(8,128)(2,1)S(1)} %copy-done, bf16[1,4096,256]{2,1,0:T(8,128)(2,1)S(1)} %get-tuple-element.44.refs_3_, ...), custom_call_target="tpu_custom_call" | custom-call | tf_op jit(solution)/shard_map/pallas_call | solution.py:265
  20.2 0.7 %collective-permute-start.7 = (bf16[32,512]{1,0:T(8,128)(2,1)S(1)}, bf16[32,512]{1,0:T(8,128)(2,1)S(1)}, u32[]{:S(2)}, u32[]{:S(2)}) collective-permute-start(bf16[32,512]{1,0:T(8,128)(2,1)S(1)} %get-tuple-element.45.refs_0_), channel_id=1, source_target_pairs={{0,2},{1,3},{2,0},{3,1},{4,6},{5,7},{6,4},{7,5},{8,10},{9,11},{10,... | collective-permute-start | bytes 98312 | tf_op jit(solution)/shard_map/ppermute | solution.py:20
  20.9 1.6 %collective-permute-done.8.refs_3_ = bf16[64,3072]{1,0:T(8,128)(2,1)S(1)} collective-permute-done((bf16[64,3072]{1,0:T(8,128)(2,1)S(1)}, bf16[64,3072]{1,0:T(8,128)(2,1)S(1)}, u32[]{:S(2)}, u32[]{:S(2)}) %collective-permute-start.8) | collective-permute-done | bytes 393248 | tf_op jit(solution)/shard_map/ppermute | solution.py:20
  22.5 1.7 %collective-permute-done.7.refs_1_ = bf16[32,512]{1,0:T(8,128)(2,1)S(1)} collective-permute-done((bf16[32,512]{1,0:T(8,128)(2,1)S(1)}, bf16[32,512]{1,0:T(8,128)(2,1)S(1)}, u32[]{:S(2)}, u32[]{:S(2)}) %collective-permute-start.7) | collective-permute-done | bytes 32800 | tf_op jit(solution)/shard_map/ppermute | solution.py:20
  24.2 0.0 collective-permute-done.9.refs_6_
  24.2 0.0 copy-done.1
  24.2 1.1 %shard_map.94 = bf16[8,4,2048]{2,1,0:T(4,128)(2,1)S(1)} custom-call(bf16[32,512]{1,0:T(8,128)(2,1)S(1)} %get-tuple-element.45.refs_0_, bf16[32,512]{1,0:T(8,128)(2,1)S(1)} %collective-permute-done.7.refs_1_, bf16[64,3072]{1,0:T(8,128)(2,1)S(1)} %pad_maximum_fusion.refs_2_, bf16[64,3072]{1,0:T(8,128)(2,1)S(1)} %collective-permute-done.8.refs_3_, ...), custom_call_target="tpu_custom_call" | custom-call | tf_op jit(solution)/shard_map/pallas_call | solution.py:277
  25.3 10.7 %all_to_all.5.back_ref = bf16[8,4,2048]{2,1,0:T(4,128)(2,1)S(1)} all-to-all(bf16[8,4,2048]{2,1,0:T(4,128)(2,1)S(1)} %shard_map.94), channel_id=1, replica_groups=mesh['groups'=2,'expert'=4,'quad'=2,'pair'=2] {'expert','quad'}, dimensions={0} | all-to-all | bytes 262144 | tf_op jit(solution)/shard_map/all_to_all | solution.py:289
  36.0 1.1 %shard_map.95 = bf16[64,4096]{1,0:T(8,128)(2,1)} custom-call(bf16[48,64]{1,0:T(8,128)(2,1)S(1)} %get-tuple-element.28.table_ref, bf16[8,4,2048]{2,1,0:T(4,128)(2,1)S(1)} %all_to_all.5.back_ref), custom_call_target="tpu_custom_call" | custom-call | tf_op jit(solution)/shard_map/pallas_call | solution.py:290
  (1 shorter events, 0.0 us)
Async XLA Ops:
  0.0 18.6 %copy-start = (bf16[1,4096,256]{2,1,0:T(8,128)(2,1)S(1)}, bf16[1,4096,256]{2,1,0:T(8,128)(2,1)}, u32[]{:S(2)}) copy-start(bf16[1,4096,256]{2,1,0:T(8,128)(2,1)} %refs_2_.1) | copy-start | bytes 6291460
  1.5 11.4 %collective-permute-start.3 = (bf16[32,3072]{1,0:T(8,128)(2,1)S(1)}, bf16[32,3072]{1,0:T(8,128)(2,1)S(1)}, u32[]{:S(2)}, u32[]{:S(2)}) collective-permute-start(bf16[32,3072]{1,0:T(8,128)(2,1)S(1)} %get-tuple-element.33), channel_id=1, source_target_pairs={{0,2},{1,3},{2,0},{3,1},{4,6},{5,7},{6,4},{7,5},{8,10},{9,11},{10,... | collective-permute-start | bytes 589832 | tf_op jit(solution)/shard_map/ppermute | solution.py:20
  4.5 6.1 %collective-permute-start = (bf16[4,4224]{1,0:T(4,128)(2,1)S(1)}, bf16[4,4224]{1,0:T(4,128)(2,1)S(1)}, u32[]{:S(2)}, u32[]{:S(2)}) collective-permute-start(bf16[4,4224]{1,0:T(4,128)(2,1)S(1)} %get-tuple-element.29), channel_id=1, source_target_pairs={{0,12},{4,8},{8,4},{12,0},{1,13},{5,9},{9,5},{13,1},{2,14},{6,10},... | collective-permute-start | bytes 101384 | tf_op jit(solution)/shard_map/ppermute | solution.py:20
  8.1 4.8 %collective-permute-start.1 = (bf16[4,4224]{1,0:T(4,128)(2,1)S(1)}, bf16[4,4224]{1,0:T(4,128)(2,1)S(1)}, u32[]{:S(2)}, u32[]{:S(2)}) collective-permute-start(bf16[4,4224]{1,0:T(4,128)(2,1)S(1)} %get-tuple-element.30), channel_id=1, source_target_pairs={{0,8},{4,12},{8,0},{12,4},{1,9},{5,13},{9,1},{13,5},{2,10},{6,14},... | collective-permute-start | bytes 101384 | tf_op jit(solution)/shard_map/ppermute | solution.py:20
  8.1 4.8 %collective-permute-start.2 = (bf16[4,4224]{1,0:T(4,128)(2,1)S(1)}, bf16[4,4224]{1,0:T(4,128)(2,1)S(1)}, u32[]{:S(2)}, u32[]{:S(2)}) collective-permute-start(bf16[4,4224]{1,0:T(4,128)(2,1)S(1)} %get-tuple-element.31), channel_id=1, source_target_pairs={{0,4},{4,0},{8,12},{12,8},{1,5},{5,1},{9,13},{13,9},{2,6},{6,2},{1... | collective-permute-start | bytes 101384 | tf_op jit(solution)/shard_map/ppermute | solution.py:20
  8.9 9.7 %collective-permute-start.5 = (bf16[1,4096,256]{2,1,0:T(8,128)(2,1)}, bf16[1,4096,256]{2,1,0:T(8,128)(2,1)S(1)}, u32[]{:S(2)}, u32[]{:S(2)}) collective-permute-start(bf16[1,4096,256]{2,1,0:T(8,128)(2,1)} %refs_2_.1), channel_id=1, source_target_pairs={{0,1},{1,0},{2,3},{3,2},{4,5},{5,4},{6,7},{7,6},{8,9},{9,8},{10,11... | collective-permute-start | bytes 6291464 | tf_op jit(solution)/shard_map/ppermute | solution.py:20
  13.0 5.1 %collective-permute-start.4 = (bf16[16,4224]{1,0:T(8,128)(2,1)S(1)}, bf16[16,4224]{1,0:T(8,128)(2,1)S(1)}, u32[]{:S(2)}, u32[]{:S(2)}) collective-permute-start(bf16[16,4224]{1,0:T(8,128)(2,1)S(1)} %pad_maximum_fusion.1.refs_0_), channel_id=1, source_target_pairs={{0,2},{1,3},{2,0},{3,1},{4,6},{5,7},{6,4},{7,5},{8,10},{9,11},{10,... | collective-permute-start | bytes 405512 | tf_op jit(solution)/shard_map/ppermute | solution.py:20
  13.6 5.0 %collective-permute-start.6 = (bf16[1,4096,256]{2,1,0:T(8,128)(2,1)S(1)}, bf16[1,4096,256]{2,1,0:T(8,128)(2,1)S(1)}, u32[]{:S(2)}, u32[]{:S(2)}) collective-permute-start(bf16[1,4096,256]{2,1,0:T(8,128)(2,1)S(1)} %get-tuple-element.44.refs_3_), channel_id=1, source_target_pairs={{0,1},{1,0},{2,3},{3,2},{4,5},{5,4},{6,7},{7,6},{8,9},{9,8},{10,11... | collective-permute-start | bytes 6291464 | tf_op jit(solution)/shard_map/ppermute | solution.py:20
  18.1 6.1 %copy-start.1 = (bf16[1,1024,1024]{2,1,0:T(8,128)(2,1)S(1)}, bf16[1,1024,1024]{2,1,0:T(8,128)(2,1)}, u32[]{:S(2)}) copy-start(bf16[1,1024,1024]{2,1,0:T(8,128)(2,1)} %param.15) | copy-start | bytes 6291460
  18.1 6.1 %collective-permute-start.9 = (bf16[1024,1024]{1,0:T(8,128)(2,1)}, bf16[1024,1024]{1,0:T(8,128)(2,1)S(1)}, u32[]{:S(2)}, u32[]{:S(2)}) collective-permute-start(bf16[1024,1024]{1,0:T(8,128)(2,1)} %bitcast.6), channel_id=1, source_target_pairs={{0,1},{1,0},{2,3},{3,2},{4,5},{5,4},{6,7},{7,6},{8,9},{9,8},{10,11... | collective-permute-start | bytes 6291464 | tf_op jit(solution)/shard_map/ppermute | solution.py:20
  18.1 4.3 %collective-permute-start.8 = (bf16[64,3072]{1,0:T(8,128)(2,1)S(1)}, bf16[64,3072]{1,0:T(8,128)(2,1)S(1)}, u32[]{:S(2)}, u32[]{:S(2)}) collective-permute-start(bf16[64,3072]{1,0:T(8,128)(2,1)S(1)} %pad_maximum_fusion.refs_2_), channel_id=1, source_target_pairs={{0,1},{1,0},{2,3},{3,2},{4,5},{5,4},{6,7},{7,6},{8,9},{9,8},{10,11... | collective-permute-start | bytes 1179656 | tf_op jit(solution)/shard_map/ppermute | solution.py:20
  20.2 4.0 %collective-permute-start.7 = (bf16[32,512]{1,0:T(8,128)(2,1)S(1)}, bf16[32,512]{1,0:T(8,128)(2,1)S(1)}, u32[]{:S(2)}, u32[]{:S(2)}) collective-permute-start(bf16[32,512]{1,0:T(8,128)(2,1)S(1)} %get-tuple-element.45.refs_0_), channel_id=1, source_target_pairs={{0,2},{1,3},{2,0},{3,1},{4,6},{5,7},{6,4},{7,5},{8,10},{9,11},{10,... | collective-permute-start | bytes 98312 | tf_op jit(solution)/shard_map/ppermute | solution.py:20

commit v5 on v4

--- a/solution.py
+++ b/solution.py
@@ -242,8 +242,11 @@
     )(*in_hbm(ids, weights, up_weight), packed[0])
 
     factors = [factors[0]] + [xor_permute(factors[q], REQUEST, q * PAIR) for q in range(1, quads)]
-    blocks, up, factors[1:] = lax.optimization_barrier((blocks[::-1], up, factors[1:]))
-    blocks = blocks[::-1]
+    far_first = sorted(range(1, experts), key=lambda s: (s == 1, s))
+    tied, up, factors[1:] = lax.optimization_barrier(
+        ([blocks[s] for s in far_first], up, factors[1:])
+    )
+    blocks = [blocks[0]] + [tied[far_first.index(s)] for s in range(1, experts)]
     rows = jnp.concatenate(blocks, axis=0)
     rows, up_source = lax.optimization_barrier((rows, up))
     up2 = xor_permute(up_source, REQUEST, 1)

time: 37.3 us -> 37 us (level)
  no operation moved by 1% of the time
where the time goes in v5:
time: 37 us; the launch traced here: 36.8 us
  blocking collectives  10.5 us (28%)
  waiting for transfers between devices  10.2 us (28%)
  starting transfers between devices  9 us (24%)
  Pallas kernels  6.91 us (19%)
    all_to_all x1, blocking collectives, body(): back = lax.all_to_all(out, ('expert', 'quad'), 0, 0, tiled=True)  10.5 us
    ppermute x10, waiting for transfers between devices, xor_permute(): lax.ppermute(value, axis, [(i, i ^ offset) for i in range(lax.axis_size(a...  10.2 us
    ppermute x10, starting transfers between devices, xor_permute(): lax.ppermute(value, axis, [(i, i ^ offset) for i in range(lax.axis_size(a...  9 us
    pallas_call x1, Pallas kernels, body(): pl.pallas_call(stage_kernel, out_shape=[jax.ShapeDtypeStruct((3 * experts...  1.65 us
    pallas_call x1, Pallas kernels, body(): pl.pallas_call(functools.partial(hidden_kernel, len(slots)), out_shape=[j...  1.56 us
    pallas_call x1, Pallas kernels, body(): pl.pallas_call(functools.partial(pack_kernel, quads), out_shape=[jax.Shap...  1.5 us
    pallas_call x1, Pallas kernels, body(): pl.pallas_call(functools.partial(down_kernel, order, n_req, cols), out_sh...  1.14 us
    pallas_call x1, Pallas kernels, body(): pl.pallas_call(combine_kernel, out_shape=jax.ShapeDtypeStruct((tokens, wi...  1.06 us
  transfers between devices with their start and end apart: 10, of which 4 were waited for; matrix products, arithmetic and copies ran while one was open for 0% of the time, Pallas kernels for 9%

profile of v5, /device:TPU:0, one launch (start us, length us, event | category | flops | bytes accessed | tf_op | source)
XLA Modules:
  0.0 36.8 jit_solution(7863993598902800320)
XLA Ops:
  0.0 0.0 copy-start
  0.0 1.5 %shard_map.91 = (bf16[32,3072]{1,0:T(8,128)(2,1)S(1)}, bf16[32,3072]{1,0:T(8,128)(2,1)S(1)}, bf16[4,4224]{1,0:T(4,128)(2,1)S(1)}, bf16[4,4224]{1,0:T(4,128)(2,1)...) custom-call(s32[8,64]{1,0:T(8,128)} %bitcast.10, s32[1,64]{1,0:T(1,128)} %bitcast.13, ...), custom_call_target="tpu_custom_call" | custom-call | tf_op jit(solution)/shard_map/pallas_call | solution.py:200
  1.5 3.0 %collective-permute-start.3 = (bf16[32,3072]{1,0:T(8,128)(2,1)S(1)}, bf16[32,3072]{1,0:T(8,128)(2,1)S(1)}, u32[]{:S(2)}, u32[]{:S(2)}) collective-permute-start(bf16[32,3072]{1,0:T(8,128)(2,1)S(1)} %get-tuple-element.32), channel_id=1, source_target_pairs={{0,2},{1,3},{2,0},{3,1},{4,6},{5,7},{6,4},{7,5},{8,10},{9,11},{10,... | collective-permute-start | bytes 589832 | tf_op jit(solution)/shard_map/ppermute | solution.py:20
  4.5 2.6 %collective-permute-start = (bf16[4,4224]{1,0:T(4,128)(2,1)S(1)}, bf16[4,4224]{1,0:T(4,128)(2,1)S(1)}, u32[]{:S(2)}, u32[]{:S(2)}) collective-permute-start(bf16[4,4224]{1,0:T(4,128)(2,1)S(1)} %get-tuple-element.28), channel_id=1, source_target_pairs={{0,8},{4,12},{8,0},{12,4},{1,9},{5,13},{9,1},{13,5},{2,10},{6,14},... | collective-permute-start | bytes 101384 | tf_op jit(solution)/shard_map/ppermute | solution.py:20
  7.1 1.3 %collective-permute-start.1 = (bf16[4,4224]{1,0:T(4,128)(2,1)S(1)}, bf16[4,4224]{1,0:T(4,128)(2,1)S(1)}, u32[]{:S(2)}, u32[]{:S(2)}) collective-permute-start(bf16[4,4224]{1,0:T(4,128)(2,1)S(1)} %get-tuple-element.29), channel_id=1, source_target_pairs={{0,12},{4,8},{8,4},{12,0},{1,13},{5,9},{9,5},{13,1},{2,14},{6,10},... | collective-permute-start | bytes 101384 | tf_op jit(solution)/shard_map/ppermute | solution.py:20
  8.5 0.2 collective-permute-start.2
  8.7 0.0 collective-permute-start.5
  8.7 1.6 %shard_map.92 = (bf16[48,64]{1,0:T(8,128)(2,1)S(1)}, bf16[1,4096,256]{2,1,0:T(8,128)(2,1)S(1)}) custom-call(s32[8,64]{1,0:T(8,128)} %bitcast.11, f32[8,64]{1,0:T(8,128)} %bitcast.12, bf16[1,4096,256]{2,1,0:T(8,128)(2,1)} %up_hbm.1, bf16[4,4224]{1,0:T(4,128)(2,1)S(1)} %get-tuple-element.26.after_ref), custom_call_target="tpu_custom_call" | custom-call | tf_op jit(solution)/shard_map/pallas_call | solution.py:228
  10.3 0.0 collective-permute-done
  10.4 2.5 %collective-permute-done.1 = bf16[4,4224]{1,0:T(4,128)(2,1)S(1)} collective-permute-done((bf16[4,4224]{1,0:T(4,128)(2,1)S(1)}, bf16[4,4224]{1,0:T(4,128)(2,1)S(1)}, u32[]{:S(2)}, u32[]{:S(2)}) %collective-permute-start.1) | collective-permute-done | bytes 33824 | tf_op jit(solution)/shard_map/ppermute | solution.py:20
  12.8 0.0 collective-permute-done.2
  12.8 0.0 collective-permute-done.3
  12.8 0.1 pad_maximum_fusion.1.refs_0_
  12.9 0.6 %collective-permute-start.4 = (bf16[16,4224]{1,0:T(8,128)(2,1)S(1)}, bf16[16,4224]{1,0:T(8,128)(2,1)S(1)}, u32[]{:S(2)}, u32[]{:S(2)}) collective-permute-start(bf16[16,4224]{1,0:T(8,128)(2,1)S(1)} %pad_maximum_fusion.1.refs_0_), channel_id=1, source_target_pairs={{0,2},{1,3},{2,0},{3,1},{4,6},{5,7},{6,4},{7,5},{8,10},{9,11},{10,... | collective-permute-start | bytes 405512 | tf_op jit(solution)/shard_map/ppermute | solution.py:20
  13.5 0.0 collective-permute-start.6
  13.6 4.4 %collective-permute-done.4.refs_1_ = bf16[16,4224]{1,0:T(8,128)(2,1)S(1)} collective-permute-done((bf16[16,4224]{1,0:T(8,128)(2,1)S(1)}, bf16[16,4224]{1,0:T(8,128)(2,1)S(1)}, u32[]{:S(2)}, u32[]{:S(2)}) %collective-permute-start.4) | collective-permute-done | bytes 135200 | tf_op jit(solution)/shard_map/ppermute | solution.py:20
  18.0 0.0 copy-start.1
  18.0 0.0 collective-permute-start.9
  18.0 0.5 %collective-permute-start.8 = (bf16[64,3072]{1,0:T(8,128)(2,1)S(1)}, bf16[64,3072]{1,0:T(8,128)(2,1)S(1)}, u32[]{:S(2)}, u32[]{:S(2)}) collective-permute-start(bf16[64,3072]{1,0:T(8,128)(2,1)S(1)} %pad_maximum_fusion.refs_2_), channel_id=1, source_target_pairs={{0,1},{1,0},{2,3},{3,2},{4,5},{5,4},{6,7},{7,6},{8,9},{9,8},{10,11... | collective-permute-start | bytes 1179656 | tf_op jit(solution)/shard_map/ppermute | solution.py:20
  18.5 0.0 collective-permute-done.5.refs_4_
  18.5 0.0 collective-permute-done.6.refs_5_
  18.5 0.0 copy-done
  18.5 1.6 %shard_map.93 = (bf16[32,512]{1,0:T(8,128)(2,1)S(1)}, bf16[32,128]{1,0:T(8,128)(2,1)S(1)}) custom-call(bf16[16,4224]{1,0:T(8,128)(2,1)S(1)} %pad_maximum_fusion.1.refs_0_, bf16[16,4224]{1,0:T(8,128)(2,1)S(1)} %collective-permute-done.4.refs_1_, bf16[1,4096,256]{2,1,0:T(8,128)(2,1)S(1)} %copy-done, bf16[1,4096,256]{2,1,0:T(8,128)(2,1)S(1)} %get-tuple-element.42.refs_3_, ...), custom_call_target="tpu_custom_call" | custom-call | tf_op jit(solution)/shard_map/pallas_call | solution.py:268
  20.1 0.7 %collective-permute-start.7 = (bf16[32,512]{1,0:T(8,128)(2,1)S(1)}, bf16[32,512]{1,0:T(8,128)(2,1)S(1)}, u32[]{:S(2)}, u32[]{:S(2)}) collective-permute-start(bf16[32,512]{1,0:T(8,128)(2,1)S(1)} %get-tuple-element.43.refs_0_), channel_id=1, source_target_pairs={{0,2},{1,3},{2,0},{3,1},{4,6},{5,7},{6,4},{7,5},{8,10},{9,11},{10,... | collective-permute-start | bytes 98312 | tf_op jit(solution)/shard_map/ppermute | solution.py:20
  20.8 1.5 %collective-permute-done.8.refs_3_ = bf16[64,3072]{1,0:T(8,128)(2,1)S(1)} collective-permute-done((bf16[64,3072]{1,0:T(8,128)(2,1)S(1)}, bf16[64,3072]{1,0:T(8,128)(2,1)S(1)}, u32[]{:S(2)}, u32[]{:S(2)}) %collective-permute-start.8) | collective-permute-done | bytes 393248 | tf_op jit(solution)/shard_map/ppermute | solution.py:20
  22.4 1.7 %collective-permute-done.7.refs_1_ = bf16[32,512]{1,0:T(8,128)(2,1)S(1)} collective-permute-done((bf16[32,512]{1,0:T(8,128)(2,1)S(1)}, bf16[32,512]{1,0:T(8,128)(2,1)S(1)}, u32[]{:S(2)}, u32[]{:S(2)}) %collective-permute-start.7) | collective-permute-done | bytes 32800 | tf_op jit(solution)/shard_map/ppermute | solution.py:20
  24.1 0.0 collective-permute-done.9.refs_6_
  24.1 0.0 copy-done.1
  24.1 1.1 %shard_map.94 = bf16[8,4,2048]{2,1,0:T(4,128)(2,1)S(1)} custom-call(bf16[32,512]{1,0:T(8,128)(2,1)S(1)} %get-tuple-element.43.refs_0_, bf16[32,512]{1,0:T(8,128)(2,1)S(1)} %collective-permute-done.7.refs_1_, bf16[64,3072]{1,0:T(8,128)(2,1)S(1)} %pad_maximum_fusion.refs_2_, bf16[64,3072]{1,0:T(8,128)(2,1)S(1)} %collective-permute-done.8.refs_3_, ...), custom_call_target="tpu_custom_call" | custom-call | tf_op jit(solution)/shard_map/pallas_call | solution.py:280
  25.2 10.5 %all_to_all.5.back_ref = bf16[8,4,2048]{2,1,0:T(4,128)(2,1)S(1)} all-to-all(bf16[8,4,2048]{2,1,0:T(4,128)(2,1)S(1)} %shard_map.94), channel_id=1, replica_groups=mesh['groups'=2,'expert'=4,'quad'=2,'pair'=2] {'expert','quad'}, dimensions={0} | all-to-all | bytes 262144 | tf_op jit(solution)/shard_map/all_to_all | solution.py:292
  35.8 1.1 %shard_map.95 = bf16[64,4096]{1,0:T(8,128)(2,1)} custom-call(bf16[48,64]{1,0:T(8,128)(2,1)S(1)} %get-tuple-element.27.table_ref, bf16[8,4,2048]{2,1,0:T(4,128)(2,1)S(1)} %all_to_all.5.back_ref), custom_call_target="tpu_custom_call" | custom-call | tf_op jit(solution)/shard_map/pallas_call | solution.py:293
  (1 shorter events, 0.0 us)
Async XLA Ops:
  0.0 18.5 %copy-start = (bf16[1,4096,256]{2,1,0:T(8,128)(2,1)S(1)}, bf16[1,4096,256]{2,1,0:T(8,128)(2,1)}, u32[]{:S(2)}) copy-start(bf16[1,4096,256]{2,1,0:T(8,128)(2,1)} %refs_2_.1) | copy-start | bytes 6291460
  1.5 11.3 %collective-permute-start.3 = (bf16[32,3072]{1,0:T(8,128)(2,1)S(1)}, bf16[32,3072]{1,0:T(8,128)(2,1)S(1)}, u32[]{:S(2)}, u32[]{:S(2)}) collective-permute-start(bf16[32,3072]{1,0:T(8,128)(2,1)S(1)} %get-tuple-element.32), channel_id=1, source_target_pairs={{0,2},{1,3},{2,0},{3,1},{4,6},{5,7},{6,4},{7,5},{8,10},{9,11},{10,... | collective-permute-start | bytes 589832 | tf_op jit(solution)/shard_map/ppermute | solution.py:20
  4.5 5.8 %collective-permute-start = (bf16[4,4224]{1,0:T(4,128)(2,1)S(1)}, bf16[4,4224]{1,0:T(4,128)(2,1)S(1)}, u32[]{:S(2)}, u32[]{:S(2)}) collective-permute-start(bf16[4,4224]{1,0:T(4,128)(2,1)S(1)} %get-tuple-element.28), channel_id=1, source_target_pairs={{0,8},{4,12},{8,0},{12,4},{1,9},{5,13},{9,1},{13,5},{2,10},{6,14},... | collective-permute-start | bytes 101384 | tf_op jit(solution)/shard_map/ppermute | solution.py:20
  7.1 5.7 %collective-permute-start.1 = (bf16[4,4224]{1,0:T(4,128)(2,1)S(1)}, bf16[4,4224]{1,0:T(4,128)(2,1)S(1)}, u32[]{:S(2)}, u32[]{:S(2)}) collective-permute-start(bf16[4,4224]{1,0:T(4,128)(2,1)S(1)} %get-tuple-element.29), channel_id=1, source_target_pairs={{0,12},{4,8},{8,4},{12,0},{1,13},{5,9},{9,5},{13,1},{2,14},{6,10},... | collective-permute-start | bytes 101384 | tf_op jit(solution)/shard_map/ppermute | solution.py:20
  8.5 4.4 %collective-permute-start.2 = (bf16[4,4224]{1,0:T(4,128)(2,1)S(1)}, bf16[4,4224]{1,0:T(4,128)(2,1)S(1)}, u32[]{:S(2)}, u32[]{:S(2)}) collective-permute-start(bf16[4,4224]{1,0:T(4,128)(2,1)S(1)} %get-tuple-element.30), channel_id=1, source_target_pairs={{0,4},{4,0},{8,12},{12,8},{1,5},{5,1},{9,13},{13,9},{2,6},{6,2},{1... | collective-permute-start | bytes 101384 | tf_op jit(solution)/shard_map/ppermute | solution.py:20
  8.7 9.8 %collective-permute-start.5 = (bf16[1,4096,256]{2,1,0:T(8,128)(2,1)}, bf16[1,4096,256]{2,1,0:T(8,128)(2,1)S(1)}, u32[]{:S(2)}, u32[]{:S(2)}) collective-permute-start(bf16[1,4096,256]{2,1,0:T(8,128)(2,1)} %refs_2_.1), channel_id=1, source_target_pairs={{0,1},{1,0},{2,3},{3,2},{4,5},{5,4},{6,7},{7,6},{8,9},{9,8},{10,11... | collective-permute-start | bytes 6291464 | tf_op jit(solution)/shard_map/ppermute | solution.py:20
  12.9 5.1 %collective-permute-start.4 = (bf16[16,4224]{1,0:T(8,128)(2,1)S(1)}, bf16[16,4224]{1,0:T(8,128)(2,1)S(1)}, u32[]{:S(2)}, u32[]{:S(2)}) collective-permute-start(bf16[16,4224]{1,0:T(8,128)(2,1)S(1)} %pad_maximum_fusion.1.refs_0_), channel_id=1, source_target_pairs={{0,2},{1,3},{2,0},{3,1},{4,6},{5,7},{6,4},{7,5},{8,10},{9,11},{10,... | collective-permute-start | bytes 405512 | tf_op jit(solution)/shard_map/ppermute | solution.py:20
  13.5 5.0 %collective-permute-start.6 = (bf16[1,4096,256]{2,1,0:T(8,128)(2,1)S(1)}, bf16[1,4096,256]{2,1,0:T(8,128)(2,1)S(1)}, u32[]{:S(2)}, u32[]{:S(2)}) collective-permute-start(bf16[1,4096,256]{2,1,0:T(8,128)(2,1)S(1)} %get-tuple-element.42.refs_3_), channel_id=1, source_target_pairs={{0,1},{1,0},{2,3},{3,2},{4,5},{5,4},{6,7},{7,6},{8,9},{9,8},{10,11... | collective-permute-start | bytes 6291464 | tf_op jit(solution)/shard_map/ppermute | solution.py:20
  18.0 6.1 %copy-start.1 = (bf16[1,1024,1024]{2,1,0:T(8,128)(2,1)S(1)}, bf16[1,1024,1024]{2,1,0:T(8,128)(2,1)}, u32[]{:S(2)}) copy-start(bf16[1,1024,1024]{2,1,0:T(8,128)(2,1)} %param.15) | copy-start | bytes 6291460
  18.0 6.1 %collective-permute-start.9 = (bf16[1024,1024]{1,0:T(8,128)(2,1)}, bf16[1024,1024]{1,0:T(8,128)(2,1)S(1)}, u32[]{:S(2)}, u32[]{:S(2)}) collective-permute-start(bf16[1024,1024]{1,0:T(8,128)(2,1)} %bitcast.6), channel_id=1, source_target_pairs={{0,1},{1,0},{2,3},{3,2},{4,5},{5,4},{6,7},{7,6},{8,9},{9,8},{10,11... | collective-permute-start | bytes 6291464 | tf_op jit(solution)/shard_map/ppermute | solution.py:20
  18.0 4.3 %collective-permute-start.8 = (bf16[64,3072]{1,0:T(8,128)(2,1)S(1)}, bf16[64,3072]{1,0:T(8,128)(2,1)S(1)}, u32[]{:S(2)}, u32[]{:S(2)}) collective-permute-start(bf16[64,3072]{1,0:T(8,128)(2,1)S(1)} %pad_maximum_fusion.refs_2_), channel_id=1, source_target_pairs={{0,1},{1,0},{2,3},{3,2},{4,5},{5,4},{6,7},{7,6},{8,9},{9,8},{10,11... | collective-permute-start | bytes 1179656 | tf_op jit(solution)/shard_map/ppermute | solution.py:20
  20.1 4.0 %collective-permute-start.7 = (bf16[32,512]{1,0:T(8,128)(2,1)S(1)}, bf16[32,512]{1,0:T(8,128)(2,1)S(1)}, u32[]{:S(2)}, u32[]{:S(2)}) collective-permute-start(bf16[32,512]{1,0:T(8,128)(2,1)S(1)} %get-tuple-element.43.refs_0_), channel_id=1, source_target_pairs={{0,2},{1,3},{2,0},{3,1},{4,6},{5,7},{6,4},{7,5},{8,10},{9,11},{10,... | collective-permute-start | bytes 98312 | tf_op jit(solution)/shard_map/ppermute | solution.py:20

commit v6 on v5

--- a/solution.py
+++ b/solution.py
@@ -51,7 +51,9 @@
     factor_refs, out_refs, scratches = refs[:quads], refs[quads:-5], refs[-5:]
     ids_ref, req_ref, x_ref, scratch, sems = scratches
     half = second_hbm.shape[1] // quads
-    pairs = [(ids_hbm, ids_ref), (req_hbm, req_ref), (x_hbm, x_ref)]
+    pairs = [(ids_hbm, ids_ref), (req_hbm, req_ref)]
+    parts = [pl.ds(i * half, half) for i in range(quads)]
+    pairs += [(x_hbm.at[:, at], x_ref.at[:, at]) for at in parts]
     for q, factor_ref in enumerate(factor_refs):
         at = pl.multiple_of((lax.axis_index("quad") ^ q) * half, half)
         pairs.append((second_hbm.at[:, pl.ds(at, half)], factor_ref.at[:, pl.ds(0, half)]))
@@ -67,13 +69,13 @@
     table = jnp.concatenate([slot_values(ids, ones, me ^ s) for s in range(experts)], axis=0)
     owner = jnp.sum(table * (req_ref[...] + 1).astype(jnp.float32), axis=1, keepdims=True) - 1.0
     scratch[:, width:] = jnp.broadcast_to(owner, (owner.shape[0], LANES))
-    copies[2].wait()
-    scratch[:, :width] = jnp.dot(
-        table.astype(jnp.bfloat16), x_ref[...], preferred_element_type=jnp.float32
-    )
+    table = table.astype(jnp.bfloat16)
+    for copy, at in zip(copies[2:], parts):
+        copy.wait()
+        scratch[:, at] = jnp.dot(table, x_ref[:, at], preferred_element_type=jnp.float32)
     for s, out_ref in enumerate(out_refs[::-1]):
         out_ref[...] = scratch[pl.ds(s * CAP, CAP), :].astype(out_ref.dtype)
-    for copy in copies[3:]:
+    for copy in copies[2 + quads :]:
         copy.wait()
 
 
@@ -156,20 +158,22 @@
 
 def combine_kernel(table_ref, back_ref, mixed_hbm, scratch, done, sems):
     experts = scratch.shape[0] // CAP
-    quads = done.shape[0]
-    cols = done.shape[2]
+    chunks, _, size = done.shape
+    quads = back_ref.shape[0] // experts
+    each = chunks // quads
     copies = []
-    for q in range(quads):
+    for i in range(chunks):
+        q, lanes = i // each, pl.ds(i % each * size, size)
         for e in range(experts):
-            scratch[pl.ds(e * CAP, CAP), :] = back_ref[e * quads + q].astype(jnp.float32)
-        rows = scratch[...].astype(jnp.bfloat16)
+            scratch[pl.ds(e * CAP, CAP), lanes] = back_ref[e * quads + q, :, lanes].astype(jnp.float32)
+        rows = scratch[:, lanes].astype(jnp.bfloat16)
         mixed = lax.dot_general(
             table_ref[...], jnp.concatenate([rows] * 3, axis=0), (((0,), (0,)), ((), ())),
             preferred_element_type=jnp.float32,
         )
-        done[q] = mixed.astype(done.dtype)
-        at = pl.ds(q * cols, cols)
-        copies.append(pltpu.make_async_copy(done.at[q], mixed_hbm.at[:, at], sems.at[q]))
+        done[i] = mixed.astype(done.dtype)
+        at = pl.ds(i * size, size)
+        copies.append(pltpu.make_async_copy(done.at[i], mixed_hbm.at[:, at], sems.at[i]))
         copies[-1].start()
     for copy in copies:
         copy.wait()
@@ -208,7 +212,7 @@
             pltpu.VMEM((1, tokens), jnp.int32),
             pltpu.VMEM(token_input.shape, bf16),
             pltpu.VMEM((experts * CAP, width + LANES), f32),
-            dma((3 + 2 * quads,)),
+            dma((2 + 3 * quads,)),
         ],
         compiler_params=PARAMS,
     )(
@@ -297,8 +301,8 @@
         out_specs=HBM,
         scratch_shapes=[
             pltpu.VMEM((experts * CAP, PAIR * cols), f32),
-            pltpu.VMEM((quads, tokens, PAIR * cols), bf16),
-            dma((quads,)),
+            pltpu.VMEM((PAIR * quads, tokens, cols), bf16),
+            dma((PAIR * quads,)),
         ],
         compiler_params=PARAMS,
     )(table, back)

time: 37 us -> 37 us (level)
  no operation moved by 1% of the time
where the time goes in v6:
time: 37 us; the launch traced here: 36.8 us
  blocking collectives  10.5 us (28%)
  waiting for transfers between devices  10.2 us (28%)
  starting transfers between devices  9 us (24%)
  Pallas kernels  6.94 us (19%)
    all_to_all x1, blocking collectives, body(): back = lax.all_to_all(out, ('expert', 'quad'), 0, 0, tiled=True)  10.5 us
    ppermute x10, waiting for transfers between devices, xor_permute(): lax.ppermute(value, axis, [(i, i ^ offset) for i in range(lax.axis_size(a...  10.2 us
    ppermute x10, starting transfers between devices, xor_permute(): lax.ppermute(value, axis, [(i, i ^ offset) for i in range(lax.axis_size(a...  9 us
    pallas_call x1, Pallas kernels, body(): pl.pallas_call(stage_kernel, out_shape=[jax.ShapeDtypeStruct((3 * experts...  1.65 us
    pallas_call x1, Pallas kernels, body(): pl.pallas_call(functools.partial(hidden_kernel, len(slots)), out_shape=[j...  1.56 us
    pallas_call x1, Pallas kernels, body(): pl.pallas_call(functools.partial(pack_kernel, quads), out_shape=[jax.Shap...  1.55 us
    pallas_call x1, Pallas kernels, body(): pl.pallas_call(functools.partial(down_kernel, order, n_req, cols), out_sh...  1.14 us
    pallas_call x1, Pallas kernels, body(): pl.pallas_call(combine_kernel, out_shape=jax.ShapeDtypeStruct((tokens, wi...  1.03 us
  transfers between devices with their start and end apart: 10, of which 4 were waited for; matrix products, arithmetic and copies ran while one was open for 0% of the time, Pallas kernels for 9%

profile of v6, /device:TPU:0, one launch (start us, length us, event | category | flops | bytes accessed | tf_op | source)
XLA Modules:
  0.0 36.8 jit_solution(15102868655443577515)
XLA Ops:
  0.0 0.0 copy-start
  0.0 1.6 %shard_map.91 = (bf16[32,3072]{1,0:T(8,128)(2,1)S(1)}, bf16[32,3072]{1,0:T(8,128)(2,1)S(1)}, bf16[4,4224]{1,0:T(4,128)(2,1)S(1)}, bf16[4,4224]{1,0:T(4,128)(2,1)...) custom-call(s32[8,64]{1,0:T(8,128)} %bitcast.10, s32[1,64]{1,0:T(1,128)} %bitcast.13, ...), custom_call_target="tpu_custom_call" | custom-call | tf_op jit(solution)/shard_map/pallas_call | solution.py:204
  1.6 3.0 %collective-permute-start.3 = (bf16[32,3072]{1,0:T(8,128)(2,1)S(1)}, bf16[32,3072]{1,0:T(8,128)(2,1)S(1)}, u32[]{:S(2)}, u32[]{:S(2)}) collective-permute-start(bf16[32,3072]{1,0:T(8,128)(2,1)S(1)} %get-tuple-element.32), channel_id=1, source_target_pairs={{0,2},{1,3},{2,0},{3,1},{4,6},{5,7},{6,4},{7,5},{8,10},{9,11},{10,... | collective-permute-start | bytes 589832 | tf_op jit(solution)/shard_map/ppermute | solution.py:20
  4.6 2.6 %collective-permute-start = (bf16[4,4224]{1,0:T(4,128)(2,1)S(1)}, bf16[4,4224]{1,0:T(4,128)(2,1)S(1)}, u32[]{:S(2)}, u32[]{:S(2)}) collective-permute-start(bf16[4,4224]{1,0:T(4,128)(2,1)S(1)} %get-tuple-element.28), channel_id=1, source_target_pairs={{0,8},{4,12},{8,0},{12,4},{1,9},{5,13},{9,1},{13,5},{2,10},{6,14},... | collective-permute-start | bytes 101384 | tf_op jit(solution)/shard_map/ppermute | solution.py:20
  7.2 1.3 %collective-permute-start.1 = (bf16[4,4224]{1,0:T(4,128)(2,1)S(1)}, bf16[4,4224]{1,0:T(4,128)(2,1)S(1)}, u32[]{:S(2)}, u32[]{:S(2)}) collective-permute-start(bf16[4,4224]{1,0:T(4,128)(2,1)S(1)} %get-tuple-element.29), channel_id=1, source_target_pairs={{0,12},{4,8},{8,4},{12,0},{1,13},{5,9},{9,5},{13,1},{2,14},{6,10},... | collective-permute-start | bytes 101384 | tf_op jit(solution)/shard_map/ppermute | solution.py:20
  8.5 0.2 collective-permute-start.2
  8.7 0.0 collective-permute-start.5
  8.7 1.6 %shard_map.92 = (bf16[48,64]{1,0:T(8,128)(2,1)S(1)}, bf16[1,4096,256]{2,1,0:T(8,128)(2,1)S(1)}) custom-call(s32[8,64]{1,0:T(8,128)} %bitcast.11, f32[8,64]{1,0:T(8,128)} %bitcast.12, bf16[1,4096,256]{2,1,0:T(8,128)(2,1)} %up_hbm.1, bf16[4,4224]{1,0:T(4,128)(2,1)S(1)} %get-tuple-element.26.after_ref), custom_call_target="tpu_custom_call" | custom-call | tf_op jit(solution)/shard_map/pallas_call | solution.py:232
  10.4 0.0 collective-permute-done
  10.4 2.5 %collective-permute-done.1 = bf16[4,4224]{1,0:T(4,128)(2,1)S(1)} collective-permute-done((bf16[4,4224]{1,0:T(4,128)(2,1)S(1)}, bf16[4,4224]{1,0:T(4,128)(2,1)S(1)}, u32[]{:S(2)}, u32[]{:S(2)}) %collective-permute-start.1) | collective-permute-done | bytes 33824 | tf_op jit(solution)/shard_map/ppermute | solution.py:20
  12.9 0.0 collective-permute-done.2
  12.9 0.0 collective-permute-done.3
  12.9 0.1 pad_maximum_fusion.1.refs_0_
  13.0 0.6 %collective-permute-start.4 = (bf16[16,4224]{1,0:T(8,128)(2,1)S(1)}, bf16[16,4224]{1,0:T(8,128)(2,1)S(1)}, u32[]{:S(2)}, u32[]{:S(2)}) collective-permute-start(bf16[16,4224]{1,0:T(8,128)(2,1)S(1)} %pad_maximum_fusion.1.refs_0_), channel_id=1, source_target_pairs={{0,2},{1,3},{2,0},{3,1},{4,6},{5,7},{6,4},{7,5},{8,10},{9,11},{10,... | collective-permute-start | bytes 405512 | tf_op jit(solution)/shard_map/ppermute | solution.py:20
  13.6 0.0 collective-permute-start.6
  13.6 4.4 %collective-permute-done.4.refs_1_ = bf16[16,4224]{1,0:T(8,128)(2,1)S(1)} collective-permute-done((bf16[16,4224]{1,0:T(8,128)(2,1)S(1)}, bf16[16,4224]{1,0:T(8,128)(2,1)S(1)}, u32[]{:S(2)}, u32[]{:S(2)}) %collective-permute-start.4) | collective-permute-done | bytes 135200 | tf_op jit(solution)/shard_map/ppermute | solution.py:20
  18.1 0.0 copy-start.1
  18.1 0.0 collective-permute-start.9
  18.1 0.5 %collective-permute-start.8 = (bf16[64,3072]{1,0:T(8,128)(2,1)S(1)}, bf16[64,3072]{1,0:T(8,128)(2,1)S(1)}, u32[]{:S(2)}, u32[]{:S(2)}) collective-permute-start(bf16[64,3072]{1,0:T(8,128)(2,1)S(1)} %pad_maximum_fusion.refs_2_), channel_id=1, source_target_pairs={{0,1},{1,0},{2,3},{3,2},{4,5},{5,4},{6,7},{7,6},{8,9},{9,8},{10,11... | collective-permute-start | bytes 1179656 | tf_op jit(solution)/shard_map/ppermute | solution.py:20
  18.6 0.0 collective-permute-done.5.refs_4_
  18.6 0.0 collective-permute-done.6.refs_5_
  18.6 0.0 copy-done
  18.6 1.6 %shard_map.93 = (bf16[32,512]{1,0:T(8,128)(2,1)S(1)}, bf16[32,128]{1,0:T(8,128)(2,1)S(1)}) custom-call(bf16[16,4224]{1,0:T(8,128)(2,1)S(1)} %pad_maximum_fusion.1.refs_0_, bf16[16,4224]{1,0:T(8,128)(2,1)S(1)} %collective-permute-done.4.refs_1_, bf16[1,4096,256]{2,1,0:T(8,128)(2,1)S(1)} %copy-done, bf16[1,4096,256]{2,1,0:T(8,128)(2,1)S(1)} %get-tuple-element.42.refs_3_, ...), custom_call_target="tpu_custom_call" | custom-call | tf_op jit(solution)/shard_map/pallas_call | solution.py:272
  20.1 0.7 %collective-permute-start.7 = (bf16[32,512]{1,0:T(8,128)(2,1)S(1)}, bf16[32,512]{1,0:T(8,128)(2,1)S(1)}, u32[]{:S(2)}, u32[]{:S(2)}) collective-permute-start(bf16[32,512]{1,0:T(8,128)(2,1)S(1)} %get-tuple-element.43.refs_0_), channel_id=1, source_target_pairs={{0,2},{1,3},{2,0},{3,1},{4,6},{5,7},{6,4},{7,5},{8,10},{9,11},{10,... | collective-permute-start | bytes 98312 | tf_op jit(solution)/shard_map/ppermute | solution.py:20
  20.9 1.5 %collective-permute-done.8.refs_3_ = bf16[64,3072]{1,0:T(8,128)(2,1)S(1)} collective-permute-done((bf16[64,3072]{1,0:T(8,128)(2,1)S(1)}, bf16[64,3072]{1,0:T(8,128)(2,1)S(1)}, u32[]{:S(2)}, u32[]{:S(2)}) %collective-permute-start.8) | collective-permute-done | bytes 393248 | tf_op jit(solution)/shard_map/ppermute | solution.py:20
  22.4 1.7 %collective-permute-done.7.refs_1_ = bf16[32,512]{1,0:T(8,128)(2,1)S(1)} collective-permute-done((bf16[32,512]{1,0:T(8,128)(2,1)S(1)}, bf16[32,512]{1,0:T(8,128)(2,1)S(1)}, u32[]{:S(2)}, u32[]{:S(2)}) %collective-permute-start.7) | collective-permute-done | bytes 32800 | tf_op jit(solution)/shard_map/ppermute | solution.py:20
  24.1 0.0 collective-permute-done.9.refs_6_
  24.1 0.0 copy-done.1
  24.1 1.1 %shard_map.94 = bf16[8,4,2048]{2,1,0:T(4,128)(2,1)S(1)} custom-call(bf16[32,512]{1,0:T(8,128)(2,1)S(1)} %get-tuple-element.43.refs_0_, bf16[32,512]{1,0:T(8,128)(2,1)S(1)} %collective-permute-done.7.refs_1_, bf16[64,3072]{1,0:T(8,128)(2,1)S(1)} %pad_maximum_fusion.refs_2_, bf16[64,3072]{1,0:T(8,128)(2,1)S(1)} %collective-permute-done.8.refs_3_, ...), custom_call_target="tpu_custom_call" | custom-call | tf_op jit(solution)/shard_map/pallas_call | solution.py:284
  25.3 10.5 %all_to_all.5.back_ref = bf16[8,4,2048]{2,1,0:T(4,128)(2,1)S(1)} all-to-all(bf16[8,4,2048]{2,1,0:T(4,128)(2,1)S(1)} %shard_map.94), channel_id=1, replica_groups=mesh['groups'=2,'expert'=4,'quad'=2,'pair'=2] {'expert','quad'}, dimensions={0} | all-to-all | bytes 262144 | tf_op jit(solution)/shard_map/all_to_all | solution.py:296
  35.8 1.0 %shard_map.95 = bf16[64,4096]{1,0:T(8,128)(2,1)} custom-call(bf16[48,64]{1,0:T(8,128)(2,1)S(1)} %get-tuple-element.27.table_ref, bf16[8,4,2048]{2,1,0:T(4,128)(2,1)S(1)} %all_to_all.5.back_ref), custom_call_target="tpu_custom_call" | custom-call | tf_op jit(solution)/shard_map/pallas_call | solution.py:297
  (1 shorter events, 0.0 us)
Async XLA Ops:
  0.0 18.6 %copy-start = (bf16[1,4096,256]{2,1,0:T(8,128)(2,1)S(1)}, bf16[1,4096,256]{2,1,0:T(8,128)(2,1)}, u32[]{:S(2)}) copy-start(bf16[1,4096,256]{2,1,0:T(8,128)(2,1)} %refs_2_.1) | copy-start | bytes 6291460
  1.6 11.3 %collective-permute-start.3 = (bf16[32,3072]{1,0:T(8,128)(2,1)S(1)}, bf16[32,3072]{1,0:T(8,128)(2,1)S(1)}, u32[]{:S(2)}, u32[]{:S(2)}) collective-permute-start(bf16[32,3072]{1,0:T(8,128)(2,1)S(1)} %get-tuple-element.32), channel_id=1, source_target_pairs={{0,2},{1,3},{2,0},{3,1},{4,6},{5,7},{6,4},{7,5},{8,10},{9,11},{10,... | collective-permute-start | bytes 589832 | tf_op jit(solution)/shard_map/ppermute | solution.py:20
  4.6 5.8 %collective-permute-start = (bf16[4,4224]{1,0:T(4,128)(2,1)S(1)}, bf16[4,4224]{1,0:T(4,128)(2,1)S(1)}, u32[]{:S(2)}, u32[]{:S(2)}) collective-permute-start(bf16[4,4224]{1,0:T(4,128)(2,1)S(1)} %get-tuple-element.28), channel_id=1, source_target_pairs={{0,8},{4,12},{8,0},{12,4},{1,9},{5,13},{9,1},{13,5},{2,10},{6,14},... | collective-permute-start | bytes 101384 | tf_op jit(solution)/shard_map/ppermute | solution.py:20
  7.2 5.7 %collective-permute-start.1 = (bf16[4,4224]{1,0:T(4,128)(2,1)S(1)}, bf16[4,4224]{1,0:T(4,128)(2,1)S(1)}, u32[]{:S(2)}, u32[]{:S(2)}) collective-permute-start(bf16[4,4224]{1,0:T(4,128)(2,1)S(1)} %get-tuple-element.29), channel_id=1, source_target_pairs={{0,12},{4,8},{8,4},{12,0},{1,13},{5,9},{9,5},{13,1},{2,14},{6,10},... | collective-permute-start | bytes 101384 | tf_op jit(solution)/shard_map/ppermute | solution.py:20
  8.5 4.4 %collective-permute-start.2 = (bf16[4,4224]{1,0:T(4,128)(2,1)S(1)}, bf16[4,4224]{1,0:T(4,128)(2,1)S(1)}, u32[]{:S(2)}, u32[]{:S(2)}) collective-permute-start(bf16[4,4224]{1,0:T(4,128)(2,1)S(1)} %get-tuple-element.30), channel_id=1, source_target_pairs={{0,4},{4,0},{8,12},{12,8},{1,5},{5,1},{9,13},{13,9},{2,6},{6,2},{1... | collective-permute-start | bytes 101384 | tf_op jit(solution)/shard_map/ppermute | solution.py:20
  8.7 9.8 %collective-permute-start.5 = (bf16[1,4096,256]{2,1,0:T(8,128)(2,1)}, bf16[1,4096,256]{2,1,0:T(8,128)(2,1)S(1)}, u32[]{:S(2)}, u32[]{:S(2)}) collective-permute-start(bf16[1,4096,256]{2,1,0:T(8,128)(2,1)} %refs_2_.1), channel_id=1, source_target_pairs={{0,1},{1,0},{2,3},{3,2},{4,5},{5,4},{6,7},{7,6},{8,9},{9,8},{10,11... | collective-permute-start | bytes 6291464 | tf_op jit(solution)/shard_map/ppermute | solution.py:20
  13.0 5.1 %collective-permute-start.4 = (bf16[16,4224]{1,0:T(8,128)(2,1)S(1)}, bf16[16,4224]{1,0:T(8,128)(2,1)S(1)}, u32[]{:S(2)}, u32[]{:S(2)}) collective-permute-start(bf16[16,4224]{1,0:T(8,128)(2,1)S(1)} %pad_maximum_fusion.1.refs_0_), channel_id=1, source_target_pairs={{0,2},{1,3},{2,0},{3,1},{4,6},{5,7},{6,4},{7,5},{8,10},{9,11},{10,... | collective-permute-start | bytes 405512 | tf_op jit(solution)/shard_map/ppermute | solution.py:20
  13.6 5.0 %collective-permute-start.6 = (bf16[1,4096,256]{2,1,0:T(8,128)(2,1)S(1)}, bf16[1,4096,256]{2,1,0:T(8,128)(2,1)S(1)}, u32[]{:S(2)}, u32[]{:S(2)}) collective-permute-start(bf16[1,4096,256]{2,1,0:T(8,128)(2,1)S(1)} %get-tuple-element.42.refs_3_), channel_id=1, source_target_pairs={{0,1},{1,0},{2,3},{3,2},{4,5},{5,4},{6,7},{7,6},{8,9},{9,8},{10,11... | collective-permute-start | bytes 6291464 | tf_op jit(solution)/shard_map/ppermute | solution.py:20
  18.1 6.1 %copy-start.1 = (bf16[1,1024,1024]{2,1,0:T(8,128)(2,1)S(1)}, bf16[1,1024,1024]{2,1,0:T(8,128)(2,1)}, u32[]{:S(2)}) copy-start(bf16[1,1024,1024]{2,1,0:T(8,128)(2,1)} %param.15) | copy-start | bytes 6291460
  18.1 6.1 %collective-permute-start.9 = (bf16[1024,1024]{1,0:T(8,128)(2,1)}, bf16[1024,1024]{1,0:T(8,128)(2,1)S(1)}, u32[]{:S(2)}, u32[]{:S(2)}) collective-permute-start(bf16[1024,1024]{1,0:T(8,128)(2,1)} %bitcast.6), channel_id=1, source_target_pairs={{0,1},{1,0},{2,3},{3,2},{4,5},{5,4},{6,7},{7,6},{8,9},{9,8},{10,11... | collective-permute-start | bytes 6291464 | tf_op jit(solution)/shard_map/ppermute | solution.py:20
  18.1 4.3 %collective-permute-start.8 = (bf16[64,3072]{1,0:T(8,128)(2,1)S(1)}, bf16[64,3072]{1,0:T(8,128)(2,1)S(1)}, u32[]{:S(2)}, u32[]{:S(2)}) collective-permute-start(bf16[64,3072]{1,0:T(8,128)(2,1)S(1)} %pad_maximum_fusion.refs_2_), channel_id=1, source_target_pairs={{0,1},{1,0},{2,3},{3,2},{4,5},{5,4},{6,7},{7,6},{8,9},{9,8},{10,11... | collective-permute-start | bytes 1179656 | tf_op jit(solution)/shard_map/ppermute | solution.py:20
  20.1 4.0 %collective-permute-start.7 = (bf16[32,512]{1,0:T(8,128)(2,1)S(1)}, bf16[32,512]{1,0:T(8,128)(2,1)S(1)}, u32[]{:S(2)}, u32[]{:S(2)}) collective-permute-start(bf16[32,512]{1,0:T(8,128)(2,1)S(1)} %get-tuple-element.43.refs_0_), channel_id=1, source_target_pairs={{0,2},{1,3},{2,0},{3,1},{4,6},{5,7},{6,4},{7,5},{8,10},{9,11},{10,... | collective-permute-start | bytes 98312 | tf_op jit(solution)/shard_map/ppermute | solution.py:20

commit v7 on v5

--- a/solution.py
+++ b/solution.py
@@ -48,8 +48,8 @@
 def pack_kernel(
     quads, ids_hbm, req_hbm, x_hbm, first_hbm, second_hbm, *refs
 ):
-    factor_refs, out_refs, scratches = refs[:quads], refs[quads:-5], refs[-5:]
-    ids_ref, req_ref, x_ref, scratch, sems = scratches
+    factor_refs, out_refs, scratches = refs[:quads], refs[quads:-6], refs[-6:]
+    ids_ref, req_ref, x_ref, scratch, folded, sems = scratches
     half = second_hbm.shape[1] // quads
     pairs = [(ids_hbm, ids_ref), (req_hbm, req_ref), (x_hbm, x_ref)]
     for q, factor_ref in enumerate(factor_refs):
@@ -71,6 +71,15 @@
     scratch[:, :width] = jnp.dot(
         table.astype(jnp.bfloat16), x_ref[...], preferred_element_type=jnp.float32
     )
+    start = half + first_hbm.shape[1]
+    lanes = factor_refs[0].shape[1] - start
+    full = scratch.shape[1]
+    folded[...] = jnp.zeros_like(folded)
+    for i in range(-(-full // lanes)):
+        size = min(lanes, full - i * lanes)
+        folded[pl.ds(i * CAP, CAP), :size] = scratch[:CAP, i * lanes : i * lanes + size]
+    for factor_ref in factor_refs:
+        factor_ref[:, start:] = folded[...].astype(factor_ref.dtype)
     for s, out_ref in enumerate(out_refs[::-1]):
         out_ref[...] = scratch[pl.ds(s * CAP, CAP), :].astype(out_ref.dtype)
     for copy in copies[3:]:
@@ -96,11 +105,30 @@
         copy.wait()
 
 
-def hidden_kernel(pieces, *refs):
-    slot_refs, refs = refs[:pieces], refs[pieces:]
-    gate_ref, up_ref, gate2_ref, up2_ref, hidden_ref, owner_ref = refs
+def hidden_kernel(order, start, *refs):
+    quads = len(order)
+    own_ref, folded_refs, refs = refs[0], refs[1:quads], refs[quads:]
+    slot_refs, refs = refs[:2], refs[2:]
+    gate_ref, up_ref, gate2_ref, up2_ref, hidden_ref, owner_ref, slots, folded = refs
     width, part = gate_ref.shape[1:]
-    slots = jnp.concatenate([ref[...].astype(jnp.float32) for ref in slot_refs], axis=0)
+    full = slots.shape[1]
+    block = slots.shape[0] // quads
+    rest = block - CAP
+    pieces = [ref[...].astype(jnp.float32) for ref in slot_refs]
+    held = pieces[0].shape[0] // rest
+    for i, o in enumerate(order):
+        at = (i % held) * rest
+        slots[pl.ds(i * block + CAP, rest), :] = pieces[i // held][at : at + rest, :]
+        if o == 0:
+            slots[pl.ds(i * block, CAP), :] = own_ref[...].astype(jnp.float32)
+            continue
+        folded[...] = folded_refs[o - 1][:, start:].astype(jnp.float32)
+        lanes = folded.shape[1]
+        for k in range(-(-full // lanes)):
+            size = min(lanes, full - k * lanes)
+            slots[pl.ds(i * block, CAP), k * lanes : k * lanes + size] = folded[
+                pl.ds(k * CAP, CAP), :size
+            ]
     rows = slots[:, :width].astype(jnp.bfloat16)
     owner_ref[...] = slots[:, width:].astype(owner_ref.dtype)
     for b, (g_ref, u_ref) in enumerate(((gate_ref, up_ref), (gate2_ref, up2_ref))):
@@ -130,7 +158,9 @@
     per_dev = factor_refs[0].shape[0] // quads
     rank = per_dev // n_req
     lane = lax.broadcasted_iota(jnp.int32, (1, per_dev * quads * PAIR), 1)
-    first = jnp.concatenate([ref[:, PAIR * cols :] for ref in factor_refs], axis=0)
+    first = jnp.concatenate(
+        [ref[:, PAIR * cols : PAIR * cols + depth] for ref in factor_refs], axis=0
+    )
     low = lax.dot_general(
         hidden, first, (((1,), (1,)), ((), ())), preferred_element_type=jnp.float32
     )
@@ -195,11 +225,12 @@
     dma = pltpu.SemaphoreType.DMA
     own = n_req * rank
 
+    fold = -(-(width // LANES + 1) // (own // CAP)) * LANES
     ids = token_expert_index.T
     weights = choice_weight.T
     outs = pl.pallas_call(
         functools.partial(pack_kernel, quads),
-        out_shape=[jax.ShapeDtypeStruct((own, width // quads + depth), bf16)] * quads
+        out_shape=[jax.ShapeDtypeStruct((own, width // quads + depth + fold), bf16)] * quads
         + [jax.ShapeDtypeStruct((CAP, width + LANES), bf16)] * experts,
         in_specs=[HBM] * 5,
         out_specs=[VMEM] * (quads + experts),
@@ -208,6 +239,7 @@
             pltpu.VMEM((1, tokens), jnp.int32),
             pltpu.VMEM(token_input.shape, bf16),
             pltpu.VMEM((experts * CAP, width + LANES), f32),
+            pltpu.VMEM((own, fold), f32),
             dma((3 + 2 * quads,)),
         ],
         compiler_params=PARAMS,
@@ -247,7 +279,7 @@
         ([blocks[s] for s in far_first], up, factors[1:])
     )
     blocks = [blocks[0]] + [tied[far_first.index(s)] for s in range(1, experts)]
-    rows = jnp.concatenate(blocks, axis=0)
+    rows = jnp.concatenate(blocks[1:], axis=0)
     rows, up_source = lax.optimization_barrier((rows, up))
     up2 = xor_permute(up_source, REQUEST, 1)
     order, bit, slots = [0], quads // 2, []
@@ -258,6 +290,7 @@
         slots = [rows, far]
         rows = jnp.concatenate(slots, axis=0) if bit else rows
 
+    folded = factors[1:]
     factors = jnp.concatenate(factors, axis=0)
     down = down_weight[0]
     slots, down, factors = lax.optimization_barrier((slots, down, factors))
@@ -266,15 +299,16 @@
 
     total = experts * CAP * quads
     hidden, owner = pl.pallas_call(
-        functools.partial(hidden_kernel, len(slots)),
+        functools.partial(hidden_kernel, order, PAIR * cols + depth),
         out_shape=[
             jax.ShapeDtypeStruct((total, PAIR * part), bf16),
             jax.ShapeDtypeStruct((total, LANES), bf16),
         ],
-        in_specs=[VMEM] * (len(slots) + 4),
+        in_specs=[VMEM] * (quads + 6),
         out_specs=[VMEM] * 2,
-        compiler_params=PARAMS,
-    )(*slots, gate_weight, up, gate2, up2)
+        scratch_shapes=[pltpu.VMEM((total, width + LANES), f32), pltpu.VMEM((own, fold), f32)],
+        compiler_params=PARAMS,
+    )(blocks[0], *folded, *slots, gate_weight, up, gate2, up2)
 
     shared = [hidden] + [xor_permute(hidden, REQUEST, q * PAIR) for q in range(1, quads)]
     out = pl.pallas_call(

time: 37 us -> 37.1 us (level)
  no operation moved by 1% of the time
where the time goes in v7:
time: 37.1 us; the launch traced here: 36.9 us
  blocking collectives  10.7 us (29%)
  waiting for transfers between devices  10.2 us (27%)
  starting transfers between devices  9 us (24%)
  Pallas kernels  6.92 us (19%)
    all_to_all x1, blocking collectives, body(): back = lax.all_to_all(out, ('expert', 'quad'), 0, 0, tiled=True)  10.7 us
    ppermute x10, waiting for transfers between devices, xor_permute(): lax.ppermute(value, axis, [(i, i ^ offset) for i in range(lax.axis_size(a...  10.2 us
    ppermute x10, starting transfers between devices, xor_permute(): lax.ppermute(value, axis, [(i, i ^ offset) for i in range(lax.axis_size(a...  9 us
    pallas_call x1, Pallas kernels, body(): pl.pallas_call(stage_kernel, out_shape=[jax.ShapeDtypeStruct((3 * experts...  1.65 us
    pallas_call x1, Pallas kernels, body(): pl.pallas_call(functools.partial(hidden_kernel, order, PAIR * cols + dept...  1.56 us
    pallas_call x1, Pallas kernels, body(): pl.pallas_call(functools.partial(pack_kernel, quads), out_shape=[jax.Shap...  1.51 us
    pallas_call x1, Pallas kernels, body(): pl.pallas_call(functools.partial(down_kernel, order, n_req, cols), out_sh...  1.13 us
    pallas_call x1, Pallas kernels, body(): pl.pallas_call(combine_kernel, out_shape=jax.ShapeDtypeStruct((tokens, wi...  1.06 us
  transfers between devices with their start and end apart: 10, of which 4 were waited for; matrix products, arithmetic and copies ran while one was open for 0% of the time, Pallas kernels for 9%

profile of v7, /device:TPU:0, one launch (start us, length us, event | category | flops | bytes accessed | tf_op | source)
XLA Modules:
  0.0 36.9 jit_solution(17223111037495290244)
XLA Ops:
  0.0 0.0 copy-start.1
  0.0 0.0 copy-start
  0.0 1.5 %shard_map.91 = (bf16[32,3712]{1,0:T(8,128)(2,1)S(1)}, bf16[32,3712]{1,0:T(8,128)(2,1)S(1)}, bf16[4,4224]{1,0:T(4,128)(2,1)S(1)}, bf16[4,4224]{1,0:T(4,128)(2,1)...) custom-call(s32[8,64]{1,0:T(8,128)} %bitcast.10, s32[1,64]{1,0:T(1,128)} %bitcast.13, ...), custom_call_target="tpu_custom_call" | custom-call | tf_op jit(solution)/shard_map/pallas_call | solution.py:231
  1.5 3.0 %collective-permute-start.3 = (bf16[32,3712]{1,0:T(8,128)(2,1)S(1)}, bf16[32,3712]{1,0:T(8,128)(2,1)S(1)}, u32[]{:S(2)}, u32[]{:S(2)}) collective-permute-start(bf16[32,3712]{1,0:T(8,128)(2,1)S(1)} %get-tuple-element.32), channel_id=1, source_target_pairs={{0,2},{1,3},{2,0},{3,1},{4,6},{5,7},{6,4},{7,5},{8,10},{9,11},{10,... | collective-permute-start | bytes 712712 | tf_op jit(solution)/shard_map/ppermute | solution.py:20
  4.5 2.6 %collective-permute-start = (bf16[4,4224]{1,0:T(4,128)(2,1)S(1)}, bf16[4,4224]{1,0:T(4,128)(2,1)S(1)}, u32[]{:S(2)}, u32[]{:S(2)}) collective-permute-start(bf16[4,4224]{1,0:T(4,128)(2,1)S(1)} %get-tuple-element.28), channel_id=1, source_target_pairs={{0,8},{4,12},{8,0},{12,4},{1,9},{5,13},{9,1},{13,5},{2,10},{6,14},... | collective-permute-start | bytes 101384 | tf_op jit(solution)/shard_map/ppermute | solution.py:20
  7.1 1.3 %collective-permute-start.1 = (bf16[4,4224]{1,0:T(4,128)(2,1)S(1)}, bf16[4,4224]{1,0:T(4,128)(2,1)S(1)}, u32[]{:S(2)}, u32[]{:S(2)}) collective-permute-start(bf16[4,4224]{1,0:T(4,128)(2,1)S(1)} %get-tuple-element.29), channel_id=1, source_target_pairs={{0,12},{4,8},{8,4},{12,0},{1,13},{5,9},{9,5},{13,1},{2,14},{6,10},... | collective-permute-start | bytes 101384 | tf_op jit(solution)/shard_map/ppermute | solution.py:20
  8.5 0.2 collective-permute-start.2
  8.7 0.0 collective-permute-start.5
  8.7 1.6 %shard_map.92 = (bf16[48,64]{1,0:T(8,128)(2,1)S(1)}, bf16[1,4096,256]{2,1,0:T(8,128)(2,1)S(1)}) custom-call(s32[8,64]{1,0:T(8,128)} %bitcast.11, f32[8,64]{1,0:T(8,128)} %bitcast.12, bf16[1,4096,256]{2,1,0:T(8,128)(2,1)} %up_hbm.1, bf16[4,4224]{1,0:T(4,128)(2,1)S(1)} %get-tuple-element.26.after_ref.refs_0_), custom_call_target="tpu_custom_call" | custom-call | tf_op jit(solution)/shard_map/pallas_call | solution.py:260
  10.4 0.0 collective-permute-done
  10.4 2.5 %collective-permute-done.1 = bf16[4,4224]{1,0:T(4,128)(2,1)S(1)} collective-permute-done((bf16[4,4224]{1,0:T(4,128)(2,1)S(1)}, bf16[4,4224]{1,0:T(4,128)(2,1)S(1)}, u32[]{:S(2)}, u32[]{:S(2)}) %collective-permute-start.1) | collective-permute-done | bytes 33824 | tf_op jit(solution)/shard_map/ppermute | solution.py:20
  12.8 0.0 collective-permute-done.2
  12.8 0.0 collective-permute-done.3.refs_1_
  12.9 0.1 pad_maximum_fusion.1.refs_2_
  12.9 0.6 %collective-permute-start.4 = (bf16[12,4224]{1,0:T(8,128)(2,1)S(1)}, bf16[12,4224]{1,0:T(8,128)(2,1)S(1)}, u32[]{:S(2)}, u32[]{:S(2)}) collective-permute-start(bf16[12,4224]{1,0:T(8,128)(2,1)S(1)} %pad_maximum_fusion.1.refs_2_), channel_id=1, source_target_pairs={{0,2},{1,3},{2,0},{3,1},{4,6},{5,7},{6,4},{7,5},{8,10},{9,11},{10,... | collective-permute-start | bytes 304136 | tf_op jit(solution)/shard_map/ppermute | solution.py:20
  13.5 0.0 collective-permute-start.6
  13.6 4.4 %collective-permute-done.4.refs_3_ = bf16[12,4224]{1,0:T(8,128)(2,1)S(1)} collective-permute-done((bf16[12,4224]{1,0:T(8,128)(2,1)S(1)}, bf16[12,4224]{1,0:T(8,128)(2,1)S(1)}, u32[]{:S(2)}, u32[]{:S(2)}) %collective-permute-start.4) | collective-permute-done | bytes 101408 | tf_op jit(solution)/shard_map/ppermute | solution.py:20
  18.0 0.0 copy-done.1
  18.0 0.0 collective-permute-start.9
  18.0 0.5 %collective-permute-start.8 = (bf16[64,3712]{1,0:T(8,128)(2,1)S(1)}, bf16[64,3712]{1,0:T(8,128)(2,1)S(1)}, u32[]{:S(2)}, u32[]{:S(2)}) collective-permute-start(bf16[64,3712]{1,0:T(8,128)(2,1)S(1)} %pad_maximum_fusion.refs_2_), channel_id=1, source_target_pairs={{0,1},{1,0},{2,3},{3,2},{4,5},{5,4},{6,7},{7,6},{8,9},{9,8},{10,11... | collective-permute-start | bytes 1425416 | tf_op jit(solution)/shard_map/ppermute | solution.py:20
  18.5 0.0 collective-permute-done.5.refs_6_
  18.5 0.0 collective-permute-done.6.refs_7_
  18.5 0.0 copy-done
  18.5 1.6 %shard_map.93 = (bf16[32,512]{1,0:T(8,128)(2,1)S(1)}, bf16[32,128]{1,0:T(8,128)(2,1)S(1)}) custom-call(bf16[4,4224]{1,0:T(4,128)(2,1)S(1)} %get-tuple-element.26.after_ref.refs_0_, bf16[32,3712]{1,0:T(8,128)(2,1)S(1)} %collective-permute-done.3.refs_1_, bf16[12,4224]{1,0:T(8,128)(2,1)S(1)} %pad_maximum_fusion.1.refs_2_, ...), custom_call_target="tpu_custom_call" | custom-call | tf_op jit(solution)/shard_map/pallas_call | solution.py:301
  20.1 0.7 %collective-permute-start.7 = (bf16[32,512]{1,0:T(8,128)(2,1)S(1)}, bf16[32,512]{1,0:T(8,128)(2,1)S(1)}, u32[]{:S(2)}, u32[]{:S(2)}) collective-permute-start(bf16[32,512]{1,0:T(8,128)(2,1)S(1)} %get-tuple-element.43.refs_0_), channel_id=1, source_target_pairs={{0,2},{1,3},{2,0},{3,1},{4,6},{5,7},{6,4},{7,5},{8,10},{9,11},{10,... | collective-permute-start | bytes 98312 | tf_op jit(solution)/shard_map/ppermute | solution.py:20
  20.8 2.0 %collective-permute-done.8.refs_3_ = bf16[64,3712]{1,0:T(8,128)(2,1)S(1)} collective-permute-done((bf16[64,3712]{1,0:T(8,128)(2,1)S(1)}, bf16[64,3712]{1,0:T(8,128)(2,1)S(1)}, u32[]{:S(2)}, u32[]{:S(2)}) %collective-permute-start.8) | collective-permute-done | bytes 475168 | tf_op jit(solution)/shard_map/ppermute | solution.py:20
  22.8 1.2 %collective-permute-done.7.refs_1_ = bf16[32,512]{1,0:T(8,128)(2,1)S(1)} collective-permute-done((bf16[32,512]{1,0:T(8,128)(2,1)S(1)}, bf16[32,512]{1,0:T(8,128)(2,1)S(1)}, u32[]{:S(2)}, u32[]{:S(2)}) %collective-permute-start.7) | collective-permute-done | bytes 32800 | tf_op jit(solution)/shard_map/ppermute | solution.py:20
  24.1 0.0 collective-permute-done.9.refs_6_
  24.1 1.1 %shard_map.94 = bf16[8,4,2048]{2,1,0:T(4,128)(2,1)S(1)} custom-call(bf16[32,512]{1,0:T(8,128)(2,1)S(1)} %get-tuple-element.43.refs_0_, bf16[32,512]{1,0:T(8,128)(2,1)S(1)} %collective-permute-done.7.refs_1_, bf16[64,3712]{1,0:T(8,128)(2,1)S(1)} %pad_maximum_fusion.refs_2_, bf16[64,3712]{1,0:T(8,128)(2,1)S(1)} %collective-permute-done.8.refs_3_, ...), custom_call_target="tpu_custom_call" | custom-call | tf_op jit(solution)/shard_map/pallas_call | solution.py:314
  25.2 10.7 %all_to_all.5.back_ref = bf16[8,4,2048]{2,1,0:T(4,128)(2,1)S(1)} all-to-all(bf16[8,4,2048]{2,1,0:T(4,128)(2,1)S(1)} %shard_map.94), channel_id=1, replica_groups=mesh['groups'=2,'expert'=4,'quad'=2,'pair'=2] {'expert','quad'}, dimensions={0} | all-to-all | bytes 262144 | tf_op jit(solution)/shard_map/all_to_all | solution.py:326
  35.9 1.1 %shard_map.95 = bf16[64,4096]{1,0:T(8,128)(2,1)} custom-call(bf16[48,64]{1,0:T(8,128)(2,1)S(1)} %get-tuple-element.27.table_ref, bf16[8,4,2048]{2,1,0:T(4,128)(2,1)S(1)} %all_to_all.5.back_ref), custom_call_target="tpu_custom_call" | custom-call | tf_op jit(solution)/shard_map/pallas_call | solution.py:327
  (1 shorter events, 0.0 us)
Async XLA Ops:
  0.0 18.0 %copy-start.1 = (bf16[1,1024,1024]{2,1,0:T(8,128)(2,1)S(1)}, bf16[1,1024,1024]{2,1,0:T(8,128)(2,1)}, u32[]{:S(2)}) copy-start(bf16[1,1024,1024]{2,1,0:T(8,128)(2,1)} %param.15) | copy-start | bytes 6291460
  0.0 18.5 %copy-start = (bf16[1,4096,256]{2,1,0:T(8,128)(2,1)S(1)}, bf16[1,4096,256]{2,1,0:T(8,128)(2,1)}, u32[]{:S(2)}) copy-start(bf16[1,4096,256]{2,1,0:T(8,128)(2,1)} %refs_4_.1) | copy-start | bytes 6291460
  1.5 11.3 %collective-permute-start.3 = (bf16[32,3712]{1,0:T(8,128)(2,1)S(1)}, bf16[32,3712]{1,0:T(8,128)(2,1)S(1)}, u32[]{:S(2)}, u32[]{:S(2)}) collective-permute-start(bf16[32,3712]{1,0:T(8,128)(2,1)S(1)} %get-tuple-element.32), channel_id=1, source_target_pairs={{0,2},{1,3},{2,0},{3,1},{4,6},{5,7},{6,4},{7,5},{8,10},{9,11},{10,... | collective-permute-start | bytes 712712 | tf_op jit(solution)/shard_map/ppermute | solution.py:20
  4.5 5.8 %collective-permute-start = (bf16[4,4224]{1,0:T(4,128)(2,1)S(1)}, bf16[4,4224]{1,0:T(4,128)(2,1)S(1)}, u32[]{:S(2)}, u32[]{:S(2)}) collective-permute-start(bf16[4,4224]{1,0:T(4,128)(2,1)S(1)} %get-tuple-element.28), channel_id=1, source_target_pairs={{0,8},{4,12},{8,0},{12,4},{1,9},{5,13},{9,1},{13,5},{2,10},{6,14},... | collective-permute-start | bytes 101384 | tf_op jit(solution)/shard_map/ppermute | solution.py:20
  7.1 5.7 %collective-permute-start.1 = (bf16[4,4224]{1,0:T(4,128)(2,1)S(1)}, bf16[4,4224]{1,0:T(4,128)(2,1)S(1)}, u32[]{:S(2)}, u32[]{:S(2)}) collective-permute-start(bf16[4,4224]{1,0:T(4,128)(2,1)S(1)} %get-tuple-element.29), channel_id=1, source_target_pairs={{0,12},{4,8},{8,4},{12,0},{1,13},{5,9},{9,5},{13,1},{2,14},{6,10},... | collective-permute-start | bytes 101384 | tf_op jit(solution)/shard_map/ppermute | solution.py:20
  8.5 4.4 %collective-permute-start.2 = (bf16[4,4224]{1,0:T(4,128)(2,1)S(1)}, bf16[4,4224]{1,0:T(4,128)(2,1)S(1)}, u32[]{:S(2)}, u32[]{:S(2)}) collective-permute-start(bf16[4,4224]{1,0:T(4,128)(2,1)S(1)} %get-tuple-element.30), channel_id=1, source_target_pairs={{0,4},{4,0},{8,12},{12,8},{1,5},{5,1},{9,13},{13,9},{2,6},{6,2},{1... | collective-permute-start | bytes 101384 | tf_op jit(solution)/shard_map/ppermute | solution.py:20
  8.7 9.8 %collective-permute-start.5 = (bf16[1,4096,256]{2,1,0:T(8,128)(2,1)}, bf16[1,4096,256]{2,1,0:T(8,128)(2,1)S(1)}, u32[]{:S(2)}, u32[]{:S(2)}) collective-permute-start(bf16[1,4096,256]{2,1,0:T(8,128)(2,1)} %refs_4_.1), channel_id=1, source_target_pairs={{0,1},{1,0},{2,3},{3,2},{4,5},{5,4},{6,7},{7,6},{8,9},{9,8},{10,11... | collective-permute-start | bytes 6291464 | tf_op jit(solution)/shard_map/ppermute | solution.py:20
  12.9 5.1 %collective-permute-start.4 = (bf16[12,4224]{1,0:T(8,128)(2,1)S(1)}, bf16[12,4224]{1,0:T(8,128)(2,1)S(1)}, u32[]{:S(2)}, u32[]{:S(2)}) collective-permute-start(bf16[12,4224]{1,0:T(8,128)(2,1)S(1)} %pad_maximum_fusion.1.refs_2_), channel_id=1, source_target_pairs={{0,2},{1,3},{2,0},{3,1},{4,6},{5,7},{6,4},{7,5},{8,10},{9,11},{10,... | collective-permute-start | bytes 304136 | tf_op jit(solution)/shard_map/ppermute | solution.py:20
  13.5 5.0 %collective-permute-start.6 = (bf16[1,4096,256]{2,1,0:T(8,128)(2,1)S(1)}, bf16[1,4096,256]{2,1,0:T(8,128)(2,1)S(1)}, u32[]{:S(2)}, u32[]{:S(2)}) collective-permute-start(bf16[1,4096,256]{2,1,0:T(8,128)(2,1)S(1)} %get-tuple-element.42.refs_5_), channel_id=1, source_target_pairs={{0,1},{1,0},{2,3},{3,2},{4,5},{5,4},{6,7},{7,6},{8,9},{9,8},{10,11... | collective-permute-start | bytes 6291464 | tf_op jit(solution)/shard_map/ppermute | solution.py:20
  18.0 6.1 %collective-permute-start.9 = (bf16[1024,1024]{1,0:T(8,128)(2,1)S(1)}, bf16[1024,1024]{1,0:T(8,128)(2,1)S(1)}, u32[]{:S(2)}, u32[]{:S(2)}) collective-permute-start(bf16[1024,1024]{1,0:T(8,128)(2,1)S(1)} %bitcast.6), channel_id=1, source_target_pairs={{0,1},{1,0},{2,3},{3,2},{4,5},{5,4},{6,7},{7,6},{8,9},{9,8},{10,11... | collective-permute-start | bytes 6291464 | tf_op jit(solution)/shard_map/ppermute | solution.py:20
  18.0 4.8 %collective-permute-start.8 = (bf16[64,3712]{1,0:T(8,128)(2,1)S(1)}, bf16[64,3712]{1,0:T(8,128)(2,1)S(1)}, u32[]{:S(2)}, u32[]{:S(2)}) collective-permute-start(bf16[64,3712]{1,0:T(8,128)(2,1)S(1)} %pad_maximum_fusion.refs_2_), channel_id=1, source_target_pairs={{0,1},{1,0},{2,3},{3,2},{4,5},{5,4},{6,7},{7,6},{8,9},{9,8},{10,11... | collective-permute-start | bytes 1425416 | tf_op jit(solution)/shard_map/ppermute | solution.py:20
  20.1 4.0 %collective-permute-start.7 = (bf16[32,512]{1,0:T(8,128)(2,1)S(1)}, bf16[32,512]{1,0:T(8,128)(2,1)S(1)}, u32[]{:S(2)}, u32[]{:S(2)}) collective-permute-start(bf16[32,512]{1,0:T(8,128)(2,1)S(1)} %get-tuple-element.43.refs_0_), channel_id=1, source_target_pairs={{0,2},{1,3},{2,0},{3,1},{4,6},{5,7},{6,4},{7,5},{8,10},{9,11},{10,... | collective-permute-start | bytes 98312 | tf_op jit(solution)/shard_map/ppermute | solution.py:20
